TPU v7x, 32 devices: a whole 2x2x4 slice. The times are simulated.
32 devices in a mesh: grp: 4 (over y, x), dev: 8 (over z, core).
Axes of the slice: x: 2, y: 2, z: 4, core: 2. Of those that a mesh axis runs over, the one named last changes fastest.
Arguments:
- integral_slabs: bfloat16 [8, 512, 512], P('dev'), may hold values from -6 to 6
- slab_owner: int32 [8], replicated, may hold values from 0 to 7, each once
- pair_orbs: int32 [256, 2], P(('grp', 'dev')), may hold values from 0 to 7, all different within a row; in each aligned block of 8 rows (0 to 7, 8 to 15, ...) at most 2 rows name the same one
- domain_bases: bfloat16 [256, 512, 128], P(('grp', 'dev')), may hold values from -0.25 to 0.25
- amplitudes: bfloat16 [256, 128, 128], P(('grp', 'dev')), may hold values from -6 to 6
- coupled: int32 [256, 32], P(('grp', 'dev')), may hold values from 0 to 31
- coupled_len: int32 [256], P(('grp', 'dev')), may hold values from 1 to 32, as said below
Outputs:
- residual: float32 [256, 128, 128], P(('grp', 'dev'))
Inputs may be any that keep to these rules, and one draw needn't show every extreme that they name: `slab_owner`: a permutation of the positions. `pair_orbs`: the two orbitals of a pair differ; among the pairs of one device no orbital is named more than 2 times. `coupled_len`: pair 0 uses all 32 slots.
All inputs are finite; a program needn't handle non-finite values.
Results may differ from a plain program's by a relative error of at most 0.005.
Values may be sent and summed in bfloat16 or wider, within the bound.
No kernel may reach another device: no remote copies, remote signals or barrier semaphores. Data moves between devices by JAX's collectives and lax.ppermute only.
A program may use at most 128 MiB of HBM per device.

v0:
```python
import functools
import math

import jax
import jax.numpy as jnp
from jax import lax
from jax.experimental import pallas as pl
from jax.experimental.pallas import tpu as pltpu
from jax.sharding import PartitionSpec as P

MARGIN = 0
PACK_LIMIT = 56 * 1024 * 1024
DECLARED = 20_000_000_000
OWN_COST, FIRST_COST, SECOND_COST, LAST_COST = 0, 0, 0, DECLARED
SMEM_SPEC = pl.BlockSpec(memory_space=pltpu.SMEM)
VMEM_SPEC = pl.BlockSpec(memory_space=pltpu.VMEM)
HBM_SPEC = pl.BlockSpec(memory_space=pltpu.HBM)


def call_kernel(body, out_shape, scratch, name, smem_args, vmem_args, flops, hbm_args=(), aliases={}):
    outs = out_shape if isinstance(out_shape, tuple) else (out_shape,)
    held = [a for a in (*vmem_args, *scratch, *outs) if a.dtype in (jnp.float32, jnp.bfloat16)]
    return pl.pallas_call(
        body,
        out_shape=out_shape,
        in_specs=[SMEM_SPEC] * len(smem_args) + [VMEM_SPEC] * len(vmem_args) + [HBM_SPEC] * len(hbm_args),
        out_specs=(VMEM_SPEC,) * len(outs) if isinstance(out_shape, tuple) else VMEM_SPEC,
        scratch_shapes=scratch,
        input_output_aliases=aliases,
        compiler_params=pltpu.CompilerParams(
            vmem_limit_bytes=sum(math.prod(a.shape) * a.dtype.itemsize for a in held) + MARGIN
        ),
        cost_estimate=pl.CostEstimate(flops=flops, bytes_accessed=0, transcendentals=0),
        name=name,
    )(*smem_args, *vmem_args, *hbm_args)


class Side:
    def __init__(self, left, packs, orbs, pno):
        self.left, self.packs, self.orbs, self.pno = left, packs, orbs, pno

    def basis(self, k):
        return self.packs[k][: self.orbs, :]

    def amps(self, k):
        return self.packs[k][self.orbs : self.orbs + self.pno, :]

    def counts(self, lanes):
        rows = [pack[self.orbs + self.pno :, :].astype(jnp.float32) for pack in self.packs]
        return lambda p, c: rows[p][0:1, lanes[c] : lanes[c] + 1]


def project(side, other, count, inter_ref, proj_ref, copies=()):
    pno = side.pno
    empty = jnp.zeros((pno, pno), jnp.bfloat16)
    for j in range(0, len(other.packs), 2):
        for copy in copies[j : j + 2]:
            copy.wait()
        pair = jnp.concatenate([other.basis(j), other.basis(j + 1)], axis=1)
        inter = jnp.dot(side.left[...], pair, preferred_element_type=jnp.float32).astype(jnp.bfloat16)
        inter_ref[:, j * pno : (j + 2) * pno] = inter
        diagonal = jnp.concatenate(
            [
                jnp.concatenate([other.amps(j), empty], axis=1),
                jnp.concatenate([empty, other.amps(j + 1)], axis=1),
            ],
            axis=0,
        )
        proj = jnp.dot(inter, diagonal, preferred_element_type=jnp.float32)
        for p in range(side.left.shape[0] // pno):
            for c in range(2):
                block = proj[p * pno : (p + 1) * pno, c * pno : (c + 1) * pno]
                proj_ref[p * pno : (p + 1) * pno, (j + c) * pno : (j + c + 1) * pno] = (
                    block * count(p, j + c)
                ).astype(jnp.bfloat16)


def coupled_kernel(lanes, begun, weight_ref, left_ref, *refs):
    *acc_ref, one_ref, two_ref, out_ref, inter_ref, proj_ref = refs
    pairs, pno, _ = out_ref.shape
    half, orbs = pairs // 2, left_ref.shape[1]
    own = Side(left_ref, (), orbs, pno)
    other = Side(None, [ref.at[k] for ref in (one_ref, two_ref) for k in range(half)], orbs, pno)
    project(own, other, lambda p, c: weight_ref[p, lanes[c]], inter_ref, proj_ref)
    for p in range(pairs):
        total = one_sum(proj_ref, inter_ref, p, pno)
        out_ref[p] = acc_ref[0][p] + total if begun else total


def one_sum(proj_ref, inter_ref, p, pno):
    at = slice(p * pno, (p + 1) * pno)
    return lax.dot_general(
        proj_ref[at, :], inter_ref[at, :], (((1,), (1,)), ((), ())), preferred_element_type=jnp.float32
    )


def both_sums(one_ref, two_ref, turned_ref, one_lanes, two_lanes, products, orbs):
    half, _, pno = one_ref.shape
    sides = []
    for first, ref in ((0, one_ref), (half, two_ref)):
        for k in range(half):
            turned_ref[(first + k) * pno : (first + k + 1) * pno, :] = ref[k, :orbs, :].T
        left = turned_ref.at[first * pno : (first + half) * pno, :]
        sides.append(Side(left, [ref.at[k] for k in range(half)], orbs, pno))
    project(sides[0], sides[1], sides[0].counts(two_lanes), products[0], products[1])
    project(sides[1], sides[0], sides[1].counts(one_lanes), products[2], products[3])

    def total(proj, inter):
        def of(k):
            at = slice(k * pno, (k + 1) * pno)
            return jnp.dot(proj[at, :], inter[:, at], preferred_element_type=jnp.float32)

        return of

    return total(products[1], products[2]), total(products[3], products[0])


def first_across_kernel(orbs, x_low, y_high, out_one, out_two, turned_ref, *products):
    half = out_one.shape[0]
    block = 3 * 2 * half
    low, high = range(block, block + half), range(block + half, block + 2 * half)
    one, two = both_sums(x_low, y_high, turned_ref, low, high, products, orbs)
    for k in range(half):
        out_one[k] = one(k)
        out_two[k] = two(k)


def second_across_kernel(orbs, upper_ref, low1, low2, *refs):
    x_low, x_high, y_low, y_high, back_x, back_y, turned_ref, *products = refs
    half, pno = low1.shape[0], low1.shape[1]
    block = 3 * 2 * half
    none = jnp.zeros((pno, pno), jnp.bfloat16)

    @pl.when(upper_ref[0] == 0)
    def _():
        low = range(block, block + half)
        one, two = both_sums(x_low, y_low, turned_ref, low, low, products, orbs)
        for k in range(half):
            back_x[k] = (low1[k] + one(k)).astype(jnp.bfloat16)
            back_x[half + k] = none
            back_y[k] = two(k).astype(jnp.bfloat16)
            back_y[half + k] = low2[k].astype(jnp.bfloat16)

    @pl.when(upper_ref[0] == 1)
    def _():
        high = range(block + half, block + 2 * half)
        one, two = both_sums(x_high, y_high, turned_ref, high, high, products, orbs)
        for k in range(half):
            back_x[k] = low1[k].astype(jnp.bfloat16)
            back_x[half + k] = one(k).astype(jnp.bfloat16)
            back_y[k] = none
            back_y[half + k] = (low2[k] + two(k)).astype(jnp.bfloat16)


def add_coupled(lanes, weights, own_t, acc, received, flops):
    half, _, pno = received[0].shape
    rows, pairs = own_t.shape[0], 2 * half
    shape = jax.ShapeDtypeStruct((pairs, pno, pno), jnp.float32)
    body = functools.partial(coupled_kernel, lanes, acc is not None)
    vmem_args = (own_t, *received) if acc is None else (own_t, acc, *received)
    return call_kernel(body, shape, [pltpu.VMEM((rows, rows), jnp.bfloat16)] * 2, "coupled", (weights,), vmem_args, flops)


def across(body, name, scalars, vmem_args, half, shapes, orbs, flops):
    wide = half * shapes[0].shape[2]
    scratch = [pltpu.VMEM((2 * wide, orbs), jnp.bfloat16), *[pltpu.VMEM((wide, wide), jnp.bfloat16)] * 4]
    return call_kernel(functools.partial(body, orbs), shapes, scratch, name, scalars, vmem_args, flops)


def half_transforms(uses_ref, slab_refs, own_ref, store, base, pno):
    last = own_ref.shape[0] // pno - 1

    def rows(side):
        return own_ref[pl.ds(pl.multiple_of(jnp.minimum(side // 2, last) * pno, pno), pno), :]

    def both_sides(slab, k):
        one, two = uses_ref[k, 0], uses_ref[k, 1]
        bases = jnp.concatenate([rows(one), rows(two)], axis=0)
        both = lax.dot_general(slab, bases, (((1,), (1,)), ((), ())), preferred_element_type=jnp.float32)
        both = both.astype(jnp.bfloat16)
        store(k, 0, one, both[:, :pno])
        store(k, 1, two, both[:, pno:])

    for slab_ref in slab_refs:
        if slab_ref.shape[0] > 4:

            def step(k, carry, slab_ref=slab_ref, base=base):
                both_sides(slab_ref[k], base + k)
                return carry

            lax.fori_loop(0, slab_ref.shape[0], step, 0)
        else:
            for k in range(slab_ref.shape[0]):
                both_sides(slab_ref[k], base + k)
        base += slab_ref.shape[0]


def halves_kernel(base, uses_ref, *refs):
    *slab_refs, own_ref, half_ref = refs

    def store(k, use, side, half):
        half_ref[side] = half

    half_transforms(uses_ref, slab_refs, own_ref, store, base, half_ref.shape[2])


def more_halves_kernel(base, uses_ref, *refs):
    *slab_refs, own_ref, _, half_ref = refs
    halves_kernel(base, uses_ref, *slab_refs, own_ref, half_ref)


def exchange_kernel(scale, base, uses_ref, turn_ref, *refs):
    *slab_refs, own_ref, early_ref, acc_ref, back1_ref, back2_ref, out_ref, late_ref = refs

    def store(k, use, side, half):
        late_ref[2 * (k - base) + use] = half

    def half(p, side):
        k = turn_ref[p, side]
        late = jnp.where(uses_ref[k, 0] == 2 * p + side, 0, 1) + 2 * jnp.maximum(k - base, 0)
        return jnp.where(k < base, early_ref[2 * p + side], late_ref[late])

    half_transforms(uses_ref, slab_refs, own_ref, store, base, out_ref.shape[1])
    for p in range(out_ref.shape[0]):
        product = lax.dot_general(half(p, 0), half(p, 1), (((0,), (0,)), ((), ())), preferred_element_type=jnp.float32)
        back = back1_ref[p].astype(jnp.float32) + back2_ref[p].astype(jnp.float32)
        out_ref[p] = acc_ref[p] + back + product * scale


def half_products(uses, base, slabs, own_t, pno, done=None):
    sides = own_t.shape[0] // pno * 2
    shape = jax.ShapeDtypeStruct((sides + 1, slabs[0].shape[1], pno), jnp.bfloat16)
    if done is None:
        return call_kernel(functools.partial(halves_kernel, base), shape, [], "halves", (uses,), (*slabs, own_t), 0)
    args = (*slabs, own_t, done)
    return call_kernel(
        functools.partial(more_halves_kernel, base), shape, [], "more_halves", (uses,), args, 0, aliases={len(args): 0}
    )


def add_exchange(uses, turn, base, slabs, own_t, early, sums):
    return call_kernel(
        functools.partial(exchange_kernel, 1.0 / math.sqrt(slabs[0].shape[1]), base),
        jax.ShapeDtypeStruct(sums[0].shape, jnp.float32),
        [pltpu.VMEM((2 * sum(slab.shape[0] for slab in slabs),) + early.shape[1:], jnp.bfloat16)],
        "exchange",
        (uses, turn),
        (*slabs, own_t, early, *sums),
        0,
    )


def slab_uses(slab_owner, pair_orbs, order):
    n_dev = order.shape[0]
    sides = pair_orbs.shape[0] * 2
    table = jnp.arange(n_dev, dtype=jnp.int32)
    position = jnp.sum(jnp.where(pair_orbs.reshape(sides)[:, None] == table, slab_owner, 0), axis=1)
    turn = jnp.sum(jnp.where(position[:, None] == table, order, 0), axis=1).astype(jnp.int32)
    hit = turn[:, None] == table
    side = jnp.arange(sides, dtype=jnp.int32)[:, None]
    last = jnp.max(jnp.where(hit, side, -1), axis=0)
    first = jnp.min(jnp.where(hit, side, sides), axis=0)
    return turn.reshape(-1, 2), jnp.stack([first, jnp.where(last < 0, sides, last)], axis=1)


def pack_kernel(scale, group_ref, coupled_ref, length_ref, base_ref, amp_ref, *refs):
    low_ref, high_ref, weight_ref, held_ref, sems = refs
    pairs, orbs, pno = base_ref.shape
    half = pairs // 2
    copies = []

    def copy(ref, k, row, sem):
        rows = pl.ds(row, ref.shape[1])
        copies.append(pltpu.make_async_copy(ref.at[pl.ds(k * half, half)], held_ref.at[k, :, rows], sems.at[sem]))
        copies[-1].start()

    for k in range(2):
        copy(base_ref, k, 0, 2 * k)
        copy(amp_ref, k, orbs, 2 * k + 1)
    lane = lax.broadcasted_iota(jnp.int32, (1, pno), 1)
    for p in range(pairs):
        counts = jnp.zeros((1, pno), jnp.float32)
        for s in range(coupled_ref.shape[1]):
            named = coupled_ref[p, s]
            at = (lax.div(named, pairs) ^ group_ref[0]) * pairs + lax.rem(named, pairs)
            counts += jnp.where(lane == jnp.where(s < length_ref[p], at, -1), scale, 0.0)
        weight_ref[p : p + 1, :] = counts
        rows = slice(orbs + amp_ref.shape[1], held_ref.shape[2])
        held_ref[p // half, p % half, rows, :] = jnp.broadcast_to(counts, (16, pno)).astype(jnp.bfloat16)
    for started in copies:
        started.wait()
    stores = [
        pltpu.make_async_copy(held_ref.at[k], out_ref, sems.at[4 + k]) for k, out_ref in enumerate((low_ref, high_ref))
    ]
    for store in stores:
        store.start()
    for store in stores:
        store.wait()


def pack(group, coupled, coupled_len, bases, amps, scale):
    pairs, orbs, pno = bases.shape
    packed = jax.ShapeDtypeStruct((pairs // 2, orbs + amps.shape[1] + 16, pno), bases.dtype)
    return pl.pallas_call(
        functools.partial(pack_kernel, scale),
        out_shape=(packed, packed, jax.ShapeDtypeStruct((pairs, pno), jnp.float32)),
        in_specs=[SMEM_SPEC] * 3 + [HBM_SPEC] * 2,
        out_specs=(HBM_SPEC, HBM_SPEC, VMEM_SPEC),
        scratch_shapes=[pltpu.VMEM((2,) + packed.shape, bases.dtype), pltpu.SemaphoreType.DMA((6,))],
        compiler_params=pltpu.CompilerParams(vmem_limit_bytes=PACK_LIMIT),
        name="pack",
    )(group, coupled, coupled_len, bases, amps)


def after(value, *earlier):
    return lax.optimization_barrier((value,) + earlier)[0]


def on_device(integral_slabs, slab_owner, pair_orbs, domain_bases, amplitudes, coupled, coupled_len):
    n_grp, n_dev = lax.axis_size("grp"), lax.axis_size("dev")
    pairs, orbs, pno = domain_bases.shape
    group, me = lax.axis_index("grp"), lax.axis_index("dev")
    chips = n_dev // 2
    chip, core = me // 2, me % 2

    half = pairs // 2

    def along_x(value):
        return lax.ppermute(value, "grp", [(g, g ^ 1) for g in range(n_grp)])

    def along_y(value):
        return lax.ppermute(value, "grp", [(g, g ^ 2) for g in range(n_grp)])

    def next_chip(value):
        return lax.ppermute(value, "dev", [(d, (d + 2) % n_dev) for d in range(n_dev)])

    def other_core(value):
        return lax.ppermute(value, "dev", [(d, d ^ 1) for d in range(n_dev)])

    own_lo, own_hi, weights = pack(
        group.astype(jnp.int32).reshape(1), coupled, coupled_len, domain_bases, amplitudes, orbs / pno
    )
    own_t = jnp.swapaxes(domain_bases, 1, 2).reshape(pairs * pno, orbs)
    upper = jnp.where(group >= 2, 1, 0).astype(jnp.int32).reshape(1)

    x_lo, y_hi = along_x(own_lo), along_y(own_hi)
    x_hi, y_lo = along_x(after(own_hi, own_lo)), along_y(after(own_lo, own_hi))

    slab = integral_slabs[0]
    around = chips <= 4
    position = jnp.arange(n_dev, dtype=jnp.int32)
    order, ahead = position, n_dev // 2
    acc = add_coupled(list(range(pairs)), weights, own_t, None, (own_lo, own_hi), OWN_COST)
    if around:
        order = 2 * ((chip - position // 2) % chips) + jnp.where(position % 2 == core, 0, 1)
        ahead = 6
        round1 = next_chip(slab)
        round2 = next_chip(after(round1, acc))
        swap0, swap1 = other_core(after(slab, x_lo, y_hi)), other_core(after(round1, x_lo, y_hi))
    turns, uses = slab_uses(slab_owner, pair_orbs, order)

    lanes = [*range(pairs, pairs + half), *range(2 * pairs + half, 3 * pairs)]
    acc = add_coupled(lanes, weights, own_t, acc, (x_lo, y_hi), DECLARED)
    part = jax.ShapeDtypeStruct((half, pno, pno), jnp.float32)
    first = across(
        first_across_kernel, "first_across", (), (after(x_lo, acc), after(y_hi, acc)), half, (part, part), orbs, FIRST_COST
    )
    if around:
        slabs = [slab[None], swap0[None], round1[None], swap1[None]]
        halves = half_products(uses, 0, slabs, after(own_t, *first), pno)
        round2 = after(round2, halves)
        round3, swap2 = next_chip(round2), other_core(round2)
        halves = half_products(uses, 4, [round2[None], swap2[None]], own_t, pno, halves)
    else:
        gathered = lax.all_gather(slab, "dev", axis=0, tiled=False)
        halves = half_products(uses, 0, [gathered[:ahead]], own_t, pno)
        rest = [gathered[ahead:]]
    whole = jax.ShapeDtypeStruct((pairs, pno, pno), jnp.bfloat16)
    back_x, back_y = across(
        second_across_kernel,
        "second_across",
        (upper,),
        (after(first[0], halves), first[1], x_lo, x_hi, y_lo, y_hi),
        half,
        (whole, whole),
        orbs,
        SECOND_COST,
    )
    back = (along_x(back_x), along_y(back_y))
    lanes = [*range(pairs + half, 2 * pairs), *range(2 * pairs, 2 * pairs + half)]
    acc = add_coupled(lanes, weights, own_t, after(acc, back_x), (x_hi, y_lo), LAST_COST)
    if around:
        round3 = after(round3, acc, *back)
        rest = [round3[None], other_core(round3)[None]]
    return add_exchange(uses, turns, ahead, rest, own_t, halves, (acc, *back))


def solution(mesh):
    in_specs = (
        P("dev", None, None),
        P(),
        P(("grp", "dev"), None),
        P(("grp", "dev"), None, None),
        P(("grp", "dev"), None, None),
        P(("grp", "dev"), None),
        P(("grp", "dev")),
    )
    out_specs = P(("grp", "dev"), None, None)
    return jax.shard_map(
        on_device, mesh=mesh, in_specs=in_specs, out_specs=out_specs, check_vma=False
    )
```

profile of v0, /device:TPU:0, one launch (start us, length us, event | category | flops | bytes accessed | tf_op | source)
XLA Modules:
  0.0 62.6 jit_solution(10222273469689722816)
XLA Ops:
  0.0 3.8 %pack.1 = (bf16[4,656,128]{2,1,0:T(8,128)(2,1)}, bf16[4,656,128]{2,1,0:T(8,128)(2,1)}, f32[8,128]{1,0:T(8,128)}) custom-call(s32[1]{0:T(128)} %bitcast.3.group_ref, s32[8,32]{1,0:T(8,128)} %coupled_ref.1, s32[8]{0:T(128)} %length_ref.1, bf16[8,512,128]{2,1,0:T(8,128)(2,1)} %base_ref.1, bf16[8,128,128]{2,1,0:T(8,128)(2,1)} %amp_ref.1), custom_call_target="tpu_custom_call" | custom-call | tf_op jit(solution)/shard_map/pack/pallas_call | solution.py:304
  3.9 3.0 %collective-permute-start.2 = (bf16[4,656,128]{2,1,0:T(8,128)(2,1)}, bf16[4,656,128]{2,1,0:T(8,128)(2,1)S(1)}, u32[]{:S(2)}, u32[]{:S(2)}) collective-permute-start(bf16[4,656,128]{2,1,0:T(8,128)(2,1)} %get-tuple-element.38.refs_0_), channel_id=1, source_target_pairs={{0,8},{8,0},{16,24},{24,16},{1,9},{9,1},{17,25},{25,17},{2,10},{10... | collective-permute-start | bytes 2015240 | tf_op jit(solution)/shard_map/ppermute | solution.py:329
  6.9 1.5 %collective-permute-start.3 = (bf16[4,656,128]{2,1,0:T(8,128)(2,1)}, bf16[4,656,128]{2,1,0:T(8,128)(2,1)S(1)}, u32[]{:S(2)}, u32[]{:S(2)}) collective-permute-start(bf16[4,656,128]{2,1,0:T(8,128)(2,1)} %get-tuple-element.37.refs_1_), channel_id=1, source_target_pairs={{0,16},{8,24},{16,0},{24,8},{1,17},{9,25},{17,1},{25,9},{2,18},{10... | collective-permute-start | bytes 2015240 | tf_op jit(solution)/shard_map/ppermute | solution.py:332
  8.4 1.6 %collective-permute-start = (bf16[512,512]{1,0:T(8,128)(2,1)}, bf16[512,512]{1,0:T(8,128)(2,1)}, u32[]{:S(2)}, u32[]{:S(2)}) collective-permute-start(bf16[512,512]{1,0:T(8,128)(2,1)} %bitcast.21), channel_id=1, source_target_pairs={{0,2},{1,3},{2,4},{3,5},{4,6},{5,7},{6,0},{7,1},{8,10},{9,11},{10,... | collective-permute-start | bytes 1572872 | tf_op jit(solution)/shard_map/ppermute | solution.py:335
  10.0 0.5 collective-permute-start.8
  10.5 0.5 collective-permute-start.9
  11.0 1.5 %copy.25 = bf16[8,128,512]{2,1,0:T(8,128)(2,1)S(1)} copy(bf16[8,128,512]{1,2,0:T(8,128)(2,1)} %bitcast.25) | data formatting | bytes 2097152 | tf_op jit(solution)/shard_map/transpose | solution.py:343
  12.8 0.1 select_reduce_fusion.2
  12.9 0.2 select_reduce_fusion.1
  13.1 1.1 %copy-done.5 = bf16[4,656,128]{2,1,0:T(8,128)(2,1)S(1)} copy-done((bf16[4,656,128]{2,1,0:T(8,128)(2,1)S(1)}, bf16[4,656,128]{2,1,0:T(8,128)(2,1)}, u32[]{:S(2)}) %copy-start.5) | copy-done | bytes 671768
  14.2 0.7 %copy-done.13 = f32[8,128]{1,0:T(8,128)S(1)} copy-done((f32[8,128]{1,0:T(8,128)S(1)}, f32[8,128]{1,0:T(8,128)}, u32[]{:S(2)}) %copy-start.13) | copy-done | bytes 4120
  14.9 3.9 %coupled.3.refs_0_ = f32[8,128,128]{2,1,0:T(8,128)S(1)} custom-call(f32[8,128]{1,0:T(8,128)S(1)} %copy-done.13, bf16[1024,512]{1,0:T(8,128)(2,1)S(1)} %bitcast.15, bf16[4,656,128]{2,1,0:T(8,128)(2,1)S(1)} %copy-done.4, bf16[4,656,128]{2,1,0:T(8,128)(2,1)S(1)} %copy-done.5), custom_call_target="tpu_custom_call" | custom-call | tf_op jit(solution)/shard_map/coupled/pallas_call | solution.py:23
  18.9 4.8 %collective-permute-done = bf16[512,512]{1,0:T(8,128)(2,1)} collective-permute-done((bf16[512,512]{1,0:T(8,128)(2,1)}, bf16[512,512]{1,0:T(8,128)(2,1)}, u32[]{:S(2)}, u32[]{:S(2)}) %collective-permute-start) | collective-permute-done | bytes 524320 | tf_op jit(solution)/shard_map/ppermute | solution.py:335
  23.7 1.4 %collective-permute-done.3.refs_2_.y_high.refs_3_ = bf16[4,656,128]{2,1,0:T(8,128)(2,1)S(1)} collective-permute-done((bf16[4,656,128]{2,1,0:T(8,128)(2,1)}, bf16[4,656,128]{2,1,0:T(8,128)(2,1)S(1)}, u32[]{:S(2)}, u32[]{:S(2)}) %collective-permute-start.3) | collective-permute-done | bytes 671776 | tf_op jit(solution)/shard_map/ppermute | solution.py:332
  25.1 0.5 collective-permute-start.4
  25.6 3.9 %coupled.4.refs_0_ = f32[8,128,128]{2,1,0:T(8,128)S(1)} custom-call(f32[8,128]{1,0:T(8,128)S(1)} %copy-done.14, bf16[1024,512]{1,0:T(8,128)(2,1)S(1)} %bitcast.16, f32[8,128,128]{2,1,0:T(8,128)S(1)} %coupled.3.refs_0_, bf16[4,656,128]{2,1,0:T(8,128)(2,1)S(1)} %collective-permute-done.2.refs_1_.x_low.refs_0_, ...), custom_call_target="tpu_custom_call" | custom-call | flops 20000000000 | tf_op jit(solution)/shard_map/coupled/pallas_call | solution.py:23
  29.6 2.1 %first_across.1 = (f32[4,128,128]{2,1,0:T(8,128)S(1)}, f32[4,128,128]{2,1,0:T(8,128)S(1)}) custom-call(bf16[4,656,128]{2,1,0:T(8,128)(2,1)S(1)} %collective-permute-done.2.refs_1_.x_low.refs_0_, bf16[4,656,128]{2,1,0:T(8,128)(2,1)S(1)} %collective-permute-done.3.refs_2_.y_high.refs_3_), custom_call_target="tpu_custom_call" | custom-call | tf_op jit(solution)/shard_map/first_across/pallas_call | solution.py:23
  31.7 2.0 %halves.1.refs_3_ = bf16[17,512,128]{2,1,0:T(8,128)(2,1)S(1)} custom-call(s32[8,2]{1,0:T(8,128)S(1)} %copy.28.uses_ref, bf16[1,512,512]{2,1,0:T(8,128)(2,1)S(1)} %copy-done.6, bf16[1,512,512]{2,1,0:T(8,128)(2,1)S(1)} %bitcast.24, bf16[1,512,512]{2,1,0:T(8,128)(2,1)} %bitcast.7.refs_2_, bf16[1,512,512]{2,1,0:T(8,128)(2,1)S(1)} %bitcast.23, ...), custom_call_target="tpu_custom_call" | custom-call | tf_op jit(solution)/shard_map/halves/pallas_call | solution.py:23
  33.7 4.3 %collective-permute-done.1 = bf16[512,512]{1,0:T(8,128)(2,1)} collective-permute-done((bf16[512,512]{1,0:T(8,128)(2,1)}, bf16[512,512]{1,0:T(8,128)(2,1)}, u32[]{:S(2)}, u32[]{:S(2)}) %collective-permute-start.1) | collective-permute-done | bytes 524320 | tf_op jit(solution)/shard_map/ppermute | solution.py:335
  38.0 2.2 %collective-permute-done.7 = bf16[512,512]{1,0:T(8,128)(2,1)} collective-permute-done((bf16[512,512]{1,0:T(8,128)(2,1)}, bf16[512,512]{1,0:T(8,128)(2,1)}, u32[]{:S(2)}, u32[]{:S(2)}) %collective-permute-start.7) | collective-permute-done | bytes 524320 | tf_op jit(solution)/shard_map/ppermute | solution.py:338
  40.3 1.8 %more_halves.1.refs_3_ = bf16[17,512,128]{2,1,0:T(8,128)(2,1)S(1)} custom-call(s32[8,2]{1,0:T(8,128)S(1)} %copy.28.uses_ref, bf16[1,512,512]{2,1,0:T(8,128)(2,1)} %bitcast.10.refs_0_, bf16[1,512,512]{2,1,0:T(8,128)(2,1)} %bitcast.11.refs_1_, bf16[1024,512]{1,0:T(8,128)(2,1)S(1)} %bitcast.18, ...), custom_call_target="tpu_custom_call", output_to_operand_aliasing={{}: (4, {})} | custom-call | tf_op jit(solution)/shard_map/more_halves/pallas_call | solution.py:23
  42.2 3.4 %second_across.1 = (bf16[8,128,128]{2,1,0:T(8,128)(2,1)S(1)}, bf16[8,128,128]{2,1,0:T(8,128)(2,1)S(1)}) custom-call(s32[1]{0:T(128)} %bitcast.9.upper_ref, f32[4,128,128]{2,1,0:T(8,128)S(1)} %get-tuple-element.36.low1, f32[4,128,128]{2,1,0:T(8,128)S(1)} %copy-done.12, bf16[4,656,128]{2,1,0:T(8,128)(2,1)S(1)} %copy-done.1, ...), custom_call_target="tpu_custom_call" | custom-call | tf_op jit(solution)/shard_map/second_across/pallas_call | solution.py:23
  45.6 0.6 collective-permute-start.10
  46.2 0.7 %collective-permute-start.11 = (bf16[8,128,128]{2,1,0:T(8,128)(2,1)S(1)}, bf16[8,128,128]{2,1,0:T(8,128)(2,1)S(1)}, u32[]{:S(2)}, u32[]{:S(2)}) collective-permute-start(bf16[8,128,128]{2,1,0:T(8,128)(2,1)S(1)} %get-tuple-element.41), channel_id=1, source_target_pairs={{0,16},{8,24},{16,0},{24,8},{1,17},{9,25},{17,1},{25,9},{2,18},{10... | collective-permute-start | bytes 786440 | tf_op jit(solution)/shard_map/ppermute | solution.py:332
  47.0 4.7 %coupled.5.refs_4_ = f32[8,128,128]{2,1,0:T(8,128)S(1)} custom-call(f32[8,128]{1,0:T(8,128)S(1)} %copy-done.14, bf16[1024,512]{1,0:T(8,128)(2,1)S(1)} %bitcast.19, f32[8,128,128]{2,1,0:T(8,128)S(1)} %copy-done.16, bf16[4,656,128]{2,1,0:T(8,128)(2,1)} %collective-permute-done.8.refs_1_, bf16[4,656,128]{2,1,0:T(8,128)(2,1)} %collective-permute-done.9.refs_2_), custom_call_target="tpu_custom_call" | custom-call | flops 20000000000 | tf_op jit(solution)/shard_map/coupled/pallas_call | solution.py:23
  51.7 0.8 %copy-done.7 = f32[8,128,128]{2,1,0:T(8,128)} copy-done((f32[8,128,128]{2,1,0:T(8,128)}, f32[8,128,128]{2,1,0:T(8,128)S(1)}, u32[]{:S(2)}) %copy-start.7) | copy-done | bytes 524312
  52.4 2.0 %collective-permute-done.6 = bf16[512,512]{1,0:T(8,128)(2,1)} collective-permute-done((bf16[512,512]{1,0:T(8,128)(2,1)}, bf16[512,512]{1,0:T(8,128)(2,1)}, u32[]{:S(2)}, u32[]{:S(2)}) %collective-permute-start.6) | collective-permute-done | bytes 524320 | tf_op jit(solution)/shard_map/ppermute | solution.py:335
  54.5 0.7 %copy-done.9 = bf16[8,128,128]{2,1,0:T(8,128)(2,1)} copy-done((bf16[8,128,128]{2,1,0:T(8,128)(2,1)}, bf16[8,128,128]{2,1,0:T(8,128)(2,1)S(1)}, u32[]{:S(2)}) %copy-start.9) | copy-done | bytes 262168
  55.3 2.2 %collective-permute-done.12 = bf16[512,512]{1,0:T(8,128)(2,1)} collective-permute-done((bf16[512,512]{1,0:T(8,128)(2,1)}, bf16[512,512]{1,0:T(8,128)(2,1)}, u32[]{:S(2)}, u32[]{:S(2)}) %collective-permute-start.12) | collective-permute-done | bytes 524320 | tf_op jit(solution)/shard_map/ppermute | solution.py:338
  57.4 1.0 %copy-done.8 = f32[8,128,128]{2,1,0:T(8,128)S(1)} copy-done((f32[8,128,128]{2,1,0:T(8,128)S(1)}, f32[8,128,128]{2,1,0:T(8,128)}, u32[]{:S(2)}) %copy-start.8) | copy-done | bytes 524312
  58.5 0.9 %copy-done.10 = bf16[8,128,128]{2,1,0:T(8,128)(2,1)S(1)} copy-done((bf16[8,128,128]{2,1,0:T(8,128)(2,1)S(1)}, bf16[8,128,128]{2,1,0:T(8,128)(2,1)}, u32[]{:S(2)}) %copy-start.10) | copy-done | bytes 262168
  59.4 3.2 %exchange.1 = f32[8,128,128]{2,1,0:T(8,128)} custom-call(s32[8,2]{1,0:T(8,128)S(1)} %copy.28.uses_ref, s32[8,2]{1,0:T(8,128)S(1)} %reshape.25.turn_ref, bf16[1,512,512]{2,1,0:T(8,128)(2,1)} %bitcast.12.refs_0_, bf16[1,512,512]{2,1,0:T(8,128)(2,1)} %bitcast.13.refs_1_, bf16[1024,512]{1,0:T(8,128)(2,1)S(1)} %bitcast.20, ...), custom_call_target="tpu_custom_call" | custom-call | tf_op jit(solution)/shard_map/exchange/pallas_call | solution.py:23
  (52 shorter events, 0.5 us)
Async XLA Ops:
  0.0 12.5 %copy-start.17 = (s32[8,2]{0,1:T(2,128)S(1)}, s32[8,2]{0,1:T(2,128)}, u32[]{:S(2)}) copy-start(s32[8,2]{0,1:T(2,128)} %param.9) | copy-start | bytes 196
  0.0 12.7 %copy-start.18 = (s32[8]{0:T(128)S(1)}, s32[8]{0:T(128)}, u32[]{:S(2)}) copy-start(s32[8]{0:T(128)} %param.8) | copy-start | bytes 100
  3.8 9.3 %copy-start.4 = (bf16[4,656,128]{2,1,0:T(8,128)(2,1)S(1)}, bf16[4,656,128]{2,1,0:T(8,128)(2,1)}, u32[]{:S(2)}) copy-start(bf16[4,656,128]{2,1,0:T(8,128)(2,1)} %get-tuple-element.38.refs_0_) | copy-start | bytes 2015236
  3.9 19.8 %collective-permute-start.2 = (bf16[4,656,128]{2,1,0:T(8,128)(2,1)}, bf16[4,656,128]{2,1,0:T(8,128)(2,1)S(1)}, u32[]{:S(2)}, u32[]{:S(2)}) collective-permute-start(bf16[4,656,128]{2,1,0:T(8,128)(2,1)} %get-tuple-element.38.refs_0_), channel_id=1, source_target_pairs={{0,8},{8,0},{16,24},{24,16},{1,9},{9,1},{17,25},{25,17},{2,10},{10... | collective-permute-start | bytes 2015240 | tf_op jit(solution)/shard_map/ppermute | solution.py:329
  6.9 18.2 %collective-permute-start.3 = (bf16[4,656,128]{2,1,0:T(8,128)(2,1)}, bf16[4,656,128]{2,1,0:T(8,128)(2,1)S(1)}, u32[]{:S(2)}, u32[]{:S(2)}) collective-permute-start(bf16[4,656,128]{2,1,0:T(8,128)(2,1)} %get-tuple-element.37.refs_1_), channel_id=1, source_target_pairs={{0,16},{8,24},{16,0},{24,8},{1,17},{9,25},{17,1},{25,9},{2,18},{10... | collective-permute-start | bytes 2015240 | tf_op jit(solution)/shard_map/ppermute | solution.py:332
  8.4 15.3 %collective-permute-start = (bf16[512,512]{1,0:T(8,128)(2,1)}, bf16[512,512]{1,0:T(8,128)(2,1)}, u32[]{:S(2)}, u32[]{:S(2)}) collective-permute-start(bf16[512,512]{1,0:T(8,128)(2,1)} %bitcast.21), channel_id=1, source_target_pairs={{0,2},{1,3},{2,4},{3,5},{4,6},{5,7},{6,0},{7,1},{8,10},{9,11},{10,... | collective-permute-start | bytes 1572872 | tf_op jit(solution)/shard_map/ppermute | solution.py:335
  10.0 32.2 %collective-permute-start.8 = (bf16[4,656,128]{2,1,0:T(8,128)(2,1)}, bf16[4,656,128]{2,1,0:T(8,128)(2,1)}, u32[]{:S(2)}, u32[]{:S(2)}) collective-permute-start(bf16[4,656,128]{2,1,0:T(8,128)(2,1)} %get-tuple-element.37.refs_1_), channel_id=1, source_target_pairs={{0,8},{8,0},{16,24},{24,16},{1,9},{9,1},{17,25},{25,17},{2,10},{10... | collective-permute-start | bytes 2015240 | tf_op jit(solution)/shard_map/ppermute | solution.py:329
  10.5 31.7 %collective-permute-start.9 = (bf16[4,656,128]{2,1,0:T(8,128)(2,1)}, bf16[4,656,128]{2,1,0:T(8,128)(2,1)}, u32[]{:S(2)}, u32[]{:S(2)}) collective-permute-start(bf16[4,656,128]{2,1,0:T(8,128)(2,1)} %get-tuple-element.38.refs_0_), channel_id=1, source_target_pairs={{0,16},{8,24},{16,0},{24,8},{1,17},{9,25},{17,1},{25,9},{2,18},{10... | collective-permute-start | bytes 2015240 | tf_op jit(solution)/shard_map/ppermute | solution.py:332
  11.0 14.6 %copy-start.14 = (f32[8,128]{1,0:T(8,128)S(1)}, f32[8,128]{1,0:T(8,128)}, u32[]{:S(2)}) copy-start(f32[8,128]{1,0:T(8,128)} %get-tuple-element.24.weight_ref) | copy-start | bytes 12292
  13.1 1.1 %copy-start.5 = (bf16[4,656,128]{2,1,0:T(8,128)(2,1)S(1)}, bf16[4,656,128]{2,1,0:T(8,128)(2,1)}, u32[]{:S(2)}) copy-start(bf16[4,656,128]{2,1,0:T(8,128)(2,1)} %get-tuple-element.37.refs_1_) | copy-start | bytes 2015236
  14.2 0.7 %copy-start.13 = (f32[8,128]{1,0:T(8,128)S(1)}, f32[8,128]{1,0:T(8,128)}, u32[]{:S(2)}) copy-start(f32[8,128]{1,0:T(8,128)} %get-tuple-element.24.weight_ref) | copy-start | bytes 12292
  14.9 10.2 %copy-start.6 = (bf16[1,512,512]{2,1,0:T(8,128)(2,1)S(1)}, bf16[1,512,512]{2,1,0:T(8,128)(2,1)}, u32[]{:S(2)}) copy-start(bf16[1,512,512]{2,1,0:T(8,128)(2,1)} %refs_0_.1) | copy-start | bytes 1572868
  23.7 14.4 %collective-permute-start.1 = (bf16[512,512]{1,0:T(8,128)(2,1)}, bf16[512,512]{1,0:T(8,128)(2,1)}, u32[]{:S(2)}, u32[]{:S(2)}) collective-permute-start(bf16[512,512]{1,0:T(8,128)(2,1)} %collective-permute-done), channel_id=1, source_target_pairs={{0,2},{1,3},{2,4},{3,5},{4,6},{5,7},{6,0},{7,1},{8,10},{9,11},{10,... | collective-permute-start | bytes 1572872 | tf_op jit(solution)/shard_map/ppermute | solution.py:335
  23.7 5.9 %copy-start = (bf16[4,656,128]{2,1,0:T(8,128)(2,1)}, bf16[4,656,128]{2,1,0:T(8,128)(2,1)S(1)}, u32[]{:S(2)}) copy-start(bf16[4,656,128]{2,1,0:T(8,128)(2,1)S(1)} %collective-permute-done.2.refs_1_.x_low.refs_0_) | copy-start | bytes 2015236
  25.1 4.5 %copy-start.2 = (bf16[4,656,128]{2,1,0:T(8,128)(2,1)}, bf16[4,656,128]{2,1,0:T(8,128)(2,1)S(1)}, u32[]{:S(2)}) copy-start(bf16[4,656,128]{2,1,0:T(8,128)(2,1)S(1)} %collective-permute-done.3.refs_2_.y_high.refs_3_) | copy-start | bytes 2015236
  25.1 6.6 %collective-permute-start.5 = (bf16[512,512]{1,0:T(8,128)(2,1)}, bf16[512,512]{1,0:T(8,128)(2,1)S(1)}, u32[]{:S(2)}, u32[]{:S(2)}) collective-permute-start(bf16[512,512]{1,0:T(8,128)(2,1)} %collective-permute-done), channel_id=1, source_target_pairs={{0,1},{1,0},{2,3},{3,2},{4,5},{5,4},{6,7},{7,6},{8,9},{9,8},{10,11... | collective-permute-start | bytes 1572872 | tf_op jit(solution)/shard_map/ppermute | solution.py:338
  25.1 6.6 %collective-permute-start.4 = (bf16[512,512]{1,0:T(8,128)(2,1)S(1)}, bf16[512,512]{1,0:T(8,128)(2,1)S(1)}, u32[]{:S(2)}, u32[]{:S(2)}) collective-permute-start(bf16[512,512]{1,0:T(8,128)(2,1)S(1)} %bitcast.22), channel_id=1, source_target_pairs={{0,1},{1,0},{2,3},{3,2},{4,5},{5,4},{6,7},{7,6},{8,9},{9,8},{10,11... | collective-permute-start | bytes 1572872 | tf_op jit(solution)/shard_map/ppermute | solution.py:338
  29.6 4.1 %copy-start.15 = (f32[8,128,128]{2,1,0:T(8,128)}, f32[8,128,128]{2,1,0:T(8,128)S(1)}, u32[]{:S(2)}) copy-start(f32[8,128,128]{2,1,0:T(8,128)S(1)} %coupled.4.refs_0_) | copy-start | bytes 1572868
  31.7 2.0 %copy-start.11 = (f32[4,128,128]{2,1,0:T(8,128)}, f32[4,128,128]{2,1,0:T(8,128)S(1)}, u32[]{:S(2)}) copy-start(f32[4,128,128]{2,1,0:T(8,128)S(1)} %get-tuple-element.33.low2) | copy-start | bytes 786436
  38.0 2.3 %collective-permute-start.7 = (bf16[512,512]{1,0:T(8,128)(2,1)}, bf16[512,512]{1,0:T(8,128)(2,1)}, u32[]{:S(2)}, u32[]{:S(2)}) collective-permute-start(bf16[512,512]{1,0:T(8,128)(2,1)} %collective-permute-done.1), channel_id=1, source_target_pairs={{0,1},{1,0},{2,3},{3,2},{4,5},{5,4},{6,7},{7,6},{8,9},{9,8},{10,11... | collective-permute-start | bytes 1572872 | tf_op jit(solution)/shard_map/ppermute | solution.py:338
  38.0 16.4 %collective-permute-start.6 = (bf16[512,512]{1,0:T(8,128)(2,1)}, bf16[512,512]{1,0:T(8,128)(2,1)}, u32[]{:S(2)}, u32[]{:S(2)}) collective-permute-start(bf16[512,512]{1,0:T(8,128)(2,1)} %collective-permute-done.1), channel_id=1, source_target_pairs={{0,2},{1,3},{2,4},{3,5},{4,6},{5,7},{6,0},{7,1},{8,10},{9,11},{10,... | collective-permute-start | bytes 1572872 | tf_op jit(solution)/shard_map/ppermute | solution.py:335
  40.3 1.9 %copy-start.1 = (bf16[4,656,128]{2,1,0:T(8,128)(2,1)S(1)}, bf16[4,656,128]{2,1,0:T(8,128)(2,1)}, u32[]{:S(2)}) copy-start(bf16[4,656,128]{2,1,0:T(8,128)(2,1)} %copy-done) | copy-start | bytes 2015236
  40.3 1.9 %copy-start.3 = (bf16[4,656,128]{2,1,0:T(8,128)(2,1)S(1)}, bf16[4,656,128]{2,1,0:T(8,128)(2,1)}, u32[]{:S(2)}) copy-start(bf16[4,656,128]{2,1,0:T(8,128)(2,1)} %copy-done.2) | copy-start | bytes 2015236
  40.3 1.9 %copy-start.12 = (f32[4,128,128]{2,1,0:T(8,128)S(1)}, f32[4,128,128]{2,1,0:T(8,128)}, u32[]{:S(2)}) copy-start(f32[4,128,128]{2,1,0:T(8,128)} %copy-done.11) | copy-start | bytes 786436
  42.1 4.9 %copy-start.16 = (f32[8,128,128]{2,1,0:T(8,128)S(1)}, f32[8,128,128]{2,1,0:T(8,128)}, u32[]{:S(2)}) copy-start(f32[8,128,128]{2,1,0:T(8,128)} %copy-done.15) | copy-start | bytes 1572868
  45.6 8.8 %collective-permute-start.10 = (bf16[8,128,128]{2,1,0:T(8,128)(2,1)S(1)}, bf16[8,128,128]{2,1,0:T(8,128)(2,1)S(1)}, u32[]{:S(2)}, u32[]{:S(2)}) collective-permute-start(bf16[8,128,128]{2,1,0:T(8,128)(2,1)S(1)} %get-tuple-element.39), channel_id=1, source_target_pairs={{0,8},{8,0},{16,24},{24,16},{1,9},{9,1},{17,25},{25,17},{2,10},{10... | collective-permute-start | bytes 786440 | tf_op jit(solution)/shard_map/ppermute | solution.py:329
  46.2 8.2 %collective-permute-start.11 = (bf16[8,128,128]{2,1,0:T(8,128)(2,1)S(1)}, bf16[8,128,128]{2,1,0:T(8,128)(2,1)S(1)}, u32[]{:S(2)}, u32[]{:S(2)}) collective-permute-start(bf16[8,128,128]{2,1,0:T(8,128)(2,1)S(1)} %get-tuple-element.41), channel_id=1, source_target_pairs={{0,16},{8,24},{16,0},{24,8},{1,17},{9,25},{17,1},{25,9},{2,18},{10... | collective-permute-start | bytes 786440 | tf_op jit(solution)/shard_map/ppermute | solution.py:332
  51.6 0.8 %copy-start.7 = (f32[8,128,128]{2,1,0:T(8,128)}, f32[8,128,128]{2,1,0:T(8,128)S(1)}, u32[]{:S(2)}) copy-start(f32[8,128,128]{2,1,0:T(8,128)S(1)} %coupled.5.refs_4_) | copy-start | bytes 1572868
  54.5 0.7 %copy-start.9 = (bf16[8,128,128]{2,1,0:T(8,128)(2,1)}, bf16[8,128,128]{2,1,0:T(8,128)(2,1)S(1)}, u32[]{:S(2)}) copy-start(bf16[8,128,128]{2,1,0:T(8,128)(2,1)S(1)} %collective-permute-done.11.refs_6_) | copy-start | bytes 786436
  55.2 2.3 %collective-permute-start.12 = (bf16[512,512]{1,0:T(8,128)(2,1)}, bf16[512,512]{1,0:T(8,128)(2,1)}, u32[]{:S(2)}, u32[]{:S(2)}) collective-permute-start(bf16[512,512]{1,0:T(8,128)(2,1)} %collective-permute-done.6), channel_id=1, source_target_pairs={{0,1},{1,0},{2,3},{3,2},{4,5},{5,4},{6,7},{7,6},{8,9},{9,8},{10,11... | collective-permute-start | bytes 1572872 | tf_op jit(solution)/shard_map/ppermute | solution.py:338
  57.4 1.0 %copy-start.8 = (f32[8,128,128]{2,1,0:T(8,128)S(1)}, f32[8,128,128]{2,1,0:T(8,128)}, u32[]{:S(2)}) copy-start(f32[8,128,128]{2,1,0:T(8,128)} %copy-done.7) | copy-start | bytes 1572868
  58.5 0.9 %copy-start.10 = (bf16[8,128,128]{2,1,0:T(8,128)(2,1)S(1)}, bf16[8,128,128]{2,1,0:T(8,128)(2,1)}, u32[]{:S(2)}) copy-start(bf16[8,128,128]{2,1,0:T(8,128)(2,1)} %copy-done.9) | copy-start | bytes 786436
where the time goes:
time: 63.1 us; the launch traced here: 62.6 us
  Pallas kernels  28.9 us (46%)
  waiting for transfers between devices  17 us (27%)
  starting transfers between devices  9.01 us (14%)
  local copies, waits for them, and re-layouts  7.13 us (11%)
    pallas_call x8, Pallas kernels, call_kernel(): pl.pallas_call(body, out_shape=out_shape, in_specs=[SMEM_SPEC] * len(smem...  25 us
    ppermute x3, waiting for transfers between devices, next_chip(): lax.ppermute(value, 'dev', [(d, (d + 2) % n_dev) for d in range(n_dev)])  11.1 us
    unnamed x39, local copies, waits for them, and re-layouts  5.4 us
    ppermute x4, waiting for transfers between devices, other_core(): return lax.ppermute(value, 'dev', [(d, d ^ 1) for d in range(n_dev)])  4.42 us
    ppermute x3, starting transfers between devices, along_x(): return lax.ppermute(value, 'grp', [(g, g ^ 1) for g in range(n_grp)])  4.14 us
    pallas_call x1, Pallas kernels, pack(): pl.pallas_call(functools.partial(pack_kernel, scale), out_shape=(packed,...  3.83 us
    ppermute x3, starting transfers between devices, along_y(): return lax.ppermute(value, 'grp', [(g, g ^ 2) for g in range(n_grp)])  2.77 us
    ppermute x3, starting transfers between devices, next_chip(): lax.ppermute(value, 'dev', [(d, (d + 2) % n_dev) for d in range(n_dev)])  1.58 us
  transfers between devices with their start and end apart: 13, of which 6 were waited for; matrix products, arithmetic and copies ran while one was open for 3% of the time, Pallas kernels for 35%

commit v1 on v0

--- a/solution.py
+++ b/solution.py
@@ -10,8 +10,9 @@
 
 MARGIN = 0
 PACK_LIMIT = 56 * 1024 * 1024
+RING_CHIPS = 4
 DECLARED = 20_000_000_000
-OWN_COST, FIRST_COST, SECOND_COST, LAST_COST = 0, 0, 0, DECLARED
+OWN_COST, FIRST_COST, SECOND_COST, LAST_COST = DECLARED, 0, 0, DECLARED
 SMEM_SPEC = pl.BlockSpec(memory_space=pltpu.SMEM)
 VMEM_SPEC = pl.BlockSpec(memory_space=pltpu.VMEM)
 HBM_SPEC = pl.BlockSpec(memory_space=pltpu.HBM)
@@ -75,16 +76,26 @@
                 ).astype(jnp.bfloat16)
 
 
-def coupled_kernel(lanes, begun, weight_ref, left_ref, *refs):
-    *acc_ref, one_ref, two_ref, out_ref, inter_ref, proj_ref = refs
+def coupled_kernel(lanes, weight_ref, left_ref, acc_ref, one_ref, two_ref, out_ref, inter_ref, proj_ref):
     pairs, pno, _ = out_ref.shape
     half, orbs = pairs // 2, left_ref.shape[1]
     own = Side(left_ref, (), orbs, pno)
     other = Side(None, [ref.at[k] for ref in (one_ref, two_ref) for k in range(half)], orbs, pno)
     project(own, other, lambda p, c: weight_ref[p, lanes[c]], inter_ref, proj_ref)
     for p in range(pairs):
-        total = one_sum(proj_ref, inter_ref, p, pno)
-        out_ref[p] = acc_ref[0][p] + total if begun else total
+        out_ref[p] = acc_ref[p] + one_sum(proj_ref, inter_ref, p, pno)
+
+
+def own_kernel(weight_ref, low_ref, high_ref, out_ref, left_ref, inter_ref, proj_ref):
+    pairs, pno, _ = out_ref.shape
+    orbs = left_ref.shape[1]
+    packs = [ref.at[k] for ref in (low_ref, high_ref) for k in range(pairs // 2)]
+    for p, pack_ref in enumerate(packs):
+        left_ref[p * pno : (p + 1) * pno, :] = pack_ref[:orbs, :].T
+    own = Side(left_ref, packs, orbs, pno)
+    project(own, own, lambda p, c: weight_ref[p, c], inter_ref, proj_ref)
+    for p in range(pairs):
+        out_ref[p] = one_sum(proj_ref, inter_ref, p, pno)
 
 
 def one_sum(proj_ref, inter_ref, p, pno):
@@ -152,13 +163,20 @@
             back_y[half + k] = (low2[k] + two(k)).astype(jnp.bfloat16)
 
 
+def own_coupled(weights, own, orbs, flops):
+    half, _, pno = own[0].shape
+    rows = 2 * half * pno
+    shapes = (jax.ShapeDtypeStruct((2 * half, pno, pno), jnp.float32), jax.ShapeDtypeStruct((rows, orbs), jnp.bfloat16))
+    scratch = [pltpu.VMEM((rows, rows), jnp.bfloat16)] * 2
+    return call_kernel(own_kernel, shapes, scratch, "own_coupled", (weights,), own, flops)
+
+
 def add_coupled(lanes, weights, own_t, acc, received, flops):
-    half, _, pno = received[0].shape
-    rows, pairs = own_t.shape[0], 2 * half
-    shape = jax.ShapeDtypeStruct((pairs, pno, pno), jnp.float32)
-    body = functools.partial(coupled_kernel, lanes, acc is not None)
-    vmem_args = (own_t, *received) if acc is None else (own_t, acc, *received)
-    return call_kernel(body, shape, [pltpu.VMEM((rows, rows), jnp.bfloat16)] * 2, "coupled", (weights,), vmem_args, flops)
+    rows = own_t.shape[0]
+    scratch = [pltpu.VMEM((rows, rows), jnp.bfloat16)] * 2
+    shape = jax.ShapeDtypeStruct(acc.shape, jnp.float32)
+    body = functools.partial(coupled_kernel, lanes)
+    return call_kernel(body, shape, scratch, "coupled", (weights,), (own_t, acc, *received), flops)
 
 
 def across(body, name, scalars, vmem_args, half, shapes, orbs, flops):
@@ -216,7 +234,7 @@
         late_ref[2 * (k - base) + use] = half
 
     def half(p, side):
-        k = turn_ref[p, side]
+        k = turn_ref[2 * p + side]
         late = jnp.where(uses_ref[k, 0] == 2 * p + side, 0, 1) + 2 * jnp.maximum(k - base, 0)
         return jnp.where(k < base, early_ref[2 * p + side], late_ref[late])
 
@@ -250,23 +268,11 @@
     )
 
 
-def slab_uses(slab_owner, pair_orbs, order):
-    n_dev = order.shape[0]
-    sides = pair_orbs.shape[0] * 2
-    table = jnp.arange(n_dev, dtype=jnp.int32)
-    position = jnp.sum(jnp.where(pair_orbs.reshape(sides)[:, None] == table, slab_owner, 0), axis=1)
-    turn = jnp.sum(jnp.where(position[:, None] == table, order, 0), axis=1).astype(jnp.int32)
-    hit = turn[:, None] == table
-    side = jnp.arange(sides, dtype=jnp.int32)[:, None]
-    last = jnp.max(jnp.where(hit, side, -1), axis=0)
-    first = jnp.min(jnp.where(hit, side, sides), axis=0)
-    return turn.reshape(-1, 2), jnp.stack([first, jnp.where(last < 0, sides, last)], axis=1)
-
-
-def pack_kernel(scale, group_ref, coupled_ref, length_ref, base_ref, amp_ref, *refs):
-    low_ref, high_ref, weight_ref, held_ref, sems = refs
+def pack_kernel(scale, chips, group_ref, me_ref, coupled_ref, length_ref, owner_ref, orbs_ref, base_ref, amp_ref, *refs):
+    low_ref, high_ref, weight_ref, uses_ref, turn_ref, held_ref, sems = refs
     pairs, orbs, pno = base_ref.shape
     half = pairs // 2
+    group, me = group_ref[0], me_ref[0]
     copies = []
 
     def copy(ref, k, row, sem):
@@ -282,7 +288,7 @@
         counts = jnp.zeros((1, pno), jnp.float32)
         for s in range(coupled_ref.shape[1]):
             named = coupled_ref[p, s]
-            at = (lax.div(named, pairs) ^ group_ref[0]) * pairs + lax.rem(named, pairs)
+            at = (lax.div(named, pairs) ^ group) * pairs + lax.rem(named, pairs)
             counts += jnp.where(lane == jnp.where(s < length_ref[p], at, -1), scale, 0.0)
         weight_ref[p : p + 1, :] = counts
         rows = slice(orbs + amp_ref.shape[1], held_ref.shape[2])
@@ -294,22 +300,46 @@
     ]
     for store in stores:
         store.start()
+
+    sides = 2 * pairs
+
+    def clear(k, carry):
+        uses_ref[k, 0] = sides
+        uses_ref[k, 1] = sides
+        return carry
+
+    lax.fori_loop(0, uses_ref.shape[0], clear, 0)
+    for f in range(sides):
+        position = owner_ref[orbs_ref[f % 2, f // 2]]
+        k = position
+        if chips <= RING_CHIPS:
+            steps = lax.rem(lax.div(me, 2) - lax.div(position, 2) + chips, chips)
+            k = 2 * steps + (lax.rem(position, 2) ^ lax.rem(me, 2))
+        turn_ref[f] = k
+        uses_ref[k, 1] = uses_ref[k, 0]
+        uses_ref[k, 0] = f
     for store in stores:
         store.wait()
 
 
-def pack(group, coupled, coupled_len, bases, amps, scale):
+def pack(group, me, chips, coupled, coupled_len, slab_owner, pair_orbs, bases, amps):
     pairs, orbs, pno = bases.shape
     packed = jax.ShapeDtypeStruct((pairs // 2, orbs + amps.shape[1] + 16, pno), bases.dtype)
     return pl.pallas_call(
-        functools.partial(pack_kernel, scale),
-        out_shape=(packed, packed, jax.ShapeDtypeStruct((pairs, pno), jnp.float32)),
-        in_specs=[SMEM_SPEC] * 3 + [HBM_SPEC] * 2,
-        out_specs=(HBM_SPEC, HBM_SPEC, VMEM_SPEC),
+        functools.partial(pack_kernel, orbs / pno, chips),
+        out_shape=(
+            packed,
+            packed,
+            jax.ShapeDtypeStruct((pairs, pno), jnp.float32),
+            jax.ShapeDtypeStruct((slab_owner.shape[0], 2), jnp.int32),
+            jax.ShapeDtypeStruct((2 * pairs,), jnp.int32),
+        ),
+        in_specs=[SMEM_SPEC] * 6 + [HBM_SPEC] * 2,
+        out_specs=(HBM_SPEC, HBM_SPEC, VMEM_SPEC, SMEM_SPEC, SMEM_SPEC),
         scratch_shapes=[pltpu.VMEM((2,) + packed.shape, bases.dtype), pltpu.SemaphoreType.DMA((6,))],
         compiler_params=pltpu.CompilerParams(vmem_limit_bytes=PACK_LIMIT),
         name="pack",
-    )(group, coupled, coupled_len, bases, amps)
+    )(group, me, coupled, coupled_len, slab_owner, pair_orbs.T, bases, amps)
 
 
 def after(value, *earlier):
@@ -321,7 +351,6 @@
     pairs, orbs, pno = domain_bases.shape
     group, me = lax.axis_index("grp"), lax.axis_index("dev")
     chips = n_dev // 2
-    chip, core = me // 2, me % 2
 
     half = pairs // 2
 
@@ -337,27 +366,22 @@
     def other_core(value):
         return lax.ppermute(value, "dev", [(d, d ^ 1) for d in range(n_dev)])
 
-    own_lo, own_hi, weights = pack(
-        group.astype(jnp.int32).reshape(1), coupled, coupled_len, domain_bases, amplitudes, orbs / pno
-    )
-    own_t = jnp.swapaxes(domain_bases, 1, 2).reshape(pairs * pno, orbs)
-    upper = jnp.where(group >= 2, 1, 0).astype(jnp.int32).reshape(1)
+    own_lo, own_hi, weights, uses, turns = pack(
+        group.astype(jnp.int32).reshape(1), me.astype(jnp.int32).reshape(1), chips, coupled, coupled_len, slab_owner, pair_orbs, domain_bases, amplitudes
+    )
+    upper = (group // 2).astype(jnp.int32).reshape(1)
 
     x_lo, y_hi = along_x(own_lo), along_y(own_hi)
     x_hi, y_lo = along_x(after(own_hi, own_lo)), along_y(after(own_lo, own_hi))
 
     slab = integral_slabs[0]
-    around = chips <= 4
-    position = jnp.arange(n_dev, dtype=jnp.int32)
-    order, ahead = position, n_dev // 2
-    acc = add_coupled(list(range(pairs)), weights, own_t, None, (own_lo, own_hi), OWN_COST)
+    around = chips <= RING_CHIPS
+    ahead = 6 if around else n_dev // 2
     if around:
-        order = 2 * ((chip - position // 2) % chips) + jnp.where(position % 2 == core, 0, 1)
-        ahead = 6
         round1 = next_chip(slab)
-        round2 = next_chip(after(round1, acc))
+        round2 = next_chip(round1)
         swap0, swap1 = other_core(after(slab, x_lo, y_hi)), other_core(after(round1, x_lo, y_hi))
-    turns, uses = slab_uses(slab_owner, pair_orbs, order)
+    acc, own_t = own_coupled(weights, (after(own_lo, round1) if around else own_lo, own_hi), orbs, OWN_COST)
 
     lanes = [*range(pairs, pairs + half), *range(2 * pairs + half, 3 * pairs)]
     acc = add_coupled(lanes, weights, own_t, acc, (x_lo, y_hi), DECLARED)

time: 63.1 us -> 61.3 us (0.971)
  local copies, waits for them, and re-layouts: 7.13 us -> 2.92 us
  waiting for transfers between devices: 17 us -> 19 us
  starting transfers between devices: 9.01 us -> 10.6 us
  Pallas kernels: 28.9 us -> 28.2 us
    unnamed x39 -> x30, local copies, waits for them, and re-layouts: 5.4 us -> 2.92 us
    ppermute x3, starting transfers between devices: 1.58 us -> 3.09 us  [next_chip(): lax.ppermute(value, 'dev', [(d, (d + 2) % n_dev) for d in range(n_dev)])]
    transpose x1 -> x0, local copies, waits for them, and re-layouts: 1.49 us -> none  [on_device(): own_t = jnp.swapaxes(domain_bases, 1, 2).reshape(pairs * pno, orbs)]
    ppermute x3, waiting for transfers between devices: 0.01 us -> 0.9 us  [along_x(): return lax.ppermute(value, 'grp', [(g, g ^ 1) for g in range(n_grp)])]
    ppermute x3, starting transfers between devices: 2.77 us -> 3.55 us  [along_y(): return lax.ppermute(value, 'grp', [(g, g ^ 2) for g in range(n_grp)])]
    ppermute x3, waiting for transfers between devices: 1.41 us -> 2.16 us  [along_y(): return lax.ppermute(value, 'grp', [(g, g ^ 2) for g in range(n_grp)])]
    ppermute x3, starting transfers between devices: 4.14 us -> 3.4 us  [along_x(): return lax.ppermute(value, 'grp', [(g, g ^ 1) for g in range(n_grp)])]
  transfers between devices with their start and end apart: 13 -> 13, of which waited for: 6 -> 8; matrix products, arithmetic and copies ran while one was open for 3% -> 0% of each run, Pallas kernels for 35% -> 42%
where the time goes in v1:
time: 61.3 us; the launch traced here: 60.9 us
  Pallas kernels  28.2 us (46%)
  waiting for transfers between devices  19 us (31%)
  starting transfers between devices  10.6 us (17%)
  local copies, waits for them, and re-layouts  2.92 us (5%)
    pallas_call x8, Pallas kernels, call_kernel(): pl.pallas_call(body, out_shape=out_shape, in_specs=[SMEM_SPEC] * len(smem...  24.4 us
    ppermute x3, waiting for transfers between devices, next_chip(): lax.ppermute(value, 'dev', [(d, (d + 2) % n_dev) for d in range(n_dev)])  11.7 us
    ppermute x4, waiting for transfers between devices, other_core(): return lax.ppermute(value, 'dev', [(d, d ^ 1) for d in range(n_dev)])  4.16 us
    pallas_call x1, Pallas kernels, pack(): pl.pallas_call(functools.partial(pack_kernel, orbs / pno, chips), out_sha...  3.77 us
    ppermute x3, starting transfers between devices, along_y(): return lax.ppermute(value, 'grp', [(g, g ^ 2) for g in range(n_grp)])  3.55 us
    ppermute x3, starting transfers between devices, along_x(): return lax.ppermute(value, 'grp', [(g, g ^ 1) for g in range(n_grp)])  3.4 us
    ppermute x3, starting transfers between devices, next_chip(): lax.ppermute(value, 'dev', [(d, (d + 2) % n_dev) for d in range(n_dev)])  3.09 us
    unnamed x30, local copies, waits for them, and re-layouts  2.92 us
  transfers between devices with their start and end apart: 13, of which 8 were waited for; matrix products, arithmetic and copies ran while one was open for 0% of the time, Pallas kernels for 42%

profile of v1, /device:TPU:0, one launch (start us, length us, event | category | flops | bytes accessed | tf_op | source)
XLA Modules:
  0.0 60.9 jit_solution(14320708406937652498)
XLA Ops:
  0.0 3.0 %collective-permute-start = (bf16[512,512]{1,0:T(8,128)(2,1)}, bf16[512,512]{1,0:T(8,128)(2,1)}, u32[]{:S(2)}, u32[]{:S(2)}) collective-permute-start(bf16[512,512]{1,0:T(8,128)(2,1)} %bitcast.12), channel_id=1, source_target_pairs={{0,2},{1,3},{2,4},{3,5},{4,6},{5,7},{6,0},{7,1},{8,10},{9,11},{10,... | collective-permute-start | bytes 1572872 | tf_op jit(solution)/shard_map/ppermute | solution.py:364
  3.0 3.8 %pack.1 = (bf16[4,656,128]{2,1,0:T(8,128)(2,1)}, bf16[4,656,128]{2,1,0:T(8,128)(2,1)}, f32[8,128]{1,0:T(8,128)}, s32[8,2]{1,0:T(8,128)}, s32[16]{0:T(128)}) custom-call(s32[1]{0:T(128)} %bitcast.group_ref, s32[1]{0:T(128)} %bitcast.1.me_ref, s32[8,32]{1,0:T(8,128)} %coupled_ref.1, s32[8]{0:T(128)} %length_ref.1, s32[8]{0:T(128)} %owner_ref.1, ...), custom_call_target="tpu_custom_call" | custom-call | tf_op jit(solution)/shard_map/pack/pallas_call | solution.py:328
  6.8 1.6 %collective-permute-start.2 = (bf16[4,656,128]{2,1,0:T(8,128)(2,1)}, bf16[4,656,128]{2,1,0:T(8,128)(2,1)S(1)}, u32[]{:S(2)}, u32[]{:S(2)}) collective-permute-start(bf16[4,656,128]{2,1,0:T(8,128)(2,1)} %get-tuple-element.46.low_ref), channel_id=1, source_target_pairs={{0,8},{8,0},{16,24},{24,16},{1,9},{9,1},{17,25},{25,17},{2,10},{10... | collective-permute-start | bytes 2015240 | tf_op jit(solution)/shard_map/ppermute | solution.py:358
  8.4 1.5 %collective-permute-start.3 = (bf16[4,656,128]{2,1,0:T(8,128)(2,1)}, bf16[4,656,128]{2,1,0:T(8,128)(2,1)S(1)}, u32[]{:S(2)}, u32[]{:S(2)}) collective-permute-start(bf16[4,656,128]{2,1,0:T(8,128)(2,1)} %get-tuple-element.45.high_ref), channel_id=1, source_target_pairs={{0,16},{8,24},{16,0},{24,8},{1,17},{9,25},{17,1},{25,9},{2,18},{10... | collective-permute-start | bytes 2015240 | tf_op jit(solution)/shard_map/ppermute | solution.py:361
  9.9 0.5 collective-permute-start.8
  10.4 0.5 collective-permute-start.9
  10.9 6.4 %collective-permute-done = bf16[512,512]{1,0:T(8,128)(2,1)} collective-permute-done((bf16[512,512]{1,0:T(8,128)(2,1)}, bf16[512,512]{1,0:T(8,128)(2,1)}, u32[]{:S(2)}, u32[]{:S(2)}) %collective-permute-start) | collective-permute-done | bytes 524320 | tf_op jit(solution)/shard_map/ppermute | solution.py:364
  17.3 1.1 %copy-done.9 = bf16[4,656,128]{2,1,0:T(8,128)(2,1)S(1)} copy-done((bf16[4,656,128]{2,1,0:T(8,128)(2,1)S(1)}, bf16[4,656,128]{2,1,0:T(8,128)(2,1)}, u32[]{:S(2)}) %copy-start.9) | copy-done | bytes 671768
  18.4 1.1 %copy-done.10 = bf16[4,656,128]{2,1,0:T(8,128)(2,1)S(1)} copy-done((bf16[4,656,128]{2,1,0:T(8,128)(2,1)S(1)}, bf16[4,656,128]{2,1,0:T(8,128)(2,1)}, u32[]{:S(2)}) %copy-start.10) | copy-done | bytes 671768
  19.5 0.7 %copy-done.11 = f32[8,128]{1,0:T(8,128)S(1)} copy-done((f32[8,128]{1,0:T(8,128)S(1)}, f32[8,128]{1,0:T(8,128)}, u32[]{:S(2)}) %copy-start.11) | copy-done | bytes 4120
  20.2 4.0 %own_coupled.1 = (f32[8,128,128]{2,1,0:T(8,128)S(1)}, bf16[1024,512]{1,0:T(8,128)(2,1)S(1)}) custom-call(f32[8,128]{1,0:T(8,128)S(1)} %copy-done.11, bf16[4,656,128]{2,1,0:T(8,128)(2,1)S(1)} %copy-done.9, bf16[4,656,128]{2,1,0:T(8,128)(2,1)S(1)} %copy-done.10), custom_call_target="tpu_custom_call" | custom-call | flops 20000000000 | tf_op jit(solution)/shard_map/own_coupled/pallas_call | solution.py:24
  24.1 0.1 collective-permute-start.1
  24.2 0.9 %collective-permute-done.2.one_ref.x_low.refs_0_ = bf16[4,656,128]{2,1,0:T(8,128)(2,1)S(1)} collective-permute-done((bf16[4,656,128]{2,1,0:T(8,128)(2,1)}, bf16[4,656,128]{2,1,0:T(8,128)(2,1)S(1)}, u32[]{:S(2)}, u32[]{:S(2)}) %collective-permute-start.2) | collective-permute-done | bytes 671776 | tf_op jit(solution)/shard_map/ppermute | solution.py:358
  25.1 1.5 %collective-permute-done.3.two_ref.y_high.refs_3_ = bf16[4,656,128]{2,1,0:T(8,128)(2,1)S(1)} collective-permute-done((bf16[4,656,128]{2,1,0:T(8,128)(2,1)}, bf16[4,656,128]{2,1,0:T(8,128)(2,1)S(1)}, u32[]{:S(2)}, u32[]{:S(2)}) %collective-permute-start.3) | collective-permute-done | bytes 671776 | tf_op jit(solution)/shard_map/ppermute | solution.py:361
  26.6 0.0 collective-permute-start.4
  26.6 0.5 collective-permute-start.5
  27.1 4.0 %coupled.2.acc_ref = f32[8,128,128]{2,1,0:T(8,128)S(1)} custom-call(f32[8,128]{1,0:T(8,128)S(1)} %copy-done.11, bf16[1024,512]{1,0:T(8,128)(2,1)S(1)} %get-tuple-element.42.left_ref.refs_4_.refs_2_, f32[8,128,128]{2,1,0:T(8,128)S(1)} %get-tuple-element.37.acc_ref, bf16[4,656,128]{2,1,0:T(8,128)(2,1)S(1)} %collective-permute-done.2.one_ref.x_low.refs_0_, ...), custom_call_target="tpu_custom_call" | custom-call | flops 20000000000 | tf_op jit(solution)/shard_map/coupled/pallas_call | solution.py:24
  31.1 0.0 copy-start.13
  31.1 2.1 %first_across.1 = (f32[4,128,128]{2,1,0:T(8,128)S(1)}, f32[4,128,128]{2,1,0:T(8,128)S(1)}) custom-call(bf16[4,656,128]{2,1,0:T(8,128)(2,1)S(1)} %collective-permute-done.2.one_ref.x_low.refs_0_, bf16[4,656,128]{2,1,0:T(8,128)(2,1)S(1)} %collective-permute-done.3.two_ref.y_high.refs_3_), custom_call_target="tpu_custom_call" | custom-call | tf_op jit(solution)/shard_map/first_across/pallas_call | solution.py:24
  33.2 2.0 %halves.1.refs_3_ = bf16[17,512,128]{2,1,0:T(8,128)(2,1)S(1)} custom-call(s32[8,2]{1,0:T(8,128)S(1)} %copy-done.7, bf16[1,512,512]{2,1,0:T(8,128)(2,1)S(1)} %copy-done.4, bf16[1,512,512]{2,1,0:T(8,128)(2,1)S(1)} %bitcast.14, bf16[1,512,512]{2,1,0:T(8,128)(2,1)} %bitcast.5.refs_2_, bf16[1,512,512]{2,1,0:T(8,128)(2,1)S(1)} %bitcast.15, ...), custom_call_target="tpu_custom_call" | custom-call | tf_op jit(solution)/shard_map/halves/pallas_call | solution.py:24
  35.2 4.2 %collective-permute-done.1 = bf16[512,512]{1,0:T(8,128)(2,1)} collective-permute-done((bf16[512,512]{1,0:T(8,128)(2,1)}, bf16[512,512]{1,0:T(8,128)(2,1)}, u32[]{:S(2)}, u32[]{:S(2)}) %collective-permute-start.1) | collective-permute-done | bytes 524320 | tf_op jit(solution)/shard_map/ppermute | solution.py:364
  39.4 2.2 %collective-permute-done.7 = bf16[512,512]{1,0:T(8,128)(2,1)} collective-permute-done((bf16[512,512]{1,0:T(8,128)(2,1)}, bf16[512,512]{1,0:T(8,128)(2,1)}, u32[]{:S(2)}, u32[]{:S(2)}) %collective-permute-start.7) | collective-permute-done | bytes 524320 | tf_op jit(solution)/shard_map/ppermute | solution.py:367
  41.7 1.8 %more_halves.1.refs_3_ = bf16[17,512,128]{2,1,0:T(8,128)(2,1)S(1)} custom-call(s32[8,2]{1,0:T(8,128)S(1)} %copy-done.7, bf16[1,512,512]{2,1,0:T(8,128)(2,1)} %bitcast.8.refs_0_, bf16[1,512,512]{2,1,0:T(8,128)(2,1)} %bitcast.9.refs_1_, bf16[1024,512]{1,0:T(8,128)(2,1)S(1)} %get-tuple-element.42.left_ref.refs_4_.refs_2_, ...), custom_call_target="tpu_custom_call", output_to_operand_aliasing={{}: (4, {})} | custom-call | tf_op jit(solution)/shard_map/more_halves/pallas_call | solution.py:24
  43.5 0.0 copy-start.14
  43.6 3.4 %second_across.1 = (bf16[8,128,128]{2,1,0:T(8,128)(2,1)S(1)}, bf16[8,128,128]{2,1,0:T(8,128)(2,1)S(1)}) custom-call(s32[1]{0:T(128)} %bitcast.7.upper_ref, f32[4,128,128]{2,1,0:T(8,128)S(1)} %get-tuple-element.44.low1, f32[4,128,128]{2,1,0:T(8,128)S(1)} %copy-done.6, bf16[4,656,128]{2,1,0:T(8,128)(2,1)S(1)} %copy-done.1, ...), custom_call_target="tpu_custom_call" | custom-call | tf_op jit(solution)/shard_map/second_across/pallas_call | solution.py:24
  47.0 1.3 %collective-permute-start.10 = (bf16[8,128,128]{2,1,0:T(8,128)(2,1)S(1)}, bf16[8,128,128]{2,1,0:T(8,128)(2,1)S(1)}, u32[]{:S(2)}, u32[]{:S(2)}) collective-permute-start(bf16[8,128,128]{2,1,0:T(8,128)(2,1)S(1)} %get-tuple-element.47), channel_id=1, source_target_pairs={{0,8},{8,0},{16,24},{24,16},{1,9},{9,1},{17,25},{25,17},{2,10},{10... | collective-permute-start | bytes 786440 | tf_op jit(solution)/shard_map/ppermute | solution.py:358
  48.3 1.5 %collective-permute-start.11 = (bf16[8,128,128]{2,1,0:T(8,128)(2,1)S(1)}, bf16[8,128,128]{2,1,0:T(8,128)(2,1)S(1)}, u32[]{:S(2)}, u32[]{:S(2)}) collective-permute-start(bf16[8,128,128]{2,1,0:T(8,128)(2,1)S(1)} %get-tuple-element.49), channel_id=1, source_target_pairs={{0,16},{8,24},{16,0},{24,8},{1,17},{9,25},{17,1},{25,9},{2,18},{10... | collective-permute-start | bytes 786440 | tf_op jit(solution)/shard_map/ppermute | solution.py:361
  49.9 4.7 %coupled.3.refs_4_ = f32[8,128,128]{2,1,0:T(8,128)S(1)} custom-call(f32[8,128]{1,0:T(8,128)S(1)} %copy-done.12, bf16[1024,512]{1,0:T(8,128)(2,1)S(1)} %get-tuple-element.42.left_ref.refs_4_.refs_2_, f32[8,128,128]{2,1,0:T(8,128)S(1)} %copy-done.14, bf16[4,656,128]{2,1,0:T(8,128)(2,1)} %collective-permute-done.8.refs_1_.one_ref, ...), custom_call_target="tpu_custom_call" | custom-call | flops 20000000000 | tf_op jit(solution)/shard_map/coupled/pallas_call | solution.py:24
  54.5 1.2 %collective-permute-done.6 = bf16[512,512]{1,0:T(8,128)(2,1)S(1)} collective-permute-done((bf16[512,512]{1,0:T(8,128)(2,1)}, bf16[512,512]{1,0:T(8,128)(2,1)S(1)}, u32[]{:S(2)}, u32[]{:S(2)}) %collective-permute-start.6) | collective-permute-done | bytes 524320 | tf_op jit(solution)/shard_map/ppermute | solution.py:364
  55.8 0.7 %collective-permute-done.11.refs_6_ = bf16[8,128,128]{2,1,0:T(8,128)(2,1)S(1)} collective-permute-done((bf16[8,128,128]{2,1,0:T(8,128)(2,1)S(1)}, bf16[8,128,128]{2,1,0:T(8,128)(2,1)S(1)}, u32[]{:S(2)}, u32[]{:S(2)}) %collective-permute-start.11) | collective-permute-done | bytes 262176 | tf_op jit(solution)/shard_map/ppermute | solution.py:361
  56.4 1.9 %collective-permute-done.12 = bf16[512,512]{1,0:T(8,128)(2,1)S(1)} collective-permute-done((bf16[512,512]{1,0:T(8,128)(2,1)S(1)}, bf16[512,512]{1,0:T(8,128)(2,1)S(1)}, u32[]{:S(2)}, u32[]{:S(2)}) %collective-permute-start.12) | collective-permute-done | bytes 524320 | tf_op jit(solution)/shard_map/ppermute | solution.py:367
  58.3 2.5 %exchange.1 = f32[8,128,128]{2,1,0:T(8,128)} custom-call(s32[8,2]{1,0:T(8,128)S(1)} %copy-done.7, s32[16]{0:T(128)S(1)} %copy-done.8, bf16[1,512,512]{2,1,0:T(8,128)(2,1)S(1)} %bitcast.16, bf16[1,512,512]{2,1,0:T(8,128)(2,1)S(1)} %bitcast.17, bf16[1024,512]{1,0:T(8,128)(2,1)S(1)} %get-tuple-element.42.left_ref.refs_4_.refs_2_, ...), custom_call_target="tpu_custom_call" | custom-call | tf_op jit(solution)/shard_map/exchange/pallas_call | solution.py:24
  (33 shorter events, 0.1 us)
Async XLA Ops:
  0.0 17.3 %collective-permute-start = (bf16[512,512]{1,0:T(8,128)(2,1)}, bf16[512,512]{1,0:T(8,128)(2,1)}, u32[]{:S(2)}, u32[]{:S(2)}) collective-permute-start(bf16[512,512]{1,0:T(8,128)(2,1)} %bitcast.12), channel_id=1, source_target_pairs={{0,2},{1,3},{2,4},{3,5},{4,6},{5,7},{6,0},{7,1},{8,10},{9,11},{10,... | collective-permute-start | bytes 1572872 | tf_op jit(solution)/shard_map/ppermute | solution.py:364
  6.8 18.3 %collective-permute-start.2 = (bf16[4,656,128]{2,1,0:T(8,128)(2,1)}, bf16[4,656,128]{2,1,0:T(8,128)(2,1)S(1)}, u32[]{:S(2)}, u32[]{:S(2)}) collective-permute-start(bf16[4,656,128]{2,1,0:T(8,128)(2,1)} %get-tuple-element.46.low_ref), channel_id=1, source_target_pairs={{0,8},{8,0},{16,24},{24,16},{1,9},{9,1},{17,25},{25,17},{2,10},{10... | collective-permute-start | bytes 2015240 | tf_op jit(solution)/shard_map/ppermute | solution.py:358
  8.4 18.2 %collective-permute-start.3 = (bf16[4,656,128]{2,1,0:T(8,128)(2,1)}, bf16[4,656,128]{2,1,0:T(8,128)(2,1)S(1)}, u32[]{:S(2)}, u32[]{:S(2)}) collective-permute-start(bf16[4,656,128]{2,1,0:T(8,128)(2,1)} %get-tuple-element.45.high_ref), channel_id=1, source_target_pairs={{0,16},{8,24},{16,0},{24,8},{1,17},{9,25},{17,1},{25,9},{2,18},{10... | collective-permute-start | bytes 2015240 | tf_op jit(solution)/shard_map/ppermute | solution.py:361
  9.9 33.7 %collective-permute-start.8 = (bf16[4,656,128]{2,1,0:T(8,128)(2,1)}, bf16[4,656,128]{2,1,0:T(8,128)(2,1)}, u32[]{:S(2)}, u32[]{:S(2)}) collective-permute-start(bf16[4,656,128]{2,1,0:T(8,128)(2,1)} %get-tuple-element.45.high_ref), channel_id=1, source_target_pairs={{0,8},{8,0},{16,24},{24,16},{1,9},{9,1},{17,25},{25,17},{2,10},{10... | collective-permute-start | bytes 2015240 | tf_op jit(solution)/shard_map/ppermute | solution.py:358
  10.4 33.1 %collective-permute-start.9 = (bf16[4,656,128]{2,1,0:T(8,128)(2,1)}, bf16[4,656,128]{2,1,0:T(8,128)(2,1)}, u32[]{:S(2)}, u32[]{:S(2)}) collective-permute-start(bf16[4,656,128]{2,1,0:T(8,128)(2,1)} %get-tuple-element.46.low_ref), channel_id=1, source_target_pairs={{0,16},{8,24},{16,0},{24,8},{1,17},{9,25},{17,1},{25,9},{2,18},{10... | collective-permute-start | bytes 2015240 | tf_op jit(solution)/shard_map/ppermute | solution.py:361
  17.3 1.1 %copy-start.9 = (bf16[4,656,128]{2,1,0:T(8,128)(2,1)S(1)}, bf16[4,656,128]{2,1,0:T(8,128)(2,1)}, u32[]{:S(2)}) copy-start(bf16[4,656,128]{2,1,0:T(8,128)(2,1)} %get-tuple-element.46.low_ref) | copy-start | bytes 2015236
  18.4 1.1 %copy-start.10 = (bf16[4,656,128]{2,1,0:T(8,128)(2,1)S(1)}, bf16[4,656,128]{2,1,0:T(8,128)(2,1)}, u32[]{:S(2)}) copy-start(bf16[4,656,128]{2,1,0:T(8,128)(2,1)} %get-tuple-element.45.high_ref) | copy-start | bytes 2015236
  19.5 0.7 %copy-start.11 = (f32[8,128]{1,0:T(8,128)S(1)}, f32[8,128]{1,0:T(8,128)}, u32[]{:S(2)}) copy-start(f32[8,128]{1,0:T(8,128)} %get-tuple-element.34.weight_ref) | copy-start | bytes 12292
  20.2 6.4 %copy-start.4 = (bf16[1,512,512]{2,1,0:T(8,128)(2,1)S(1)}, bf16[1,512,512]{2,1,0:T(8,128)(2,1)}, u32[]{:S(2)}) copy-start(bf16[1,512,512]{2,1,0:T(8,128)(2,1)} %refs_0_.1) | copy-start | bytes 1572868
  24.1 15.3 %collective-permute-start.1 = (bf16[512,512]{1,0:T(8,128)(2,1)}, bf16[512,512]{1,0:T(8,128)(2,1)}, u32[]{:S(2)}, u32[]{:S(2)}) collective-permute-start(bf16[512,512]{1,0:T(8,128)(2,1)} %collective-permute-done), channel_id=1, source_target_pairs={{0,2},{1,3},{2,4},{3,5},{4,6},{5,7},{6,0},{7,1},{8,10},{9,11},{10,... | collective-permute-start | bytes 1572872 | tf_op jit(solution)/shard_map/ppermute | solution.py:364
  25.1 6.0 %copy-start = (bf16[4,656,128]{2,1,0:T(8,128)(2,1)}, bf16[4,656,128]{2,1,0:T(8,128)(2,1)S(1)}, u32[]{:S(2)}) copy-start(bf16[4,656,128]{2,1,0:T(8,128)(2,1)S(1)} %collective-permute-done.2.one_ref.x_low.refs_0_) | copy-start | bytes 2015236
  26.6 4.5 %copy-start.2 = (bf16[4,656,128]{2,1,0:T(8,128)(2,1)}, bf16[4,656,128]{2,1,0:T(8,128)(2,1)S(1)}, u32[]{:S(2)}) copy-start(bf16[4,656,128]{2,1,0:T(8,128)(2,1)S(1)} %collective-permute-done.3.two_ref.y_high.refs_3_) | copy-start | bytes 2015236
  26.6 6.6 %collective-permute-start.4 = (bf16[512,512]{1,0:T(8,128)(2,1)S(1)}, bf16[512,512]{1,0:T(8,128)(2,1)S(1)}, u32[]{:S(2)}, u32[]{:S(2)}) collective-permute-start(bf16[512,512]{1,0:T(8,128)(2,1)S(1)} %bitcast.13), channel_id=1, source_target_pairs={{0,1},{1,0},{2,3},{3,2},{4,5},{5,4},{6,7},{7,6},{8,9},{9,8},{10,11... | collective-permute-start | bytes 1572872 | tf_op jit(solution)/shard_map/ppermute | solution.py:367
  26.6 6.6 %collective-permute-start.5 = (bf16[512,512]{1,0:T(8,128)(2,1)}, bf16[512,512]{1,0:T(8,128)(2,1)S(1)}, u32[]{:S(2)}, u32[]{:S(2)}) collective-permute-start(bf16[512,512]{1,0:T(8,128)(2,1)} %collective-permute-done), channel_id=1, source_target_pairs={{0,1},{1,0},{2,3},{3,2},{4,5},{5,4},{6,7},{7,6},{8,9},{9,8},{10,11... | collective-permute-start | bytes 1572872 | tf_op jit(solution)/shard_map/ppermute | solution.py:367
  27.1 6.1 %copy-start.7 = (s32[8,2]{1,0:T(8,128)S(1)}, s32[8,2]{1,0:T(8,128)}, u32[]{:S(2)}) copy-start(s32[8,2]{1,0:T(8,128)} %get-tuple-element.28.uses_ref) | copy-start | bytes 196
  31.1 4.1 %copy-start.13 = (f32[8,128,128]{2,1,0:T(8,128)}, f32[8,128,128]{2,1,0:T(8,128)S(1)}, u32[]{:S(2)}) copy-start(f32[8,128,128]{2,1,0:T(8,128)S(1)} %coupled.2.acc_ref) | copy-start | bytes 1572868
  33.2 2.0 %copy-start.5 = (f32[4,128,128]{2,1,0:T(8,128)}, f32[4,128,128]{2,1,0:T(8,128)S(1)}, u32[]{:S(2)}) copy-start(f32[4,128,128]{2,1,0:T(8,128)S(1)} %get-tuple-element.41.low2) | copy-start | bytes 786436
  39.4 2.3 %collective-permute-start.7 = (bf16[512,512]{1,0:T(8,128)(2,1)}, bf16[512,512]{1,0:T(8,128)(2,1)}, u32[]{:S(2)}, u32[]{:S(2)}) collective-permute-start(bf16[512,512]{1,0:T(8,128)(2,1)} %collective-permute-done.1), channel_id=1, source_target_pairs={{0,1},{1,0},{2,3},{3,2},{4,5},{5,4},{6,7},{7,6},{8,9},{9,8},{10,11... | collective-permute-start | bytes 1572872 | tf_op jit(solution)/shard_map/ppermute | solution.py:367
  39.4 16.3 %collective-permute-start.6 = (bf16[512,512]{1,0:T(8,128)(2,1)}, bf16[512,512]{1,0:T(8,128)(2,1)S(1)}, u32[]{:S(2)}, u32[]{:S(2)}) collective-permute-start(bf16[512,512]{1,0:T(8,128)(2,1)} %collective-permute-done.1), channel_id=1, source_target_pairs={{0,2},{1,3},{2,4},{3,5},{4,6},{5,7},{6,0},{7,1},{8,10},{9,11},{10,... | collective-permute-start | bytes 1572872 | tf_op jit(solution)/shard_map/ppermute | solution.py:364
  41.7 1.9 %copy-start.1 = (bf16[4,656,128]{2,1,0:T(8,128)(2,1)S(1)}, bf16[4,656,128]{2,1,0:T(8,128)(2,1)}, u32[]{:S(2)}) copy-start(bf16[4,656,128]{2,1,0:T(8,128)(2,1)} %copy-done) | copy-start | bytes 2015236
  41.7 1.9 %copy-start.3 = (bf16[4,656,128]{2,1,0:T(8,128)(2,1)S(1)}, bf16[4,656,128]{2,1,0:T(8,128)(2,1)}, u32[]{:S(2)}) copy-start(bf16[4,656,128]{2,1,0:T(8,128)(2,1)} %copy-done.2) | copy-start | bytes 2015236
  41.7 1.9 %copy-start.6 = (f32[4,128,128]{2,1,0:T(8,128)S(1)}, f32[4,128,128]{2,1,0:T(8,128)}, u32[]{:S(2)}) copy-start(f32[4,128,128]{2,1,0:T(8,128)} %copy-done.5) | copy-start | bytes 786436
  43.5 6.4 %copy-start.12 = (f32[8,128]{1,0:T(8,128)S(1)}, f32[8,128]{1,0:T(8,128)}, u32[]{:S(2)}) copy-start(f32[8,128]{1,0:T(8,128)} %get-tuple-element.34.weight_ref) | copy-start | bytes 12292
  43.5 6.4 %copy-start.14 = (f32[8,128,128]{2,1,0:T(8,128)S(1)}, f32[8,128,128]{2,1,0:T(8,128)}, u32[]{:S(2)}) copy-start(f32[8,128,128]{2,1,0:T(8,128)} %copy-done.13) | copy-start | bytes 1572868
  47.0 9.4 %collective-permute-start.10 = (bf16[8,128,128]{2,1,0:T(8,128)(2,1)S(1)}, bf16[8,128,128]{2,1,0:T(8,128)(2,1)S(1)}, u32[]{:S(2)}, u32[]{:S(2)}) collective-permute-start(bf16[8,128,128]{2,1,0:T(8,128)(2,1)S(1)} %get-tuple-element.47), channel_id=1, source_target_pairs={{0,8},{8,0},{16,24},{24,16},{1,9},{9,1},{17,25},{25,17},{2,10},{10... | collective-permute-start | bytes 786440 | tf_op jit(solution)/shard_map/ppermute | solution.py:358
  48.3 10.0 %copy-start.8 = (s32[16]{0:T(128)S(1)}, s32[16]{0:T(128)}, u32[]{:S(2)}) copy-start(s32[16]{0:T(128)} %get-tuple-element.29.turn_ref) | copy-start | bytes 196
  48.3 8.1 %collective-permute-start.11 = (bf16[8,128,128]{2,1,0:T(8,128)(2,1)S(1)}, bf16[8,128,128]{2,1,0:T(8,128)(2,1)S(1)}, u32[]{:S(2)}, u32[]{:S(2)}) collective-permute-start(bf16[8,128,128]{2,1,0:T(8,128)(2,1)S(1)} %get-tuple-element.49), channel_id=1, source_target_pairs={{0,16},{8,24},{16,0},{24,8},{1,17},{9,25},{17,1},{25,9},{2,18},{10... | collective-permute-start | bytes 786440 | tf_op jit(solution)/shard_map/ppermute | solution.py:361
  56.4 1.9 %collective-permute-start.12 = (bf16[512,512]{1,0:T(8,128)(2,1)S(1)}, bf16[512,512]{1,0:T(8,128)(2,1)S(1)}, u32[]{:S(2)}, u32[]{:S(2)}) collective-permute-start(bf16[512,512]{1,0:T(8,128)(2,1)S(1)} %collective-permute-done.6), channel_id=1, source_target_pairs={{0,1},{1,0},{2,3},{3,2},{4,5},{5,4},{6,7},{7,6},{8,9},{9,8},{10,11... | collective-permute-start | bytes 1572872 | tf_op jit(solution)/shard_map/ppermute | solution.py:367

commit v2 on v1

--- a/solution.py
+++ b/solution.py
@@ -12,7 +12,7 @@
 PACK_LIMIT = 56 * 1024 * 1024
 RING_CHIPS = 4
 DECLARED = 20_000_000_000
-OWN_COST, FIRST_COST, SECOND_COST, LAST_COST = DECLARED, 0, 0, DECLARED
+OWN_COST, FIRST_COST, SECOND_COST, LAST_COST = 0, 0, 0, DECLARED
 SMEM_SPEC = pl.BlockSpec(memory_space=pltpu.SMEM)
 VMEM_SPEC = pl.BlockSpec(memory_space=pltpu.VMEM)
 HBM_SPEC = pl.BlockSpec(memory_space=pltpu.HBM)
@@ -132,35 +132,27 @@
     low, high = range(block, block + half), range(block + half, block + 2 * half)
     one, two = both_sums(x_low, y_high, turned_ref, low, high, products, orbs)
     for k in range(half):
-        out_one[k] = one(k)
-        out_two[k] = two(k)
-
-
-def second_across_kernel(orbs, upper_ref, low1, low2, *refs):
-    x_low, x_high, y_low, y_high, back_x, back_y, turned_ref, *products = refs
-    half, pno = low1.shape[0], low1.shape[1]
+        out_one[k] = one(k).astype(jnp.bfloat16)
+        out_two[k] = two(k).astype(jnp.bfloat16)
+
+
+def second_across_kernel(orbs, upper_ref, x_low, x_high, y_low, y_high, out_one, out_two, turned_ref, *products):
+    half = out_one.shape[0]
     block = 3 * 2 * half
-    none = jnp.zeros((pno, pno), jnp.bfloat16)
+
+    def between(one_ref, two_ref, lanes):
+        one, two = both_sums(one_ref, two_ref, turned_ref, lanes, lanes, products, orbs)
+        for k in range(half):
+            out_one[k] = one(k).astype(jnp.bfloat16)
+            out_two[k] = two(k).astype(jnp.bfloat16)
 
     @pl.when(upper_ref[0] == 0)
     def _():
-        low = range(block, block + half)
-        one, two = both_sums(x_low, y_low, turned_ref, low, low, products, orbs)
-        for k in range(half):
-            back_x[k] = (low1[k] + one(k)).astype(jnp.bfloat16)
-            back_x[half + k] = none
-            back_y[k] = two(k).astype(jnp.bfloat16)
-            back_y[half + k] = low2[k].astype(jnp.bfloat16)
+        between(x_low, y_low, range(block, block + half))
 
     @pl.when(upper_ref[0] == 1)
     def _():
-        high = range(block + half, block + 2 * half)
-        one, two = both_sums(x_high, y_high, turned_ref, high, high, products, orbs)
-        for k in range(half):
-            back_x[k] = low1[k].astype(jnp.bfloat16)
-            back_x[half + k] = one(k).astype(jnp.bfloat16)
-            back_y[k] = none
-            back_y[half + k] = (low2[k] + two(k)).astype(jnp.bfloat16)
+        between(x_high, y_high, range(block + half, block + 2 * half))
 
 
 def own_coupled(weights, own, orbs, flops):
@@ -179,8 +171,10 @@
     return call_kernel(body, shape, scratch, "coupled", (weights,), (own_t, acc, *received), flops)
 
 
-def across(body, name, scalars, vmem_args, half, shapes, orbs, flops):
-    wide = half * shapes[0].shape[2]
+def across(body, name, scalars, vmem_args, orbs, flops):
+    half, _, pno = vmem_args[0].shape
+    wide = half * pno
+    shapes = (jax.ShapeDtypeStruct((half, pno, pno), jnp.bfloat16),) * 2
     scratch = [pltpu.VMEM((2 * wide, orbs), jnp.bfloat16), *[pltpu.VMEM((wide, wide), jnp.bfloat16)] * 4]
     return call_kernel(functools.partial(body, orbs), shapes, scratch, name, scalars, vmem_args, flops)
 
@@ -227,8 +221,9 @@
     halves_kernel(base, uses_ref, *slab_refs, own_ref, half_ref)
 
 
-def exchange_kernel(scale, base, uses_ref, turn_ref, *refs):
-    *slab_refs, own_ref, early_ref, acc_ref, back1_ref, back2_ref, out_ref, late_ref = refs
+def exchange_kernel(scale, base, uses_ref, turn_ref, upper_ref, *refs):
+    *slab_refs, own_ref, early_ref, acc_ref, low_ref, high_ref, row_ref, column_ref, out_ref, late_ref = refs
+    half_count = low_ref.shape[0]
 
     def store(k, use, side, half):
         late_ref[2 * (k - base) + use] = half
@@ -241,28 +236,30 @@
     half_transforms(uses_ref, slab_refs, own_ref, store, base, out_ref.shape[1])
     for p in range(out_ref.shape[0]):
         product = lax.dot_general(half(p, 0), half(p, 1), (((0,), (0,)), ((), ())), preferred_element_type=jnp.float32)
-        back = back1_ref[p].astype(jnp.float32) + back2_ref[p].astype(jnp.float32)
-        out_ref[p] = acc_ref[p] + back + product * scale
-
-
-def half_products(uses, base, slabs, own_t, pno, done=None):
+        k, upper = p % half_count, p // half_count
+        first = (low_ref, high_ref)[upper][k].astype(jnp.float32)
+        second = jnp.where(upper_ref[0] == upper, row_ref[k], column_ref[k]).astype(jnp.float32)
+        out_ref[p] = acc_ref[p] + (first + second) + product * scale
+
+
+def half_products(uses, base, slabs, own_t, pno, done, flops):
     sides = own_t.shape[0] // pno * 2
     shape = jax.ShapeDtypeStruct((sides + 1, slabs[0].shape[1], pno), jnp.bfloat16)
     if done is None:
-        return call_kernel(functools.partial(halves_kernel, base), shape, [], "halves", (uses,), (*slabs, own_t), 0)
+        return call_kernel(functools.partial(halves_kernel, base), shape, [], "halves", (uses,), (*slabs, own_t), flops)
     args = (*slabs, own_t, done)
     return call_kernel(
-        functools.partial(more_halves_kernel, base), shape, [], "more_halves", (uses,), args, 0, aliases={len(args): 0}
-    )
-
-
-def add_exchange(uses, turn, base, slabs, own_t, early, sums):
+        functools.partial(more_halves_kernel, base), shape, [], "more_halves", (uses,), args, flops, aliases={len(args): 0}
+    )
+
+
+def add_exchange(uses, turn, upper, base, slabs, own_t, early, sums):
     return call_kernel(
         functools.partial(exchange_kernel, 1.0 / math.sqrt(slabs[0].shape[1]), base),
         jax.ShapeDtypeStruct(sums[0].shape, jnp.float32),
         [pltpu.VMEM((2 * sum(slab.shape[0] for slab in slabs),) + early.shape[1:], jnp.bfloat16)],
         "exchange",
-        (uses, turn),
+        (uses, turn, upper),
         (*slabs, own_t, early, *sums),
         0,
     )
@@ -314,7 +311,8 @@
         k = position
         if chips <= RING_CHIPS:
             steps = lax.rem(lax.div(me, 2) - lax.div(position, 2) + chips, chips)
-            k = 2 * steps + (lax.rem(position, 2) ^ lax.rem(me, 2))
+            swapped = lax.rem(position, 2) ^ lax.rem(me, 2)
+            k = jnp.where(steps < 2, steps + 2 * swapped, steps + 2 + 2 * swapped)
         turn_ref[f] = k
         uses_ref[k, 1] = uses_ref[k, 0]
         uses_ref[k, 0] = f
@@ -360,15 +358,16 @@
     def along_y(value):
         return lax.ppermute(value, "grp", [(g, g ^ 2) for g in range(n_grp)])
 
-    def next_chip(value):
-        return lax.ppermute(value, "dev", [(d, (d + 2) % n_dev) for d in range(n_dev)])
+    def along_chips(value, step):
+        return lax.ppermute(value, "dev", [(d, (d + 2 * step) % n_dev) for d in range(n_dev)])
 
     def other_core(value):
         return lax.ppermute(value, "dev", [(d, d ^ 1) for d in range(n_dev)])
 
-    own_lo, own_hi, weights, uses, turns = pack(
+    *own, weights, uses, turns = pack(
         group.astype(jnp.int32).reshape(1), me.astype(jnp.int32).reshape(1), chips, coupled, coupled_len, slab_owner, pair_orbs, domain_bases, amplitudes
     )
+    own_lo, own_hi = own
     upper = (group // 2).astype(jnp.int32).reshape(1)
 
     x_lo, y_hi = along_x(own_lo), along_y(own_hi)
@@ -377,46 +376,37 @@
     slab = integral_slabs[0]
     around = chips <= RING_CHIPS
     ahead = 6 if around else n_dev // 2
+    acc, own_t = own_coupled(weights, own, orbs, OWN_COST)
     if around:
-        round1 = next_chip(slab)
-        round2 = next_chip(round1)
-        swap0, swap1 = other_core(after(slab, x_lo, y_hi)), other_core(after(round1, x_lo, y_hi))
-    acc, own_t = own_coupled(weights, (after(own_lo, round1) if around else own_lo, own_hi), orbs, OWN_COST)
+        below, above = along_chips(slab, 1), along_chips(slab, -1)
+        halves = half_products(uses, 0, [slab[None], below[None]], own_t, pno, None, DECLARED)
+        beyond = along_chips(below, 1)
+        acc = after(acc, halves)
+    else:
+        gathered = lax.all_gather(slab, "dev", axis=0, tiled=False)
+        halves = half_products(uses, 0, [gathered[:ahead]], own_t, pno, None, 0)
+        rest = [gathered[ahead:]]
 
     lanes = [*range(pairs, pairs + half), *range(2 * pairs + half, 3 * pairs)]
     acc = add_coupled(lanes, weights, own_t, acc, (x_lo, y_hi), DECLARED)
-    part = jax.ShapeDtypeStruct((half, pno, pno), jnp.float32)
-    first = across(
-        first_across_kernel, "first_across", (), (after(x_lo, acc), after(y_hi, acc)), half, (part, part), orbs, FIRST_COST
-    )
+    first = across(first_across_kernel, "first_across", (), (after(x_lo, acc), after(y_hi, acc)), orbs, FIRST_COST)
+    back_low, back_high = along_x(first[0]), along_y(first[1])
+    gate = first[0]
     if around:
-        slabs = [slab[None], swap0[None], round1[None], swap1[None]]
-        halves = half_products(uses, 0, slabs, after(own_t, *first), pno)
-        round2 = after(round2, halves)
-        round3, swap2 = next_chip(round2), other_core(round2)
-        halves = half_products(uses, 4, [round2[None], swap2[None]], own_t, pno, halves)
-    else:
-        gathered = lax.all_gather(slab, "dev", axis=0, tiled=False)
-        halves = half_products(uses, 0, [gathered[:ahead]], own_t, pno)
-        rest = [gathered[ahead:]]
-    whole = jax.ShapeDtypeStruct((pairs, pno, pno), jnp.bfloat16)
-    back_x, back_y = across(
-        second_across_kernel,
-        "second_across",
-        (upper,),
-        (after(first[0], halves), first[1], x_lo, x_hi, y_lo, y_hi),
-        half,
-        (whole, whole),
-        orbs,
-        SECOND_COST,
-    )
-    back = (along_x(back_x), along_y(back_y))
+        swaps = [other_core(after(value, x_lo, y_hi)) for value in (slab, below)]
+        more = [value[None] for value in (*swaps, beyond, above)]
+        halves = half_products(uses, 2, more, after(own_t, gate), pno, halves, 0)
+        beyond, above = after(beyond, halves), after(above, halves)
+        rest = [other_core(beyond)[None], other_core(above)[None]]
+        gate = halves
+    second = across(
+        second_across_kernel, "second_across", (upper,), (after(x_lo, gate), x_hi, y_lo, y_hi), orbs, SECOND_COST
+    )
+    back_row, back_column = along_x(second[0]), along_y(second[1])
     lanes = [*range(pairs + half, 2 * pairs), *range(2 * pairs, 2 * pairs + half)]
-    acc = add_coupled(lanes, weights, own_t, after(acc, back_x), (x_hi, y_lo), LAST_COST)
-    if around:
-        round3 = after(round3, acc, *back)
-        rest = [round3[None], other_core(round3)[None]]
-    return add_exchange(uses, turns, ahead, rest, own_t, halves, (acc, *back))
+    acc = add_coupled(lanes, weights, own_t, after(acc, second[0]), (x_hi, y_lo), LAST_COST)
+    sums = (acc, back_low, back_high, back_row, back_column)
+    return add_exchange(uses, turns, upper, ahead, rest, own_t, halves, sums)
 
 
 def solution(mesh):

time: 61.3 us -> 61.1 us (level)
  waiting for transfers between devices: 19 us -> 11.4 us
  starting transfers between devices: 10.6 us -> 15 us
  Pallas kernels: 28.2 us -> 29.7 us
  local copies, waits for them, and re-layouts: 2.92 us -> 4.37 us
    ppermute x3, waiting for transfers between devices: 11.7 us -> 4.88 us  [along_chips(): lax.ppermute(value, 'dev', [(d, (d + 2 * step) % n_dev) for d in range(n_...]
    ppermute x4, waiting for transfers between devices: 4.16 us -> 0.01 us  [other_core(): return lax.ppermute(value, 'dev', [(d, d ^ 1) for d in range(n_dev)])]
    ppermute x3 -> x4, waiting for transfers between devices: 0.9 us -> 4.75 us  [along_x(): return lax.ppermute(value, 'grp', [(g, g ^ 1) for g in range(n_grp)])]
    ppermute x3, starting transfers between devices: 3.09 us -> 5.07 us  [along_chips(): lax.ppermute(value, 'dev', [(d, (d + 2 * step) % n_dev) for d in range(n_...]
    unnamed x30 -> x28, local copies, waits for them, and re-layouts: 2.92 us -> 4.37 us
    pallas_call x8, Pallas kernels: 24.4 us -> 25.9 us  [call_kernel(): pl.pallas_call(body, out_shape=out_shape, in_specs=[SMEM_SPEC] * len(smem...]
    ppermute x3 -> x4, starting transfers between devices: 3.4 us -> 4.4 us  [along_x(): return lax.ppermute(value, 'grp', [(g, g ^ 1) for g in range(n_grp)])]
    ppermute x3 -> x4, starting transfers between devices: 3.55 us -> 4.52 us  [along_y(): return lax.ppermute(value, 'grp', [(g, g ^ 2) for g in range(n_grp)])]
  transfers between devices with their start and end apart: 13 -> 15, of which waited for: 8 -> 3; matrix products, arithmetic and copies ran while one was open for 0% -> 0% of each run, Pallas kernels for 42% -> 45%
where the time goes in v2:
time: 61.1 us; the launch traced here: 60.6 us
  Pallas kernels  29.7 us (49%)
  starting transfers between devices  15 us (25%)
  waiting for transfers between devices  11.4 us (19%)
  local copies, waits for them, and re-layouts  4.37 us (7%)
    pallas_call x8, Pallas kernels, call_kernel(): pl.pallas_call(body, out_shape=out_shape, in_specs=[SMEM_SPEC] * len(smem...  25.9 us
    ppermute x3, starting transfers between devices, along_chips(): lax.ppermute(value, 'dev', [(d, (d + 2 * step) % n_dev) for d in range(n_...  5.07 us
    ppermute x3, waiting for transfers between devices, along_chips(): lax.ppermute(value, 'dev', [(d, (d + 2 * step) % n_dev) for d in range(n_...  4.88 us
    ppermute x4, waiting for transfers between devices, along_x(): return lax.ppermute(value, 'grp', [(g, g ^ 1) for g in range(n_grp)])  4.75 us
    ppermute x4, starting transfers between devices, along_y(): return lax.ppermute(value, 'grp', [(g, g ^ 2) for g in range(n_grp)])  4.52 us
    ppermute x4, starting transfers between devices, along_x(): return lax.ppermute(value, 'grp', [(g, g ^ 1) for g in range(n_grp)])  4.4 us
    unnamed x28, local copies, waits for them, and re-layouts  4.37 us
    pallas_call x1, Pallas kernels, pack(): pl.pallas_call(functools.partial(pack_kernel, orbs / pno, chips), out_sha...  3.77 us
  transfers between devices with their start and end apart: 15, of which 3 were waited for; matrix products, arithmetic and copies ran while one was open for 0% of the time, Pallas kernels for 45%

profile of v2, /device:TPU:0, one launch (start us, length us, event | category | flops | bytes accessed | tf_op | source)
XLA Modules:
  0.0 60.6 jit_solution(12671105740089817833)
XLA Ops:
  0.0 3.0 %collective-permute-start = (bf16[512,512]{1,0:T(8,128)(2,1)}, bf16[512,512]{1,0:T(8,128)(2,1)}, u32[]{:S(2)}, u32[]{:S(2)}) collective-permute-start(bf16[512,512]{1,0:T(8,128)(2,1)} %bitcast.4), channel_id=1, source_target_pairs={{0,2},{1,3},{2,4},{3,5},{4,6},{5,7},{6,0},{7,1},{8,10},{9,11},{10,... | collective-permute-start | bytes 1572872 | tf_op jit(solution)/shard_map/ppermute | solution.py:362
  3.0 2.0 %collective-permute-start.6 = (bf16[512,512]{1,0:T(8,128)(2,1)}, bf16[512,512]{1,0:T(8,128)(2,1)}, u32[]{:S(2)}, u32[]{:S(2)}) collective-permute-start(bf16[512,512]{1,0:T(8,128)(2,1)} %bitcast.4), channel_id=1, source_target_pairs={{0,6},{1,7},{2,0},{3,1},{4,2},{5,3},{6,4},{7,5},{8,14},{9,15},{10,... | collective-permute-start | bytes 1572872 | tf_op jit(solution)/shard_map/ppermute | solution.py:362
  5.1 3.8 %pack.1 = (bf16[4,656,128]{2,1,0:T(8,128)(2,1)}, bf16[4,656,128]{2,1,0:T(8,128)(2,1)}, f32[8,128]{1,0:T(8,128)}, s32[8,2]{1,0:T(8,128)}, s32[16]{0:T(128)}) custom-call(s32[1]{0:T(128)} %bitcast.group_ref, s32[1]{0:T(128)} %bitcast.1.me_ref, s32[8,32]{1,0:T(8,128)} %coupled_ref.1, s32[8]{0:T(128)} %length_ref.1, s32[8]{0:T(128)} %owner_ref.1, ...), custom_call_target="tpu_custom_call" | custom-call | tf_op jit(solution)/shard_map/pack/pallas_call | solution.py:326
  8.8 1.8 %collective-permute-start.2 = (bf16[4,656,128]{2,1,0:T(8,128)(2,1)}, bf16[4,656,128]{2,1,0:T(8,128)(2,1)S(1)}, u32[]{:S(2)}, u32[]{:S(2)}) collective-permute-start(bf16[4,656,128]{2,1,0:T(8,128)(2,1)} %get-tuple-element.46.low_ref), channel_id=1, source_target_pairs={{0,8},{8,0},{16,24},{24,16},{1,9},{9,1},{17,25},{25,17},{2,10},{10... | collective-permute-start | bytes 2015240 | tf_op jit(solution)/shard_map/ppermute | solution.py:356
  10.6 1.5 %collective-permute-start.3 = (bf16[4,656,128]{2,1,0:T(8,128)(2,1)}, bf16[4,656,128]{2,1,0:T(8,128)(2,1)S(1)}, u32[]{:S(2)}, u32[]{:S(2)}) collective-permute-start(bf16[4,656,128]{2,1,0:T(8,128)(2,1)} %get-tuple-element.45.high_ref), channel_id=1, source_target_pairs={{0,16},{8,24},{16,0},{24,8},{1,17},{9,25},{17,1},{25,9},{2,18},{10... | collective-permute-start | bytes 2015240 | tf_op jit(solution)/shard_map/ppermute | solution.py:359
  12.1 0.5 collective-permute-start.9
  12.7 1.1 %copy-done.4 = bf16[4,656,128]{2,1,0:T(8,128)(2,1)S(1)} copy-done((bf16[4,656,128]{2,1,0:T(8,128)(2,1)S(1)}, bf16[4,656,128]{2,1,0:T(8,128)(2,1)}, u32[]{:S(2)}) %copy-start.4) | copy-done | bytes 671768
  13.8 0.7 %copy-done.9 = f32[8,128]{1,0:T(8,128)S(1)} copy-done((f32[8,128]{1,0:T(8,128)S(1)}, f32[8,128]{1,0:T(8,128)}, u32[]{:S(2)}) %copy-start.9) | copy-done | bytes 4120
  14.5 4.5 %own_coupled.1 = (f32[8,128,128]{2,1,0:T(8,128)S(1)}, bf16[1024,512]{1,0:T(8,128)(2,1)S(1)}) custom-call(f32[8,128]{1,0:T(8,128)S(1)} %copy-done.9, bf16[4,656,128]{2,1,0:T(8,128)(2,1)} %get-tuple-element.46.low_ref, bf16[4,656,128]{2,1,0:T(8,128)(2,1)S(1)} %copy-done.4), custom_call_target="tpu_custom_call" | custom-call | tf_op jit(solution)/shard_map/own_coupled/pallas_call | solution.py:24
  19.0 1.0 %collective-permute-start.10 = (bf16[4,656,128]{2,1,0:T(8,128)(2,1)}, bf16[4,656,128]{2,1,0:T(8,128)(2,1)}, u32[]{:S(2)}, u32[]{:S(2)}) collective-permute-start(bf16[4,656,128]{2,1,0:T(8,128)(2,1)} %get-tuple-element.46.low_ref), channel_id=1, source_target_pairs={{0,16},{8,24},{16,0},{24,8},{1,17},{9,25},{17,1},{25,9},{2,18},{10... | collective-permute-start | bytes 2015240 | tf_op jit(solution)/shard_map/ppermute | solution.py:359
  19.9 0.7 %copy-done.7 = s32[8,2]{1,0:T(8,128)S(1)} copy-done((s32[8,2]{1,0:T(8,128)S(1)}, s32[8,2]{1,0:T(8,128)}, u32[]{:S(2)}) %copy-start.7) | copy-done | bytes 88
  20.6 1.7 %halves.1.refs_5_ = bf16[17,512,128]{2,1,0:T(8,128)(2,1)S(1)} custom-call(s32[8,2]{1,0:T(8,128)S(1)} %copy-done.7, bf16[1,512,512]{2,1,0:T(8,128)(2,1)} %refs_0_.1, bf16[1,512,512]{2,1,0:T(8,128)(2,1)} %bitcast.9.refs_1_, bf16[1024,512]{1,0:T(8,128)(2,1)S(1)} %get-tuple-element.41.refs_2_.left_ref.refs_4_), custom_call_target="tpu_custom_call" | custom-call | flops 20000000000 | tf_op jit(solution)/shard_map/halves/pallas_call | solution.py:24
  22.4 4.7 %collective-permute-done.2.one_ref.x_low = bf16[4,656,128]{2,1,0:T(8,128)(2,1)S(1)} collective-permute-done((bf16[4,656,128]{2,1,0:T(8,128)(2,1)}, bf16[4,656,128]{2,1,0:T(8,128)(2,1)S(1)}, u32[]{:S(2)}, u32[]{:S(2)}) %collective-permute-start.2) | collective-permute-done | bytes 671776 | tf_op jit(solution)/shard_map/ppermute | solution.py:356
  27.1 0.0 collective-permute-start.1
  27.1 1.7 %collective-permute-done.3.two_ref.y_high = bf16[4,656,128]{2,1,0:T(8,128)(2,1)S(1)} collective-permute-done((bf16[4,656,128]{2,1,0:T(8,128)(2,1)}, bf16[4,656,128]{2,1,0:T(8,128)(2,1)S(1)}, u32[]{:S(2)}, u32[]{:S(2)}) %collective-permute-start.3) | collective-permute-done | bytes 671776 | tf_op jit(solution)/shard_map/ppermute | solution.py:359
  28.9 0.5 collective-permute-start.5
  29.4 4.0 %coupled.2.acc_ref = f32[8,128,128]{2,1,0:T(8,128)S(1)} custom-call(f32[8,128]{1,0:T(8,128)S(1)} %copy-done.10, bf16[1024,512]{1,0:T(8,128)(2,1)S(1)} %get-tuple-element.41.refs_2_.left_ref.refs_4_, f32[8,128,128]{2,1,0:T(8,128)S(1)} %get-tuple-element.37.acc_ref, bf16[4,656,128]{2,1,0:T(8,128)(2,1)S(1)} %collective-permute-done.2.one_ref.x_low, ...), custom_call_target="tpu_custom_call" | custom-call | flops 20000000000 | tf_op jit(solution)/shard_map/coupled/pallas_call | solution.py:24
  33.4 2.8 %first_across.1 = (bf16[4,128,128]{2,1,0:T(8,128)(2,1)S(1)}, bf16[4,128,128]{2,1,0:T(8,128)(2,1)}) custom-call(bf16[4,656,128]{2,1,0:T(8,128)(2,1)S(1)} %collective-permute-done.2.one_ref.x_low, bf16[4,656,128]{2,1,0:T(8,128)(2,1)S(1)} %collective-permute-done.3.two_ref.y_high), custom_call_target="tpu_custom_call" | custom-call | tf_op jit(solution)/shard_map/first_across/pallas_call | solution.py:24
  36.1 4.9 %collective-permute-done.1 = bf16[512,512]{1,0:T(8,128)(2,1)S(1)} collective-permute-done((bf16[512,512]{1,0:T(8,128)(2,1)}, bf16[512,512]{1,0:T(8,128)(2,1)S(1)}, u32[]{:S(2)}, u32[]{:S(2)}) %collective-permute-start.1) | collective-permute-done | bytes 524320 | tf_op jit(solution)/shard_map/ppermute | solution.py:362
  41.0 0.8 %copy-done.5 = bf16[512,512]{1,0:T(8,128)(2,1)} copy-done((bf16[512,512]{1,0:T(8,128)(2,1)}, bf16[512,512]{1,0:T(8,128)(2,1)S(1)}, u32[]{:S(2)}) %copy-start.5) | copy-done | bytes 524312
  41.8 0.7 %collective-permute-start.12 = (bf16[4,128,128]{2,1,0:T(8,128)(2,1)}, bf16[4,128,128]{2,1,0:T(8,128)(2,1)S(1)}, u32[]{:S(2)}, u32[]{:S(2)}) collective-permute-start(bf16[4,128,128]{2,1,0:T(8,128)(2,1)} %get-tuple-element.49), channel_id=1, source_target_pairs={{0,16},{8,24},{16,0},{24,8},{1,17},{9,25},{17,1},{25,9},{2,18},{10... | collective-permute-start | bytes 393224 | tf_op jit(solution)/shard_map/ppermute | solution.py:359
  42.5 1.3 %collective-permute-start.11 = (bf16[4,128,128]{2,1,0:T(8,128)(2,1)S(1)}, bf16[4,128,128]{2,1,0:T(8,128)(2,1)S(1)}, u32[]{:S(2)}, u32[]{:S(2)}) collective-permute-start(bf16[4,128,128]{2,1,0:T(8,128)(2,1)S(1)} %get-tuple-element.40), channel_id=1, source_target_pairs={{0,8},{8,0},{16,24},{24,16},{1,9},{9,1},{17,25},{25,17},{2,10},{10... | collective-permute-start | bytes 393224 | tf_op jit(solution)/shard_map/ppermute | solution.py:356
  43.8 0.0 collective-permute-done.5
  43.8 1.0 %copy-done.6 = bf16[512,512]{1,0:T(8,128)(2,1)S(1)} copy-done((bf16[512,512]{1,0:T(8,128)(2,1)S(1)}, bf16[512,512]{1,0:T(8,128)(2,1)}, u32[]{:S(2)}) %copy-start.6) | copy-done | bytes 524312
  44.9 2.3 %more_halves.1.refs_3_ = bf16[17,512,128]{2,1,0:T(8,128)(2,1)S(1)} custom-call(s32[8,2]{1,0:T(8,128)S(1)} %copy-done.8, bf16[1,512,512]{2,1,0:T(8,128)(2,1)} %bitcast.5.refs_0_, bf16[1,512,512]{2,1,0:T(8,128)(2,1)} %bitcast.6.refs_1_, bf16[1,512,512]{2,1,0:T(8,128)(2,1)S(1)} %bitcast.12, ...), custom_call_target="tpu_custom_call", output_to_operand_aliasing={{}: (6, {})} | custom-call | tf_op jit(solution)/shard_map/more_halves/pallas_call | solution.py:24
  47.2 0.0 collective-permute-done.9.x_high.one_ref
  47.2 3.5 %second_across.1 = (bf16[4,128,128]{2,1,0:T(8,128)(2,1)S(1)}, bf16[4,128,128]{2,1,0:T(8,128)(2,1)S(1)}) custom-call(s32[1]{0:T(128)} %bitcast.3.upper_ref, bf16[4,656,128]{2,1,0:T(8,128)(2,1)S(1)} %copy-done.1, bf16[4,656,128]{2,1,0:T(8,128)(2,1)} %collective-permute-done.9.x_high.one_ref, bf16[4,656,128]{2,1,0:T(8,128)(2,1)} %collective-permute-done.10.y_low.two_ref, ...), custom_call_target="tpu_custom_call" | custom-call | tf_op jit(solution)/shard_map/second_across/pallas_call | solution.py:24
  50.7 0.8 %collective-permute-start.13 = (bf16[4,128,128]{2,1,0:T(8,128)(2,1)S(1)}, bf16[4,128,128]{2,1,0:T(8,128)(2,1)S(1)}, u32[]{:S(2)}, u32[]{:S(2)}) collective-permute-start(bf16[4,128,128]{2,1,0:T(8,128)(2,1)S(1)} %get-tuple-element.47), channel_id=1, source_target_pairs={{0,8},{8,0},{16,24},{24,16},{1,9},{9,1},{17,25},{25,17},{2,10},{10... | collective-permute-start | bytes 393224 | tf_op jit(solution)/shard_map/ppermute | solution.py:356
  51.5 1.3 %collective-permute-start.14 = (bf16[4,128,128]{2,1,0:T(8,128)(2,1)S(1)}, bf16[4,128,128]{2,1,0:T(8,128)(2,1)S(1)}, u32[]{:S(2)}, u32[]{:S(2)}) collective-permute-start(bf16[4,128,128]{2,1,0:T(8,128)(2,1)S(1)} %get-tuple-element.50), channel_id=1, source_target_pairs={{0,16},{8,24},{16,0},{24,8},{1,17},{9,25},{17,1},{25,9},{2,18},{10... | collective-permute-start | bytes 393224 | tf_op jit(solution)/shard_map/ppermute | solution.py:359
  52.8 0.5 collective-permute-start.8
  53.3 4.7 %coupled.3.refs_4_ = f32[8,128,128]{2,1,0:T(8,128)S(1)} custom-call(f32[8,128]{1,0:T(8,128)S(1)} %copy-done.10, bf16[1024,512]{1,0:T(8,128)(2,1)S(1)} %get-tuple-element.41.refs_2_.left_ref.refs_4_, f32[8,128,128]{2,1,0:T(8,128)S(1)} %copy-done.13, bf16[4,656,128]{2,1,0:T(8,128)(2,1)} %collective-permute-done.9.x_high.one_ref, ...), custom_call_target="tpu_custom_call" | custom-call | flops 20000000000 | tf_op jit(solution)/shard_map/coupled/pallas_call | solution.py:24
  58.0 2.6 %exchange.1 = f32[8,128,128]{2,1,0:T(8,128)} custom-call(s32[8,2]{1,0:T(8,128)S(1)} %copy-done.8, s32[16]{0:T(128)S(1)} %copy-done.11, s32[1]{0:T(128)} %bitcast.3.upper_ref, bf16[1,512,512]{2,1,0:T(8,128)(2,1)S(1)} %bitcast.13, bf16[1,512,512]{2,1,0:T(8,128)(2,1)S(1)} %bitcast.14, bf16[1024,512]{1,0:T(8,128)(2,1)S(1)} %get-tuple-element.41.refs_2_.left_ref.refs_4_, ...), custom_call_target="tpu_custom_call" | custom-call | tf_op jit(solution)/shard_map/exchange/pallas_call | solution.py:24
  (35 shorter events, 0.1 us)
Async XLA Ops:
  0.0 18.9 %collective-permute-start = (bf16[512,512]{1,0:T(8,128)(2,1)}, bf16[512,512]{1,0:T(8,128)(2,1)}, u32[]{:S(2)}, u32[]{:S(2)}) collective-permute-start(bf16[512,512]{1,0:T(8,128)(2,1)} %bitcast.4), channel_id=1, source_target_pairs={{0,2},{1,3},{2,4},{3,5},{4,6},{5,7},{6,0},{7,1},{8,10},{9,11},{10,... | collective-permute-start | bytes 1572872 | tf_op jit(solution)/shard_map/ppermute | solution.py:362
  3.0 25.8 %collective-permute-start.6 = (bf16[512,512]{1,0:T(8,128)(2,1)}, bf16[512,512]{1,0:T(8,128)(2,1)}, u32[]{:S(2)}, u32[]{:S(2)}) collective-permute-start(bf16[512,512]{1,0:T(8,128)(2,1)} %bitcast.4), channel_id=1, source_target_pairs={{0,6},{1,7},{2,0},{3,1},{4,2},{5,3},{6,4},{7,5},{8,14},{9,15},{10,... | collective-permute-start | bytes 1572872 | tf_op jit(solution)/shard_map/ppermute | solution.py:362
  8.8 18.3 %collective-permute-start.2 = (bf16[4,656,128]{2,1,0:T(8,128)(2,1)}, bf16[4,656,128]{2,1,0:T(8,128)(2,1)S(1)}, u32[]{:S(2)}, u32[]{:S(2)}) collective-permute-start(bf16[4,656,128]{2,1,0:T(8,128)(2,1)} %get-tuple-element.46.low_ref), channel_id=1, source_target_pairs={{0,8},{8,0},{16,24},{24,16},{1,9},{9,1},{17,25},{25,17},{2,10},{10... | collective-permute-start | bytes 2015240 | tf_op jit(solution)/shard_map/ppermute | solution.py:356
  10.6 18.2 %collective-permute-start.3 = (bf16[4,656,128]{2,1,0:T(8,128)(2,1)}, bf16[4,656,128]{2,1,0:T(8,128)(2,1)S(1)}, u32[]{:S(2)}, u32[]{:S(2)}) collective-permute-start(bf16[4,656,128]{2,1,0:T(8,128)(2,1)} %get-tuple-element.45.high_ref), channel_id=1, source_target_pairs={{0,16},{8,24},{16,0},{24,8},{1,17},{9,25},{17,1},{25,9},{2,18},{10... | collective-permute-start | bytes 2015240 | tf_op jit(solution)/shard_map/ppermute | solution.py:359
  12.1 35.1 %collective-permute-start.9 = (bf16[4,656,128]{2,1,0:T(8,128)(2,1)}, bf16[4,656,128]{2,1,0:T(8,128)(2,1)}, u32[]{:S(2)}, u32[]{:S(2)}) collective-permute-start(bf16[4,656,128]{2,1,0:T(8,128)(2,1)} %get-tuple-element.45.high_ref), channel_id=1, source_target_pairs={{0,8},{8,0},{16,24},{24,16},{1,9},{9,1},{17,25},{25,17},{2,10},{10... | collective-permute-start | bytes 2015240 | tf_op jit(solution)/shard_map/ppermute | solution.py:356
  12.7 1.1 %copy-start.4 = (bf16[4,656,128]{2,1,0:T(8,128)(2,1)S(1)}, bf16[4,656,128]{2,1,0:T(8,128)(2,1)}, u32[]{:S(2)}) copy-start(bf16[4,656,128]{2,1,0:T(8,128)(2,1)} %get-tuple-element.45.high_ref) | copy-start | bytes 2015236
  13.8 0.7 %copy-start.9 = (f32[8,128]{1,0:T(8,128)S(1)}, f32[8,128]{1,0:T(8,128)}, u32[]{:S(2)}) copy-start(f32[8,128]{1,0:T(8,128)} %get-tuple-element.34.weight_ref) | copy-start | bytes 12292
  19.0 28.2 %collective-permute-start.10 = (bf16[4,656,128]{2,1,0:T(8,128)(2,1)}, bf16[4,656,128]{2,1,0:T(8,128)(2,1)}, u32[]{:S(2)}, u32[]{:S(2)}) collective-permute-start(bf16[4,656,128]{2,1,0:T(8,128)(2,1)} %get-tuple-element.46.low_ref), channel_id=1, source_target_pairs={{0,16},{8,24},{16,0},{24,8},{1,17},{9,25},{17,1},{25,9},{2,18},{10... | collective-permute-start | bytes 2015240 | tf_op jit(solution)/shard_map/ppermute | solution.py:359
  19.9 0.7 %copy-start.7 = (s32[8,2]{1,0:T(8,128)S(1)}, s32[8,2]{1,0:T(8,128)}, u32[]{:S(2)}) copy-start(s32[8,2]{1,0:T(8,128)} %get-tuple-element.28.uses_ref) | copy-start | bytes 196
  20.6 8.7 %copy-start.10 = (f32[8,128]{1,0:T(8,128)S(1)}, f32[8,128]{1,0:T(8,128)}, u32[]{:S(2)}) copy-start(f32[8,128]{1,0:T(8,128)} %get-tuple-element.34.weight_ref) | copy-start | bytes 12292
  22.4 21.5 %copy-start.8 = (s32[8,2]{1,0:T(8,128)S(1)}, s32[8,2]{1,0:T(8,128)}, u32[]{:S(2)}) copy-start(s32[8,2]{1,0:T(8,128)} %get-tuple-element.28.uses_ref) | copy-start | bytes 196
  27.1 6.2 %copy-start = (bf16[4,656,128]{2,1,0:T(8,128)(2,1)}, bf16[4,656,128]{2,1,0:T(8,128)(2,1)S(1)}, u32[]{:S(2)}) copy-start(bf16[4,656,128]{2,1,0:T(8,128)(2,1)S(1)} %collective-permute-done.2.one_ref.x_low) | copy-start | bytes 2015236
  27.1 13.9 %collective-permute-start.1 = (bf16[512,512]{1,0:T(8,128)(2,1)}, bf16[512,512]{1,0:T(8,128)(2,1)S(1)}, u32[]{:S(2)}, u32[]{:S(2)}) collective-permute-start(bf16[512,512]{1,0:T(8,128)(2,1)} %collective-permute-done), channel_id=1, source_target_pairs={{0,2},{1,3},{2,4},{3,5},{4,6},{5,7},{6,0},{7,1},{8,10},{9,11},{10,... | collective-permute-start | bytes 1572872 | tf_op jit(solution)/shard_map/ppermute | solution.py:362
  28.8 4.5 %copy-start.2 = (bf16[4,656,128]{2,1,0:T(8,128)(2,1)}, bf16[4,656,128]{2,1,0:T(8,128)(2,1)S(1)}, u32[]{:S(2)}) copy-start(bf16[4,656,128]{2,1,0:T(8,128)(2,1)S(1)} %collective-permute-done.3.two_ref.y_high) | copy-start | bytes 2015236
  28.8 13.7 %collective-permute-start.4 = (bf16[512,512]{1,0:T(8,128)(2,1)}, bf16[512,512]{1,0:T(8,128)(2,1)}, u32[]{:S(2)}, u32[]{:S(2)}) collective-permute-start(bf16[512,512]{1,0:T(8,128)(2,1)} %bitcast.4), channel_id=1, source_target_pairs={{0,1},{1,0},{2,3},{3,2},{4,5},{5,4},{6,7},{7,6},{8,9},{9,8},{10,11... | collective-permute-start | bytes 1572872 | tf_op jit(solution)/shard_map/ppermute | solution.py:365
  28.9 15.0 %collective-permute-start.5 = (bf16[512,512]{1,0:T(8,128)(2,1)}, bf16[512,512]{1,0:T(8,128)(2,1)}, u32[]{:S(2)}, u32[]{:S(2)}) collective-permute-start(bf16[512,512]{1,0:T(8,128)(2,1)} %collective-permute-done), channel_id=1, source_target_pairs={{0,1},{1,0},{2,3},{3,2},{4,5},{5,4},{6,7},{7,6},{8,9},{9,8},{10,11... | collective-permute-start | bytes 1572872 | tf_op jit(solution)/shard_map/ppermute | solution.py:365
  33.3 7.6 %copy-start.12 = (f32[8,128,128]{2,1,0:T(8,128)}, f32[8,128,128]{2,1,0:T(8,128)S(1)}, u32[]{:S(2)}) copy-start(f32[8,128,128]{2,1,0:T(8,128)S(1)} %coupled.2.acc_ref) | copy-start | bytes 1572868
  41.0 0.8 %copy-start.5 = (bf16[512,512]{1,0:T(8,128)(2,1)}, bf16[512,512]{1,0:T(8,128)(2,1)S(1)}, u32[]{:S(2)}) copy-start(bf16[512,512]{1,0:T(8,128)(2,1)S(1)} %collective-permute-done.1) | copy-start | bytes 1572868
  41.8 11.0 %collective-permute-start.12 = (bf16[4,128,128]{2,1,0:T(8,128)(2,1)}, bf16[4,128,128]{2,1,0:T(8,128)(2,1)S(1)}, u32[]{:S(2)}, u32[]{:S(2)}) collective-permute-start(bf16[4,128,128]{2,1,0:T(8,128)(2,1)} %get-tuple-element.49), channel_id=1, source_target_pairs={{0,16},{8,24},{16,0},{24,8},{1,17},{9,25},{17,1},{25,9},{2,18},{10... | collective-permute-start | bytes 393224 | tf_op jit(solution)/shard_map/ppermute | solution.py:359
  42.5 15.4 %collective-permute-start.11 = (bf16[4,128,128]{2,1,0:T(8,128)(2,1)S(1)}, bf16[4,128,128]{2,1,0:T(8,128)(2,1)S(1)}, u32[]{:S(2)}, u32[]{:S(2)}) collective-permute-start(bf16[4,128,128]{2,1,0:T(8,128)(2,1)S(1)} %get-tuple-element.40), channel_id=1, source_target_pairs={{0,8},{8,0},{16,24},{24,16},{1,9},{9,1},{17,25},{25,17},{2,10},{10... | collective-permute-start | bytes 393224 | tf_op jit(solution)/shard_map/ppermute | solution.py:356
  43.8 1.0 %copy-start.6 = (bf16[512,512]{1,0:T(8,128)(2,1)S(1)}, bf16[512,512]{1,0:T(8,128)(2,1)}, u32[]{:S(2)}) copy-start(bf16[512,512]{1,0:T(8,128)(2,1)} %copy-done.5) | copy-start | bytes 1572868
  44.9 2.3 %copy-start.1 = (bf16[4,656,128]{2,1,0:T(8,128)(2,1)S(1)}, bf16[4,656,128]{2,1,0:T(8,128)(2,1)}, u32[]{:S(2)}) copy-start(bf16[4,656,128]{2,1,0:T(8,128)(2,1)} %copy-done) | copy-start | bytes 2015236
  44.9 2.3 %copy-start.3 = (bf16[4,656,128]{2,1,0:T(8,128)(2,1)S(1)}, bf16[4,656,128]{2,1,0:T(8,128)(2,1)}, u32[]{:S(2)}) copy-start(bf16[4,656,128]{2,1,0:T(8,128)(2,1)} %copy-done.2) | copy-start | bytes 2015236
  47.2 6.1 %copy-start.13 = (f32[8,128,128]{2,1,0:T(8,128)S(1)}, f32[8,128,128]{2,1,0:T(8,128)}, u32[]{:S(2)}) copy-start(f32[8,128,128]{2,1,0:T(8,128)} %copy-done.12) | copy-start | bytes 1572868
  50.7 7.3 %collective-permute-start.13 = (bf16[4,128,128]{2,1,0:T(8,128)(2,1)S(1)}, bf16[4,128,128]{2,1,0:T(8,128)(2,1)S(1)}, u32[]{:S(2)}, u32[]{:S(2)}) collective-permute-start(bf16[4,128,128]{2,1,0:T(8,128)(2,1)S(1)} %get-tuple-element.47), channel_id=1, source_target_pairs={{0,8},{8,0},{16,24},{24,16},{1,9},{9,1},{17,25},{25,17},{2,10},{10... | collective-permute-start | bytes 393224 | tf_op jit(solution)/shard_map/ppermute | solution.py:356
  51.5 6.5 %copy-start.11 = (s32[16]{0:T(128)S(1)}, s32[16]{0:T(128)}, u32[]{:S(2)}) copy-start(s32[16]{0:T(128)} %get-tuple-element.29.turn_ref) | copy-start | bytes 196
  51.5 6.5 %collective-permute-start.14 = (bf16[4,128,128]{2,1,0:T(8,128)(2,1)S(1)}, bf16[4,128,128]{2,1,0:T(8,128)(2,1)S(1)}, u32[]{:S(2)}, u32[]{:S(2)}) collective-permute-start(bf16[4,128,128]{2,1,0:T(8,128)(2,1)S(1)} %get-tuple-element.50), channel_id=1, source_target_pairs={{0,16},{8,24},{16,0},{24,8},{1,17},{9,25},{17,1},{25,9},{2,18},{10... | collective-permute-start | bytes 393224 | tf_op jit(solution)/shard_map/ppermute | solution.py:359
  52.8 5.2 %collective-permute-start.7 = (bf16[512,512]{1,0:T(8,128)(2,1)S(1)}, bf16[512,512]{1,0:T(8,128)(2,1)S(1)}, u32[]{:S(2)}, u32[]{:S(2)}) collective-permute-start(bf16[512,512]{1,0:T(8,128)(2,1)S(1)} %copy-done.6), channel_id=1, source_target_pairs={{0,1},{1,0},{2,3},{3,2},{4,5},{5,4},{6,7},{7,6},{8,9},{9,8},{10,11... | collective-permute-start | bytes 1572872 | tf_op jit(solution)/shard_map/ppermute | solution.py:365
  52.8 5.2 %collective-permute-start.8 = (bf16[512,512]{1,0:T(8,128)(2,1)}, bf16[512,512]{1,0:T(8,128)(2,1)S(1)}, u32[]{:S(2)}, u32[]{:S(2)}) collective-permute-start(bf16[512,512]{1,0:T(8,128)(2,1)} %collective-permute-done.6), channel_id=1, source_target_pairs={{0,1},{1,0},{2,3},{3,2},{4,5},{5,4},{6,7},{7,6},{8,9},{9,8},{10,11... | collective-permute-start | bytes 1572872 | tf_op jit(solution)/shard_map/ppermute | solution.py:365

commit v3 on v2

--- a/solution.py
+++ b/solution.py
@@ -280,13 +280,13 @@
     for k in range(2):
         copy(base_ref, k, 0, 2 * k)
         copy(amp_ref, k, orbs, 2 * k + 1)
-    lane = lax.broadcasted_iota(jnp.int32, (1, pno), 1)
+    assert pairs & (pairs - 1) == 0
+    named = lax.broadcasted_iota(jnp.int32, (1, pno), 1) ^ (group * pairs)
     for p in range(pairs):
         counts = jnp.zeros((1, pno), jnp.float32)
+        length = length_ref[p]
         for s in range(coupled_ref.shape[1]):
-            named = coupled_ref[p, s]
-            at = (lax.div(named, pairs) ^ group) * pairs + lax.rem(named, pairs)
-            counts += jnp.where(lane == jnp.where(s < length_ref[p], at, -1), scale, 0.0)
+            counts += jnp.where(named == jnp.where(s < length, coupled_ref[p, s], -1), scale, 0.0)
         weight_ref[p : p + 1, :] = counts
         rows = slice(orbs + amp_ref.shape[1], held_ref.shape[2])
         held_ref[p // half, p % half, rows, :] = jnp.broadcast_to(counts, (16, pno)).astype(jnp.bfloat16)
@@ -310,8 +310,8 @@
         position = owner_ref[orbs_ref[f % 2, f // 2]]
         k = position
         if chips <= RING_CHIPS:
-            steps = lax.rem(lax.div(me, 2) - lax.div(position, 2) + chips, chips)
-            swapped = lax.rem(position, 2) ^ lax.rem(me, 2)
+            steps = lax.rem((me >> 1) - (position >> 1) + chips, chips)
+            swapped = (position ^ me) & 1
             k = jnp.where(steps < 2, steps + 2 * swapped, steps + 2 + 2 * swapped)
         turn_ref[f] = k
         uses_ref[k, 1] = uses_ref[k, 0]
@@ -371,7 +371,7 @@
     upper = (group // 2).astype(jnp.int32).reshape(1)
 
     x_lo, y_hi = along_x(own_lo), along_y(own_hi)
-    x_hi, y_lo = along_x(after(own_hi, own_lo)), along_y(after(own_lo, own_hi))
+    x_hi, y_lo = along_x(after(own_hi, own_lo)), along_y(after(own_lo, own_hi, x_lo))
 
     slab = integral_slabs[0]
     around = chips <= RING_CHIPS

time: 61.1 us -> 59.9 us (0.980)
  waiting for transfers between devices: 11.4 us -> 9.43 us
  starting transfers between devices: 15 us -> 15.7 us
    ppermute x4, waiting for transfers between devices: 1.72 us -> 0.21 us  [along_y(): return lax.ppermute(value, 'grp', [(g, g ^ 2) for g in range(n_grp)])]
    ppermute x3, waiting for transfers between devices: 4.88 us -> 3.55 us  [along_chips(): lax.ppermute(value, 'dev', [(d, (d + 2 * step) % n_dev) for d in range(n_...]
    ppermute x4, waiting for transfers between devices: 4.75 us -> 5.66 us  [along_x(): return lax.ppermute(value, 'grp', [(g, g ^ 1) for g in range(n_grp)])]
  transfers between devices with their start and end apart: 15 -> 15, of which waited for: 3 -> 3; matrix products, arithmetic and copies ran while one was open for 0% -> 0% of each run, Pallas kernels for 45% -> 46%
where the time goes in v3:
time: 59.9 us; the launch traced here: 59.5 us
  Pallas kernels  29.8 us (50%)
  starting transfers between devices  15.7 us (26%)
  waiting for transfers between devices  9.43 us (16%)
  local copies, waits for them, and re-layouts  4.36 us (7%)
    pallas_call x8, Pallas kernels, call_kernel(): pl.pallas_call(body, out_shape=out_shape, in_specs=[SMEM_SPEC] * len(smem...  26 us
    ppermute x4, waiting for transfers between devices, along_x(): return lax.ppermute(value, 'grp', [(g, g ^ 1) for g in range(n_grp)])  5.66 us
    ppermute x4, starting transfers between devices, along_y(): return lax.ppermute(value, 'grp', [(g, g ^ 2) for g in range(n_grp)])  5.12 us
    ppermute x3, starting transfers between devices, along_chips(): lax.ppermute(value, 'dev', [(d, (d + 2 * step) % n_dev) for d in range(n_...  5.11 us
    ppermute x4, starting transfers between devices, along_x(): return lax.ppermute(value, 'grp', [(g, g ^ 1) for g in range(n_grp)])  4.4 us
    unnamed x28, local copies, waits for them, and re-layouts  4.36 us
    pallas_call x1, Pallas kernels, pack(): pl.pallas_call(functools.partial(pack_kernel, orbs / pno, chips), out_sha...  3.77 us
    ppermute x3, waiting for transfers between devices, along_chips(): lax.ppermute(value, 'dev', [(d, (d + 2 * step) % n_dev) for d in range(n_...  3.55 us
  transfers between devices with their start and end apart: 15, of which 3 were waited for; matrix products, arithmetic and copies ran while one was open for 0% of the time, Pallas kernels for 46%

profile of v3, /device:TPU:0, one launch (start us, length us, event | category | flops | bytes accessed | tf_op | source)
XLA Modules:
  0.0 59.5 jit_solution(954464328417936332)
XLA Ops:
  0.0 3.0 %collective-permute-start = (bf16[512,512]{1,0:T(8,128)(2,1)}, bf16[512,512]{1,0:T(8,128)(2,1)}, u32[]{:S(2)}, u32[]{:S(2)}) collective-permute-start(bf16[512,512]{1,0:T(8,128)(2,1)} %bitcast.4), channel_id=1, source_target_pairs={{0,2},{1,3},{2,4},{3,5},{4,6},{5,7},{6,0},{7,1},{8,10},{9,11},{10,... | collective-permute-start | bytes 1572872 | tf_op jit(solution)/shard_map/ppermute | solution.py:362
  3.0 2.0 %collective-permute-start.6 = (bf16[512,512]{1,0:T(8,128)(2,1)}, bf16[512,512]{1,0:T(8,128)(2,1)}, u32[]{:S(2)}, u32[]{:S(2)}) collective-permute-start(bf16[512,512]{1,0:T(8,128)(2,1)} %bitcast.4), channel_id=1, source_target_pairs={{0,6},{1,7},{2,0},{3,1},{4,2},{5,3},{6,4},{7,5},{8,14},{9,15},{10,... | collective-permute-start | bytes 1572872 | tf_op jit(solution)/shard_map/ppermute | solution.py:362
  5.1 3.8 %pack.1 = (bf16[4,656,128]{2,1,0:T(8,128)(2,1)}, bf16[4,656,128]{2,1,0:T(8,128)(2,1)}, f32[8,128]{1,0:T(8,128)}, s32[8,2]{1,0:T(8,128)}, s32[16]{0:T(128)}) custom-call(s32[1]{0:T(128)} %bitcast.group_ref, s32[1]{0:T(128)} %bitcast.1.me_ref, s32[8,32]{1,0:T(8,128)} %coupled_ref.1, s32[8]{0:T(128)} %length_ref.1, s32[8]{0:T(128)} %owner_ref.1, ...), custom_call_target="tpu_custom_call" | custom-call | tf_op jit(solution)/shard_map/pack/pallas_call | solution.py:326
  8.8 1.8 %collective-permute-start.2 = (bf16[4,656,128]{2,1,0:T(8,128)(2,1)}, bf16[4,656,128]{2,1,0:T(8,128)(2,1)S(1)}, u32[]{:S(2)}, u32[]{:S(2)}) collective-permute-start(bf16[4,656,128]{2,1,0:T(8,128)(2,1)} %get-tuple-element.46.low_ref), channel_id=1, source_target_pairs={{0,8},{8,0},{16,24},{24,16},{1,9},{9,1},{17,25},{25,17},{2,10},{10... | collective-permute-start | bytes 2015240 | tf_op jit(solution)/shard_map/ppermute | solution.py:356
  10.6 1.5 %collective-permute-start.3 = (bf16[4,656,128]{2,1,0:T(8,128)(2,1)}, bf16[4,656,128]{2,1,0:T(8,128)(2,1)S(1)}, u32[]{:S(2)}, u32[]{:S(2)}) collective-permute-start(bf16[4,656,128]{2,1,0:T(8,128)(2,1)} %get-tuple-element.45.high_ref), channel_id=1, source_target_pairs={{0,16},{8,24},{16,0},{24,8},{1,17},{9,25},{17,1},{25,9},{2,18},{10... | collective-permute-start | bytes 2015240 | tf_op jit(solution)/shard_map/ppermute | solution.py:359
  12.1 0.5 collective-permute-start.9
  12.7 1.1 %copy-done.4 = bf16[4,656,128]{2,1,0:T(8,128)(2,1)S(1)} copy-done((bf16[4,656,128]{2,1,0:T(8,128)(2,1)S(1)}, bf16[4,656,128]{2,1,0:T(8,128)(2,1)}, u32[]{:S(2)}) %copy-start.4) | copy-done | bytes 671768
  13.8 0.7 %copy-done.9 = f32[8,128]{1,0:T(8,128)S(1)} copy-done((f32[8,128]{1,0:T(8,128)S(1)}, f32[8,128]{1,0:T(8,128)}, u32[]{:S(2)}) %copy-start.9) | copy-done | bytes 4120
  14.5 4.5 %own_coupled.1 = (f32[8,128,128]{2,1,0:T(8,128)S(1)}, bf16[1024,512]{1,0:T(8,128)(2,1)S(1)}) custom-call(f32[8,128]{1,0:T(8,128)S(1)} %copy-done.9, bf16[4,656,128]{2,1,0:T(8,128)(2,1)} %get-tuple-element.46.low_ref, bf16[4,656,128]{2,1,0:T(8,128)(2,1)S(1)} %copy-done.4), custom_call_target="tpu_custom_call" | custom-call | tf_op jit(solution)/shard_map/own_coupled/pallas_call | solution.py:24
  18.9 0.0 collective-permute-done
  19.0 0.7 %copy-done.7 = s32[8,2]{1,0:T(8,128)S(1)} copy-done((s32[8,2]{1,0:T(8,128)S(1)}, s32[8,2]{1,0:T(8,128)}, u32[]{:S(2)}) %copy-start.7) | copy-done | bytes 88
  19.6 1.7 %halves.1.refs_5_ = bf16[17,512,128]{2,1,0:T(8,128)(2,1)S(1)} custom-call(s32[8,2]{1,0:T(8,128)S(1)} %copy-done.7, bf16[1,512,512]{2,1,0:T(8,128)(2,1)} %refs_0_.1, bf16[1,512,512]{2,1,0:T(8,128)(2,1)} %bitcast.9.refs_1_, bf16[1024,512]{1,0:T(8,128)(2,1)S(1)} %get-tuple-element.41.refs_2_.left_ref.refs_4_), custom_call_target="tpu_custom_call" | custom-call | flops 20000000000 | tf_op jit(solution)/shard_map/halves/pallas_call | solution.py:24
  21.4 0.1 collective-permute-start.1
  21.5 5.7 %collective-permute-done.2.one_ref.x_low = bf16[4,656,128]{2,1,0:T(8,128)(2,1)S(1)} collective-permute-done((bf16[4,656,128]{2,1,0:T(8,128)(2,1)}, bf16[4,656,128]{2,1,0:T(8,128)(2,1)S(1)}, u32[]{:S(2)}, u32[]{:S(2)}) %collective-permute-start.2) | collective-permute-done | bytes 671776 | tf_op jit(solution)/shard_map/ppermute | solution.py:356
  27.1 1.7 %collective-permute-start.10 = (bf16[4,656,128]{2,1,0:T(8,128)(2,1)}, bf16[4,656,128]{2,1,0:T(8,128)(2,1)}, u32[]{:S(2)}, u32[]{:S(2)}) collective-permute-start(bf16[4,656,128]{2,1,0:T(8,128)(2,1)} %get-tuple-element.46.low_ref), channel_id=1, source_target_pairs={{0,16},{8,24},{16,0},{24,8},{1,17},{9,25},{17,1},{25,9},{2,18},{10... | collective-permute-start | bytes 2015240 | tf_op jit(solution)/shard_map/ppermute | solution.py:359
  28.9 0.5 collective-permute-start.5
  29.4 4.0 %coupled.2.acc_ref = f32[8,128,128]{2,1,0:T(8,128)S(1)} custom-call(f32[8,128]{1,0:T(8,128)S(1)} %copy-done.10, bf16[1024,512]{1,0:T(8,128)(2,1)S(1)} %get-tuple-element.41.refs_2_.left_ref.refs_4_, f32[8,128,128]{2,1,0:T(8,128)S(1)} %get-tuple-element.37.acc_ref, bf16[4,656,128]{2,1,0:T(8,128)(2,1)S(1)} %collective-permute-done.2.one_ref.x_low, ...), custom_call_target="tpu_custom_call" | custom-call | flops 20000000000 | tf_op jit(solution)/shard_map/coupled/pallas_call | solution.py:24
  33.4 2.8 %first_across.1 = (bf16[4,128,128]{2,1,0:T(8,128)(2,1)S(1)}, bf16[4,128,128]{2,1,0:T(8,128)(2,1)}) custom-call(bf16[4,656,128]{2,1,0:T(8,128)(2,1)S(1)} %collective-permute-done.2.one_ref.x_low, bf16[4,656,128]{2,1,0:T(8,128)(2,1)S(1)} %collective-permute-done.3.two_ref.y_high), custom_call_target="tpu_custom_call" | custom-call | tf_op jit(solution)/shard_map/first_across/pallas_call | solution.py:24
  36.1 3.5 %collective-permute-done.1 = bf16[512,512]{1,0:T(8,128)(2,1)S(1)} collective-permute-done((bf16[512,512]{1,0:T(8,128)(2,1)}, bf16[512,512]{1,0:T(8,128)(2,1)S(1)}, u32[]{:S(2)}, u32[]{:S(2)}) %collective-permute-start.1) | collective-permute-done | bytes 524320 | tf_op jit(solution)/shard_map/ppermute | solution.py:362
  39.7 0.8 %copy-done.5 = bf16[512,512]{1,0:T(8,128)(2,1)} copy-done((bf16[512,512]{1,0:T(8,128)(2,1)}, bf16[512,512]{1,0:T(8,128)(2,1)S(1)}, u32[]{:S(2)}) %copy-start.5) | copy-done | bytes 524312
  40.5 1.5 %collective-permute-start.12 = (bf16[4,128,128]{2,1,0:T(8,128)(2,1)}, bf16[4,128,128]{2,1,0:T(8,128)(2,1)S(1)}, u32[]{:S(2)}, u32[]{:S(2)}) collective-permute-start(bf16[4,128,128]{2,1,0:T(8,128)(2,1)} %get-tuple-element.49), channel_id=1, source_target_pairs={{0,16},{8,24},{16,0},{24,8},{1,17},{9,25},{17,1},{25,9},{2,18},{10... | collective-permute-start | bytes 393224 | tf_op jit(solution)/shard_map/ppermute | solution.py:359
  42.0 1.5 %collective-permute-start.11 = (bf16[4,128,128]{2,1,0:T(8,128)(2,1)S(1)}, bf16[4,128,128]{2,1,0:T(8,128)(2,1)S(1)}, u32[]{:S(2)}, u32[]{:S(2)}) collective-permute-start(bf16[4,128,128]{2,1,0:T(8,128)(2,1)S(1)} %get-tuple-element.40), channel_id=1, source_target_pairs={{0,8},{8,0},{16,24},{24,16},{1,9},{9,1},{17,25},{25,17},{2,10},{10... | collective-permute-start | bytes 393224 | tf_op jit(solution)/shard_map/ppermute | solution.py:356
  43.5 1.0 %copy-done.6 = bf16[512,512]{1,0:T(8,128)(2,1)S(1)} copy-done((bf16[512,512]{1,0:T(8,128)(2,1)S(1)}, bf16[512,512]{1,0:T(8,128)(2,1)}, u32[]{:S(2)}) %copy-start.6) | copy-done | bytes 524312
  44.6 2.3 %more_halves.1.refs_3_ = bf16[17,512,128]{2,1,0:T(8,128)(2,1)S(1)} custom-call(s32[8,2]{1,0:T(8,128)S(1)} %copy-done.8, bf16[1,512,512]{2,1,0:T(8,128)(2,1)} %bitcast.5.refs_0_, bf16[1,512,512]{2,1,0:T(8,128)(2,1)} %bitcast.6.refs_1_, bf16[1,512,512]{2,1,0:T(8,128)(2,1)S(1)} %bitcast.12, ...), custom_call_target="tpu_custom_call", output_to_operand_aliasing={{}: (6, {})} | custom-call | tf_op jit(solution)/shard_map/more_halves/pallas_call | solution.py:24
  46.9 0.1 collective-permute-start.7
  47.0 0.5 collective-permute-start.8
  47.5 3.6 %second_across.1 = (bf16[4,128,128]{2,1,0:T(8,128)(2,1)S(1)}, bf16[4,128,128]{2,1,0:T(8,128)(2,1)S(1)}) custom-call(s32[1]{0:T(128)} %bitcast.3.upper_ref, bf16[4,656,128]{2,1,0:T(8,128)(2,1)S(1)} %copy-done.1, bf16[4,656,128]{2,1,0:T(8,128)(2,1)} %collective-permute-done.9.x_high.one_ref, bf16[4,656,128]{2,1,0:T(8,128)(2,1)} %collective-permute-done.10.y_low.two_ref, ...), custom_call_target="tpu_custom_call" | custom-call | tf_op jit(solution)/shard_map/second_across/pallas_call | solution.py:24
  51.0 0.6 %collective-permute-start.13 = (bf16[4,128,128]{2,1,0:T(8,128)(2,1)S(1)}, bf16[4,128,128]{2,1,0:T(8,128)(2,1)S(1)}, u32[]{:S(2)}, u32[]{:S(2)}) collective-permute-start(bf16[4,128,128]{2,1,0:T(8,128)(2,1)S(1)} %get-tuple-element.47), channel_id=1, source_target_pairs={{0,8},{8,0},{16,24},{24,16},{1,9},{9,1},{17,25},{25,17},{2,10},{10... | collective-permute-start | bytes 393224 | tf_op jit(solution)/shard_map/ppermute | solution.py:356
  51.7 0.3 collective-permute-start.14
  52.0 4.7 %coupled.3.refs_4_ = f32[8,128,128]{2,1,0:T(8,128)S(1)} custom-call(f32[8,128]{1,0:T(8,128)S(1)} %copy-done.10, bf16[1024,512]{1,0:T(8,128)(2,1)S(1)} %get-tuple-element.41.refs_2_.left_ref.refs_4_, f32[8,128,128]{2,1,0:T(8,128)S(1)} %copy-done.13, bf16[4,656,128]{2,1,0:T(8,128)(2,1)} %collective-permute-done.9.x_high.one_ref, ...), custom_call_target="tpu_custom_call" | custom-call | flops 20000000000 | tf_op jit(solution)/shard_map/coupled/pallas_call | solution.py:24
  56.7 0.2 collective-permute-done.14.refs_8_
  56.9 2.6 %exchange.1 = f32[8,128,128]{2,1,0:T(8,128)} custom-call(s32[8,2]{1,0:T(8,128)S(1)} %copy-done.8, s32[16]{0:T(128)S(1)} %copy-done.11, s32[1]{0:T(128)} %bitcast.3.upper_ref, bf16[1,512,512]{2,1,0:T(8,128)(2,1)S(1)} %bitcast.13, bf16[1,512,512]{2,1,0:T(8,128)(2,1)S(1)} %bitcast.14, bf16[1024,512]{1,0:T(8,128)(2,1)S(1)} %get-tuple-element.41.refs_2_.left_ref.refs_4_, ...), custom_call_target="tpu_custom_call" | custom-call | tf_op jit(solution)/shard_map/exchange/pallas_call | solution.py:24
  (35 shorter events, 0.1 us)
Async XLA Ops:
  0.0 18.9 %collective-permute-start = (bf16[512,512]{1,0:T(8,128)(2,1)}, bf16[512,512]{1,0:T(8,128)(2,1)}, u32[]{:S(2)}, u32[]{:S(2)}) collective-permute-start(bf16[512,512]{1,0:T(8,128)(2,1)} %bitcast.4), channel_id=1, source_target_pairs={{0,2},{1,3},{2,4},{3,5},{4,6},{5,7},{6,0},{7,1},{8,10},{9,11},{10,... | collective-permute-start | bytes 1572872 | tf_op jit(solution)/shard_map/ppermute | solution.py:362
  3.0 25.9 %collective-permute-start.6 = (bf16[512,512]{1,0:T(8,128)(2,1)}, bf16[512,512]{1,0:T(8,128)(2,1)}, u32[]{:S(2)}, u32[]{:S(2)}) collective-permute-start(bf16[512,512]{1,0:T(8,128)(2,1)} %bitcast.4), channel_id=1, source_target_pairs={{0,6},{1,7},{2,0},{3,1},{4,2},{5,3},{6,4},{7,5},{8,14},{9,15},{10,... | collective-permute-start | bytes 1572872 | tf_op jit(solution)/shard_map/ppermute | solution.py:362
  8.8 18.3 %collective-permute-start.2 = (bf16[4,656,128]{2,1,0:T(8,128)(2,1)}, bf16[4,656,128]{2,1,0:T(8,128)(2,1)S(1)}, u32[]{:S(2)}, u32[]{:S(2)}) collective-permute-start(bf16[4,656,128]{2,1,0:T(8,128)(2,1)} %get-tuple-element.46.low_ref), channel_id=1, source_target_pairs={{0,8},{8,0},{16,24},{24,16},{1,9},{9,1},{17,25},{25,17},{2,10},{10... | collective-permute-start | bytes 2015240 | tf_op jit(solution)/shard_map/ppermute | solution.py:356
  10.6 18.3 %collective-permute-start.3 = (bf16[4,656,128]{2,1,0:T(8,128)(2,1)}, bf16[4,656,128]{2,1,0:T(8,128)(2,1)S(1)}, u32[]{:S(2)}, u32[]{:S(2)}) collective-permute-start(bf16[4,656,128]{2,1,0:T(8,128)(2,1)} %get-tuple-element.45.high_ref), channel_id=1, source_target_pairs={{0,16},{8,24},{16,0},{24,8},{1,17},{9,25},{17,1},{25,9},{2,18},{10... | collective-permute-start | bytes 2015240 | tf_op jit(solution)/shard_map/ppermute | solution.py:359
  12.1 34.8 %collective-permute-start.9 = (bf16[4,656,128]{2,1,0:T(8,128)(2,1)}, bf16[4,656,128]{2,1,0:T(8,128)(2,1)}, u32[]{:S(2)}, u32[]{:S(2)}) collective-permute-start(bf16[4,656,128]{2,1,0:T(8,128)(2,1)} %get-tuple-element.45.high_ref), channel_id=1, source_target_pairs={{0,8},{8,0},{16,24},{24,16},{1,9},{9,1},{17,25},{25,17},{2,10},{10... | collective-permute-start | bytes 2015240 | tf_op jit(solution)/shard_map/ppermute | solution.py:356
  12.7 1.1 %copy-start.4 = (bf16[4,656,128]{2,1,0:T(8,128)(2,1)S(1)}, bf16[4,656,128]{2,1,0:T(8,128)(2,1)}, u32[]{:S(2)}) copy-start(bf16[4,656,128]{2,1,0:T(8,128)(2,1)} %get-tuple-element.45.high_ref) | copy-start | bytes 2015236
  13.8 0.7 %copy-start.9 = (f32[8,128]{1,0:T(8,128)S(1)}, f32[8,128]{1,0:T(8,128)}, u32[]{:S(2)}) copy-start(f32[8,128]{1,0:T(8,128)} %get-tuple-element.34.weight_ref) | copy-start | bytes 12292
  19.0 0.7 %copy-start.7 = (s32[8,2]{1,0:T(8,128)S(1)}, s32[8,2]{1,0:T(8,128)}, u32[]{:S(2)}) copy-start(s32[8,2]{1,0:T(8,128)} %get-tuple-element.28.uses_ref) | copy-start | bytes 196
  19.6 9.7 %copy-start.10 = (f32[8,128]{1,0:T(8,128)S(1)}, f32[8,128]{1,0:T(8,128)}, u32[]{:S(2)}) copy-start(f32[8,128]{1,0:T(8,128)} %get-tuple-element.34.weight_ref) | copy-start | bytes 12292
  21.4 22.1 %copy-start.8 = (s32[8,2]{1,0:T(8,128)S(1)}, s32[8,2]{1,0:T(8,128)}, u32[]{:S(2)}) copy-start(s32[8,2]{1,0:T(8,128)} %get-tuple-element.28.uses_ref) | copy-start | bytes 196
  21.4 18.3 %collective-permute-start.1 = (bf16[512,512]{1,0:T(8,128)(2,1)}, bf16[512,512]{1,0:T(8,128)(2,1)S(1)}, u32[]{:S(2)}, u32[]{:S(2)}) collective-permute-start(bf16[512,512]{1,0:T(8,128)(2,1)} %collective-permute-done), channel_id=1, source_target_pairs={{0,2},{1,3},{2,4},{3,5},{4,6},{5,7},{6,0},{7,1},{8,10},{9,11},{10,... | collective-permute-start | bytes 1572872 | tf_op jit(solution)/shard_map/ppermute | solution.py:362
  27.1 6.2 %copy-start = (bf16[4,656,128]{2,1,0:T(8,128)(2,1)}, bf16[4,656,128]{2,1,0:T(8,128)(2,1)S(1)}, u32[]{:S(2)}) copy-start(bf16[4,656,128]{2,1,0:T(8,128)(2,1)S(1)} %collective-permute-done.2.one_ref.x_low) | copy-start | bytes 2015236
  27.1 20.3 %collective-permute-start.10 = (bf16[4,656,128]{2,1,0:T(8,128)(2,1)}, bf16[4,656,128]{2,1,0:T(8,128)(2,1)}, u32[]{:S(2)}, u32[]{:S(2)}) collective-permute-start(bf16[4,656,128]{2,1,0:T(8,128)(2,1)} %get-tuple-element.46.low_ref), channel_id=1, source_target_pairs={{0,16},{8,24},{16,0},{24,8},{1,17},{9,25},{17,1},{25,9},{2,18},{10... | collective-permute-start | bytes 2015240 | tf_op jit(solution)/shard_map/ppermute | solution.py:359
  28.9 4.5 %copy-start.2 = (bf16[4,656,128]{2,1,0:T(8,128)(2,1)}, bf16[4,656,128]{2,1,0:T(8,128)(2,1)S(1)}, u32[]{:S(2)}) copy-start(bf16[4,656,128]{2,1,0:T(8,128)(2,1)S(1)} %collective-permute-done.3.two_ref.y_high) | copy-start | bytes 2015236
  28.9 13.1 %collective-permute-start.4 = (bf16[512,512]{1,0:T(8,128)(2,1)}, bf16[512,512]{1,0:T(8,128)(2,1)}, u32[]{:S(2)}, u32[]{:S(2)}) collective-permute-start(bf16[512,512]{1,0:T(8,128)(2,1)} %bitcast.4), channel_id=1, source_target_pairs={{0,1},{1,0},{2,3},{3,2},{4,5},{5,4},{6,7},{7,6},{8,9},{9,8},{10,11... | collective-permute-start | bytes 1572872 | tf_op jit(solution)/shard_map/ppermute | solution.py:365
  28.9 14.6 %collective-permute-start.5 = (bf16[512,512]{1,0:T(8,128)(2,1)}, bf16[512,512]{1,0:T(8,128)(2,1)}, u32[]{:S(2)}, u32[]{:S(2)}) collective-permute-start(bf16[512,512]{1,0:T(8,128)(2,1)} %collective-permute-done), channel_id=1, source_target_pairs={{0,1},{1,0},{2,3},{3,2},{4,5},{5,4},{6,7},{7,6},{8,9},{9,8},{10,11... | collective-permute-start | bytes 1572872 | tf_op jit(solution)/shard_map/ppermute | solution.py:365
  33.4 6.3 %copy-start.12 = (f32[8,128,128]{2,1,0:T(8,128)}, f32[8,128,128]{2,1,0:T(8,128)S(1)}, u32[]{:S(2)}) copy-start(f32[8,128,128]{2,1,0:T(8,128)S(1)} %coupled.2.acc_ref) | copy-start | bytes 1572868
  39.7 0.8 %copy-start.5 = (bf16[512,512]{1,0:T(8,128)(2,1)}, bf16[512,512]{1,0:T(8,128)(2,1)S(1)}, u32[]{:S(2)}) copy-start(bf16[512,512]{1,0:T(8,128)(2,1)S(1)} %collective-permute-done.1) | copy-start | bytes 1572868
  40.5 11.2 %collective-permute-start.12 = (bf16[4,128,128]{2,1,0:T(8,128)(2,1)}, bf16[4,128,128]{2,1,0:T(8,128)(2,1)S(1)}, u32[]{:S(2)}, u32[]{:S(2)}) collective-permute-start(bf16[4,128,128]{2,1,0:T(8,128)(2,1)} %get-tuple-element.49), channel_id=1, source_target_pairs={{0,16},{8,24},{16,0},{24,8},{1,17},{9,25},{17,1},{25,9},{2,18},{10... | collective-permute-start | bytes 393224 | tf_op jit(solution)/shard_map/ppermute | solution.py:359
  42.0 14.6 %collective-permute-start.11 = (bf16[4,128,128]{2,1,0:T(8,128)(2,1)S(1)}, bf16[4,128,128]{2,1,0:T(8,128)(2,1)S(1)}, u32[]{:S(2)}, u32[]{:S(2)}) collective-permute-start(bf16[4,128,128]{2,1,0:T(8,128)(2,1)S(1)} %get-tuple-element.40), channel_id=1, source_target_pairs={{0,8},{8,0},{16,24},{24,16},{1,9},{9,1},{17,25},{25,17},{2,10},{10... | collective-permute-start | bytes 393224 | tf_op jit(solution)/shard_map/ppermute | solution.py:356
  43.5 1.0 %copy-start.6 = (bf16[512,512]{1,0:T(8,128)(2,1)S(1)}, bf16[512,512]{1,0:T(8,128)(2,1)}, u32[]{:S(2)}) copy-start(bf16[512,512]{1,0:T(8,128)(2,1)} %copy-done.5) | copy-start | bytes 1572868
  44.6 2.9 %copy-start.1 = (bf16[4,656,128]{2,1,0:T(8,128)(2,1)S(1)}, bf16[4,656,128]{2,1,0:T(8,128)(2,1)}, u32[]{:S(2)}) copy-start(bf16[4,656,128]{2,1,0:T(8,128)(2,1)} %copy-done) | copy-start | bytes 2015236
  44.6 2.9 %copy-start.3 = (bf16[4,656,128]{2,1,0:T(8,128)(2,1)S(1)}, bf16[4,656,128]{2,1,0:T(8,128)(2,1)}, u32[]{:S(2)}) copy-start(bf16[4,656,128]{2,1,0:T(8,128)(2,1)} %copy-done.2) | copy-start | bytes 2015236
  46.9 5.1 %copy-start.13 = (f32[8,128,128]{2,1,0:T(8,128)S(1)}, f32[8,128,128]{2,1,0:T(8,128)}, u32[]{:S(2)}) copy-start(f32[8,128,128]{2,1,0:T(8,128)} %copy-done.12) | copy-start | bytes 1572868
  46.9 10.0 %collective-permute-start.7 = (bf16[512,512]{1,0:T(8,128)(2,1)S(1)}, bf16[512,512]{1,0:T(8,128)(2,1)S(1)}, u32[]{:S(2)}, u32[]{:S(2)}) collective-permute-start(bf16[512,512]{1,0:T(8,128)(2,1)S(1)} %copy-done.6), channel_id=1, source_target_pairs={{0,1},{1,0},{2,3},{3,2},{4,5},{5,4},{6,7},{7,6},{8,9},{9,8},{10,11... | collective-permute-start | bytes 1572872 | tf_op jit(solution)/shard_map/ppermute | solution.py:365
  47.0 9.9 %collective-permute-start.8 = (bf16[512,512]{1,0:T(8,128)(2,1)}, bf16[512,512]{1,0:T(8,128)(2,1)S(1)}, u32[]{:S(2)}, u32[]{:S(2)}) collective-permute-start(bf16[512,512]{1,0:T(8,128)(2,1)} %collective-permute-done.6), channel_id=1, source_target_pairs={{0,1},{1,0},{2,3},{3,2},{4,5},{5,4},{6,7},{7,6},{8,9},{9,8},{10,11... | collective-permute-start | bytes 1572872 | tf_op jit(solution)/shard_map/ppermute | solution.py:365
  51.0 5.8 %collective-permute-start.13 = (bf16[4,128,128]{2,1,0:T(8,128)(2,1)S(1)}, bf16[4,128,128]{2,1,0:T(8,128)(2,1)S(1)}, u32[]{:S(2)}, u32[]{:S(2)}) collective-permute-start(bf16[4,128,128]{2,1,0:T(8,128)(2,1)S(1)} %get-tuple-element.47), channel_id=1, source_target_pairs={{0,8},{8,0},{16,24},{24,16},{1,9},{9,1},{17,25},{25,17},{2,10},{10... | collective-permute-start | bytes 393224 | tf_op jit(solution)/shard_map/ppermute | solution.py:356
  51.7 5.2 %copy-start.11 = (s32[16]{0:T(128)S(1)}, s32[16]{0:T(128)}, u32[]{:S(2)}) copy-start(s32[16]{0:T(128)} %get-tuple-element.29.turn_ref) | copy-start | bytes 196
  51.7 5.2 %collective-permute-start.14 = (bf16[4,128,128]{2,1,0:T(8,128)(2,1)S(1)}, bf16[4,128,128]{2,1,0:T(8,128)(2,1)S(1)}, u32[]{:S(2)}, u32[]{:S(2)}) collective-permute-start(bf16[4,128,128]{2,1,0:T(8,128)(2,1)S(1)} %get-tuple-element.50), channel_id=1, source_target_pairs={{0,16},{8,24},{16,0},{24,8},{1,17},{9,25},{17,1},{25,9},{2,18},{10... | collective-permute-start | bytes 393224 | tf_op jit(solution)/shard_map/ppermute | solution.py:359

commit v4 on v3

--- a/solution.py
+++ b/solution.py
@@ -290,12 +290,12 @@
         weight_ref[p : p + 1, :] = counts
         rows = slice(orbs + amp_ref.shape[1], held_ref.shape[2])
         held_ref[p // half, p % half, rows, :] = jnp.broadcast_to(counts, (16, pno)).astype(jnp.bfloat16)
-    for started in copies:
-        started.wait()
     stores = [
         pltpu.make_async_copy(held_ref.at[k], out_ref, sems.at[4 + k]) for k, out_ref in enumerate((low_ref, high_ref))
     ]
-    for store in stores:
+    for k, store in enumerate(stores):
+        for started in copies[2 * k : 2 * k + 2]:
+            started.wait()
         store.start()
 
     sides = 2 * pairs
@@ -381,7 +381,7 @@
         below, above = along_chips(slab, 1), along_chips(slab, -1)
         halves = half_products(uses, 0, [slab[None], below[None]], own_t, pno, None, DECLARED)
         beyond = along_chips(below, 1)
-        acc = after(acc, halves)
+        acc = after(acc, halves, above)
     else:
         gathered = lax.all_gather(slab, "dev", axis=0, tiled=False)
         halves = half_products(uses, 0, [gathered[:ahead]], own_t, pno, None, 0)
@@ -389,11 +389,12 @@
 
     lanes = [*range(pairs, pairs + half), *range(2 * pairs + half, 3 * pairs)]
     acc = add_coupled(lanes, weights, own_t, acc, (x_lo, y_hi), DECLARED)
-    first = across(first_across_kernel, "first_across", (), (after(x_lo, acc), after(y_hi, acc)), orbs, FIRST_COST)
-    back_low, back_high = along_x(first[0]), along_y(first[1])
-    gate = first[0]
     if around:
         swaps = [other_core(after(value, x_lo, y_hi)) for value in (slab, below)]
+    first = across(first_across_kernel, "first_across", (), (after(x_lo, acc, *swaps) if around else x_lo, after(y_hi, acc)), orbs, FIRST_COST)
+    gate = first[0]
+    back_low, back_high = along_x(first[0]), along_y(first[1])
+    if around:
         more = [value[None] for value in (*swaps, beyond, above)]
         halves = half_products(uses, 2, more, after(own_t, gate), pno, halves, 0)
         beyond, above = after(beyond, halves), after(above, halves)

time: 59.9 us -> 62.4 us (1.042)
  starting transfers between devices: 15.7 us -> 17.5 us
  local copies, waits for them, and re-layouts: 4.36 us -> 5.41 us
    ppermute x3, waiting for transfers between devices: 3.55 us -> 9.38 us  [along_chips(): lax.ppermute(value, 'dev', [(d, (d + 2 * step) % n_dev) for d in range(n_...]
    ppermute x4, waiting for transfers between devices: 5.66 us -> 0.01 us  [along_x(): return lax.ppermute(value, 'grp', [(g, g ^ 1) for g in range(n_grp)])]
    ppermute x3, starting transfers between devices: 5.11 us -> 6.18 us  [along_chips(): lax.ppermute(value, 'dev', [(d, (d + 2 * step) % n_dev) for d in range(n_...]
    unnamed x28 -> x34, local copies, waits for them, and re-layouts: 4.36 us -> 5.41 us
    ppermute x4, starting transfers between devices: 4.4 us -> 5.36 us  [along_x(): return lax.ppermute(value, 'grp', [(g, g ^ 1) for g in range(n_grp)])]
  transfers between devices with their start and end apart: 15 -> 15, of which waited for: 3 -> 2; matrix products, arithmetic and copies ran while one was open for 0% -> 0% of each run, Pallas kernels for 46% -> 43%
where the time goes in v4:
time: 62.4 us; the launch traced here: 61.9 us
  Pallas kernels  29.4 us (47%)
  starting transfers between devices  17.5 us (28%)
  waiting for transfers between devices  9.41 us (15%)
  local copies, waits for them, and re-layouts  5.41 us (9%)
    pallas_call x8, Pallas kernels, call_kernel(): pl.pallas_call(body, out_shape=out_shape, in_specs=[SMEM_SPEC] * len(smem...  25.7 us
    ppermute x3, waiting for transfers between devices, along_chips(): lax.ppermute(value, 'dev', [(d, (d + 2 * step) % n_dev) for d in range(n_...  9.38 us
    ppermute x3, starting transfers between devices, along_chips(): lax.ppermute(value, 'dev', [(d, (d + 2 * step) % n_dev) for d in range(n_...  6.18 us
    unnamed x34, local copies, waits for them, and re-layouts  5.41 us
    ppermute x4, starting transfers between devices, along_x(): return lax.ppermute(value, 'grp', [(g, g ^ 1) for g in range(n_grp)])  5.36 us
    ppermute x4, starting transfers between devices, along_y(): return lax.ppermute(value, 'grp', [(g, g ^ 2) for g in range(n_grp)])  4.89 us
    pallas_call x1, Pallas kernels, pack(): pl.pallas_call(functools.partial(pack_kernel, orbs / pno, chips), out_sha...  3.72 us
  transfers between devices with their start and end apart: 15, of which 2 were waited for; matrix products, arithmetic and copies ran while one was open for 0% of the time, Pallas kernels for 43%

profile of v4, /device:TPU:0, one launch (start us, length us, event | category | flops | bytes accessed | tf_op | source)
XLA Modules:
  0.0 61.9 jit_solution(16741874252532106741)
XLA Ops:
  0.0 3.0 %collective-permute-start = (bf16[512,512]{1,0:T(8,128)(2,1)}, bf16[512,512]{1,0:T(8,128)(2,1)}, u32[]{:S(2)}, u32[]{:S(2)}) collective-permute-start(bf16[512,512]{1,0:T(8,128)(2,1)} %bitcast.16), channel_id=1, source_target_pairs={{0,2},{1,3},{2,4},{3,5},{4,6},{5,7},{6,0},{7,1},{8,10},{9,11},{10,... | collective-permute-start | bytes 1572872 | tf_op jit(solution)/shard_map/ppermute | solution.py:362
  3.0 2.0 %collective-permute-start.6 = (bf16[512,512]{1,0:T(8,128)(2,1)}, bf16[512,512]{1,0:T(8,128)(2,1)}, u32[]{:S(2)}, u32[]{:S(2)}) collective-permute-start(bf16[512,512]{1,0:T(8,128)(2,1)} %bitcast.17), channel_id=1, source_target_pairs={{0,6},{1,7},{2,0},{3,1},{4,2},{5,3},{6,4},{7,5},{8,14},{9,15},{10,... | collective-permute-start | bytes 1572872 | tf_op jit(solution)/shard_map/ppermute | solution.py:362
  5.1 3.7 %pack.1 = (bf16[4,656,128]{2,1,0:T(8,128)(2,1)}, bf16[4,656,128]{2,1,0:T(8,128)(2,1)}, f32[8,128]{1,0:T(8,128)}, s32[8,2]{1,0:T(8,128)}, s32[16]{0:T(128)}) custom-call(s32[1]{0:T(128)} %bitcast.group_ref, s32[1]{0:T(128)} %bitcast.1.me_ref, s32[8,32]{1,0:T(8,128)} %coupled_ref.1, s32[8]{0:T(128)} %length_ref.1, s32[8]{0:T(128)} %owner_ref.1, ...), custom_call_target="tpu_custom_call" | custom-call | tf_op jit(solution)/shard_map/pack/pallas_call | solution.py:326
  8.8 1.8 %collective-permute-start.2 = (bf16[4,656,128]{2,1,0:T(8,128)(2,1)}, bf16[4,656,128]{2,1,0:T(8,128)(2,1)S(1)}, u32[]{:S(2)}, u32[]{:S(2)}) collective-permute-start(bf16[4,656,128]{2,1,0:T(8,128)(2,1)} %get-tuple-element.46.low_ref), channel_id=1, source_target_pairs={{0,8},{8,0},{16,24},{24,16},{1,9},{9,1},{17,25},{25,17},{2,10},{10... | collective-permute-start | bytes 2015240 | tf_op jit(solution)/shard_map/ppermute | solution.py:356
  10.6 1.5 %collective-permute-start.3 = (bf16[4,656,128]{2,1,0:T(8,128)(2,1)}, bf16[4,656,128]{2,1,0:T(8,128)(2,1)S(1)}, u32[]{:S(2)}, u32[]{:S(2)}) collective-permute-start(bf16[4,656,128]{2,1,0:T(8,128)(2,1)} %get-tuple-element.45.high_ref), channel_id=1, source_target_pairs={{0,16},{8,24},{16,0},{24,8},{1,17},{9,25},{17,1},{25,9},{2,18},{10... | collective-permute-start | bytes 2015240 | tf_op jit(solution)/shard_map/ppermute | solution.py:359
  12.1 0.5 collective-permute-start.9
  12.6 1.1 %copy-done.4 = bf16[4,656,128]{2,1,0:T(8,128)(2,1)S(1)} copy-done((bf16[4,656,128]{2,1,0:T(8,128)(2,1)S(1)}, bf16[4,656,128]{2,1,0:T(8,128)(2,1)}, u32[]{:S(2)}) %copy-start.4) | copy-done | bytes 671768
  13.7 0.7 %copy-done.11 = f32[8,128]{1,0:T(8,128)S(1)} copy-done((f32[8,128]{1,0:T(8,128)S(1)}, f32[8,128]{1,0:T(8,128)}, u32[]{:S(2)}) %copy-start.11) | copy-done | bytes 4120
  14.4 4.5 %own_coupled.1 = (f32[8,128,128]{2,1,0:T(8,128)S(1)}, bf16[1024,512]{1,0:T(8,128)(2,1)S(1)}) custom-call(f32[8,128]{1,0:T(8,128)S(1)} %copy-done.11, bf16[4,656,128]{2,1,0:T(8,128)(2,1)} %get-tuple-element.46.low_ref, bf16[4,656,128]{2,1,0:T(8,128)(2,1)S(1)} %copy-done.4), custom_call_target="tpu_custom_call" | custom-call | tf_op jit(solution)/shard_map/own_coupled/pallas_call | solution.py:24
  18.9 0.7 %copy-done.9 = s32[8,2]{1,0:T(8,128)S(1)} copy-done((s32[8,2]{1,0:T(8,128)S(1)}, s32[8,2]{1,0:T(8,128)}, u32[]{:S(2)}) %copy-start.9) | copy-done | bytes 88
  19.6 1.6 %halves.1.refs_5_ = bf16[17,512,128]{2,1,0:T(8,128)(2,1)S(1)} custom-call(s32[8,2]{1,0:T(8,128)S(1)} %copy-done.9, bf16[1,512,512]{2,1,0:T(8,128)(2,1)S(1)} %copy-done.14, bf16[1,512,512]{2,1,0:T(8,128)(2,1)} %bitcast.9.refs_1_, bf16[1024,512]{1,0:T(8,128)(2,1)S(1)} %get-tuple-element.41.refs_2_.left_ref.refs_4_), custom_call_target="tpu_custom_call" | custom-call | flops 20000000000 | tf_op jit(solution)/shard_map/halves/pallas_call | solution.py:24
  21.2 6.8 %collective-permute-done.6 = bf16[512,512]{1,0:T(8,128)(2,1)} collective-permute-done((bf16[512,512]{1,0:T(8,128)(2,1)}, bf16[512,512]{1,0:T(8,128)(2,1)}, u32[]{:S(2)}, u32[]{:S(2)}) %collective-permute-start.6) | collective-permute-done | bytes 524320 | tf_op jit(solution)/shard_map/ppermute | solution.py:362
  28.0 1.1 %collective-permute-start.1 = (bf16[512,512]{1,0:T(8,128)(2,1)}, bf16[512,512]{1,0:T(8,128)(2,1)}, u32[]{:S(2)}, u32[]{:S(2)}) collective-permute-start(bf16[512,512]{1,0:T(8,128)(2,1)} %collective-permute-done), channel_id=1, source_target_pairs={{0,2},{1,3},{2,4},{3,5},{4,6},{5,7},{6,0},{7,1},{8,10},{9,11},{10,... | collective-permute-start | bytes 1572872 | tf_op jit(solution)/shard_map/ppermute | solution.py:362
  29.1 1.5 %collective-permute-start.10 = (bf16[4,656,128]{2,1,0:T(8,128)(2,1)}, bf16[4,656,128]{2,1,0:T(8,128)(2,1)}, u32[]{:S(2)}, u32[]{:S(2)}) collective-permute-start(bf16[4,656,128]{2,1,0:T(8,128)(2,1)} %get-tuple-element.46.low_ref), channel_id=1, source_target_pairs={{0,16},{8,24},{16,0},{24,8},{1,17},{9,25},{17,1},{25,9},{2,18},{10... | collective-permute-start | bytes 2015240 | tf_op jit(solution)/shard_map/ppermute | solution.py:359
  30.6 0.0 collective-permute-done.3.two_ref.y_high
  30.6 0.5 collective-permute-start.5
  31.1 4.0 %coupled.2.acc_ref = f32[8,128,128]{2,1,0:T(8,128)S(1)} custom-call(f32[8,128]{1,0:T(8,128)S(1)} %copy-done.12, bf16[1024,512]{1,0:T(8,128)(2,1)S(1)} %get-tuple-element.41.refs_2_.left_ref.refs_4_, f32[8,128,128]{2,1,0:T(8,128)S(1)} %get-tuple-element.37.acc_ref, bf16[4,656,128]{2,1,0:T(8,128)(2,1)S(1)} %collective-permute-done.2.one_ref.x_low, ...), custom_call_target="tpu_custom_call" | custom-call | flops 20000000000 | tf_op jit(solution)/shard_map/coupled/pallas_call | solution.py:24
  35.1 0.8 %copy-done.15 = f32[8,128,128]{2,1,0:T(8,128)} copy-done((f32[8,128,128]{2,1,0:T(8,128)}, f32[8,128,128]{2,1,0:T(8,128)S(1)}, u32[]{:S(2)}) %copy-start.15) | copy-done | bytes 524312
  35.9 2.7 %first_across.1 = (bf16[4,128,128]{2,1,0:T(8,128)(2,1)S(1)}, bf16[4,128,128]{2,1,0:T(8,128)(2,1)}) custom-call(bf16[4,656,128]{2,1,0:T(8,128)(2,1)S(1)} %collective-permute-done.2.one_ref.x_low, bf16[4,656,128]{2,1,0:T(8,128)(2,1)S(1)} %collective-permute-done.3.two_ref.y_high), custom_call_target="tpu_custom_call" | custom-call | tf_op jit(solution)/shard_map/first_across/pallas_call | solution.py:24
  38.7 0.5 collective-permute-start.12
  39.2 1.5 %collective-permute-start.11 = (bf16[4,128,128]{2,1,0:T(8,128)(2,1)S(1)}, bf16[4,128,128]{2,1,0:T(8,128)(2,1)S(1)}, u32[]{:S(2)}, u32[]{:S(2)}) collective-permute-start(bf16[4,128,128]{2,1,0:T(8,128)(2,1)S(1)} %get-tuple-element.40), channel_id=1, source_target_pairs={{0,8},{8,0},{16,24},{24,16},{1,9},{9,1},{17,25},{25,17},{2,10},{10... | collective-permute-start | bytes 393224 | tf_op jit(solution)/shard_map/ppermute | solution.py:356
  40.7 2.6 %collective-permute-done.1 = bf16[512,512]{1,0:T(8,128)(2,1)} collective-permute-done((bf16[512,512]{1,0:T(8,128)(2,1)}, bf16[512,512]{1,0:T(8,128)(2,1)}, u32[]{:S(2)}, u32[]{:S(2)}) %collective-permute-start.1) | collective-permute-done | bytes 524320 | tf_op jit(solution)/shard_map/ppermute | solution.py:362
  43.3 1.0 %copy-done.6 = bf16[512,512]{1,0:T(8,128)(2,1)S(1)} copy-done((bf16[512,512]{1,0:T(8,128)(2,1)S(1)}, bf16[512,512]{1,0:T(8,128)(2,1)}, u32[]{:S(2)}) %copy-start.6) | copy-done | bytes 524312
  44.3 1.0 %copy-done.8 = bf16[512,512]{1,0:T(8,128)(2,1)S(1)} copy-done((bf16[512,512]{1,0:T(8,128)(2,1)S(1)}, bf16[512,512]{1,0:T(8,128)(2,1)}, u32[]{:S(2)}) %copy-start.8) | copy-done | bytes 524312
  45.4 2.1 %more_halves.1.refs_3_ = bf16[17,512,128]{2,1,0:T(8,128)(2,1)S(1)} custom-call(s32[8,2]{1,0:T(8,128)S(1)} %copy-done.10, bf16[1,512,512]{2,1,0:T(8,128)(2,1)S(1)} %bitcast.12, bf16[1,512,512]{2,1,0:T(8,128)(2,1)S(1)} %bitcast.13, bf16[1,512,512]{2,1,0:T(8,128)(2,1)} %bitcast.7.refs_2_, ...), custom_call_target="tpu_custom_call", output_to_operand_aliasing={{}: (6, {})} | custom-call | tf_op jit(solution)/shard_map/more_halves/pallas_call | solution.py:24
  47.5 0.1 collective-permute-start.7
  47.6 0.5 collective-permute-start.8
  48.1 3.6 %second_across.1 = (bf16[4,128,128]{2,1,0:T(8,128)(2,1)S(1)}, bf16[4,128,128]{2,1,0:T(8,128)(2,1)S(1)}) custom-call(s32[1]{0:T(128)} %bitcast.3.upper_ref, bf16[4,656,128]{2,1,0:T(8,128)(2,1)S(1)} %copy-done.1, bf16[4,656,128]{2,1,0:T(8,128)(2,1)} %collective-permute-done.9.x_high.one_ref, bf16[4,656,128]{2,1,0:T(8,128)(2,1)} %collective-permute-done.10.y_low.two_ref, ...), custom_call_target="tpu_custom_call" | custom-call | tf_op jit(solution)/shard_map/second_across/pallas_call | solution.py:24
  51.7 1.6 %collective-permute-start.13 = (bf16[4,128,128]{2,1,0:T(8,128)(2,1)S(1)}, bf16[4,128,128]{2,1,0:T(8,128)(2,1)S(1)}, u32[]{:S(2)}, u32[]{:S(2)}) collective-permute-start(bf16[4,128,128]{2,1,0:T(8,128)(2,1)S(1)} %get-tuple-element.47), channel_id=1, source_target_pairs={{0,8},{8,0},{16,24},{24,16},{1,9},{9,1},{17,25},{25,17},{2,10},{10... | collective-permute-start | bytes 393224 | tf_op jit(solution)/shard_map/ppermute | solution.py:356
  53.3 1.3 %collective-permute-start.14 = (bf16[4,128,128]{2,1,0:T(8,128)(2,1)S(1)}, bf16[4,128,128]{2,1,0:T(8,128)(2,1)S(1)}, u32[]{:S(2)}, u32[]{:S(2)}) collective-permute-start(bf16[4,128,128]{2,1,0:T(8,128)(2,1)S(1)} %get-tuple-element.50), channel_id=1, source_target_pairs={{0,16},{8,24},{16,0},{24,8},{1,17},{9,25},{17,1},{25,9},{2,18},{10... | collective-permute-start | bytes 393224 | tf_op jit(solution)/shard_map/ppermute | solution.py:359
  54.6 4.7 %coupled.3.refs_4_ = f32[8,128,128]{2,1,0:T(8,128)S(1)} custom-call(f32[8,128]{1,0:T(8,128)S(1)} %copy-done.12, bf16[1024,512]{1,0:T(8,128)(2,1)S(1)} %get-tuple-element.41.refs_2_.left_ref.refs_4_, f32[8,128,128]{2,1,0:T(8,128)S(1)} %copy-done.16, bf16[4,656,128]{2,1,0:T(8,128)(2,1)} %collective-permute-done.9.x_high.one_ref, ...), custom_call_target="tpu_custom_call" | custom-call | flops 20000000000 | tf_op jit(solution)/shard_map/coupled/pallas_call | solution.py:24
  59.4 2.6 %exchange.1 = f32[8,128,128]{2,1,0:T(8,128)} custom-call(s32[8,2]{1,0:T(8,128)S(1)} %copy-done.10, s32[16]{0:T(128)S(1)} %copy-done.13, s32[1]{0:T(128)} %bitcast.3.upper_ref, bf16[1,512,512]{2,1,0:T(8,128)(2,1)S(1)} %bitcast.14, bf16[1,512,512]{2,1,0:T(8,128)(2,1)S(1)} %bitcast.15, bf16[1024,512]{1,0:T(8,128)(2,1)S(1)} %get-tuple-element.41.refs_2_.left_ref.refs_4_, ...), custom_call_target="tpu_custom_call" | custom-call | tf_op jit(solution)/shard_map/exchange/pallas_call | solution.py:24
  (41 shorter events, 0.1 us)
Async XLA Ops:
  0.0 18.9 %collective-permute-start = (bf16[512,512]{1,0:T(8,128)(2,1)}, bf16[512,512]{1,0:T(8,128)(2,1)}, u32[]{:S(2)}, u32[]{:S(2)}) collective-permute-start(bf16[512,512]{1,0:T(8,128)(2,1)} %bitcast.16), channel_id=1, source_target_pairs={{0,2},{1,3},{2,4},{3,5},{4,6},{5,7},{6,0},{7,1},{8,10},{9,11},{10,... | collective-permute-start | bytes 1572872 | tf_op jit(solution)/shard_map/ppermute | solution.py:362
  3.0 24.9 %collective-permute-start.6 = (bf16[512,512]{1,0:T(8,128)(2,1)}, bf16[512,512]{1,0:T(8,128)(2,1)}, u32[]{:S(2)}, u32[]{:S(2)}) collective-permute-start(bf16[512,512]{1,0:T(8,128)(2,1)} %bitcast.17), channel_id=1, source_target_pairs={{0,6},{1,7},{2,0},{3,1},{4,2},{5,3},{6,4},{7,5},{8,14},{9,15},{10,... | collective-permute-start | bytes 1572872 | tf_op jit(solution)/shard_map/ppermute | solution.py:362
  5.1 13.9 %copy-start.14 = (bf16[1,512,512]{2,1,0:T(8,128)(2,1)S(1)}, bf16[1,512,512]{2,1,0:T(8,128)(2,1)}, u32[]{:S(2)}) copy-start(bf16[1,512,512]{2,1,0:T(8,128)(2,1)} %refs_0_.1) | copy-start | bytes 1572868
  8.8 20.3 %collective-permute-start.2 = (bf16[4,656,128]{2,1,0:T(8,128)(2,1)}, bf16[4,656,128]{2,1,0:T(8,128)(2,1)S(1)}, u32[]{:S(2)}, u32[]{:S(2)}) collective-permute-start(bf16[4,656,128]{2,1,0:T(8,128)(2,1)} %get-tuple-element.46.low_ref), channel_id=1, source_target_pairs={{0,8},{8,0},{16,24},{24,16},{1,9},{9,1},{17,25},{25,17},{2,10},{10... | collective-permute-start | bytes 2015240 | tf_op jit(solution)/shard_map/ppermute | solution.py:356
  10.6 20.1 %collective-permute-start.3 = (bf16[4,656,128]{2,1,0:T(8,128)(2,1)}, bf16[4,656,128]{2,1,0:T(8,128)(2,1)S(1)}, u32[]{:S(2)}, u32[]{:S(2)}) collective-permute-start(bf16[4,656,128]{2,1,0:T(8,128)(2,1)} %get-tuple-element.45.high_ref), channel_id=1, source_target_pairs={{0,16},{8,24},{16,0},{24,8},{1,17},{9,25},{17,1},{25,9},{2,18},{10... | collective-permute-start | bytes 2015240 | tf_op jit(solution)/shard_map/ppermute | solution.py:359
  12.1 35.5 %collective-permute-start.9 = (bf16[4,656,128]{2,1,0:T(8,128)(2,1)}, bf16[4,656,128]{2,1,0:T(8,128)(2,1)}, u32[]{:S(2)}, u32[]{:S(2)}) collective-permute-start(bf16[4,656,128]{2,1,0:T(8,128)(2,1)} %get-tuple-element.45.high_ref), channel_id=1, source_target_pairs={{0,8},{8,0},{16,24},{24,16},{1,9},{9,1},{17,25},{25,17},{2,10},{10... | collective-permute-start | bytes 2015240 | tf_op jit(solution)/shard_map/ppermute | solution.py:356
  12.6 1.1 %copy-start.4 = (bf16[4,656,128]{2,1,0:T(8,128)(2,1)S(1)}, bf16[4,656,128]{2,1,0:T(8,128)(2,1)}, u32[]{:S(2)}) copy-start(bf16[4,656,128]{2,1,0:T(8,128)(2,1)} %get-tuple-element.45.high_ref) | copy-start | bytes 2015236
  13.7 0.7 %copy-start.11 = (f32[8,128]{1,0:T(8,128)S(1)}, f32[8,128]{1,0:T(8,128)}, u32[]{:S(2)}) copy-start(f32[8,128]{1,0:T(8,128)} %get-tuple-element.34.weight_ref) | copy-start | bytes 12292
  18.9 0.7 %copy-start.9 = (s32[8,2]{1,0:T(8,128)S(1)}, s32[8,2]{1,0:T(8,128)}, u32[]{:S(2)}) copy-start(s32[8,2]{1,0:T(8,128)} %get-tuple-element.28.uses_ref) | copy-start | bytes 196
  19.6 11.5 %copy-start.12 = (f32[8,128]{1,0:T(8,128)S(1)}, f32[8,128]{1,0:T(8,128)}, u32[]{:S(2)}) copy-start(f32[8,128]{1,0:T(8,128)} %get-tuple-element.34.weight_ref) | copy-start | bytes 12292
  28.0 15.3 %copy-start.10 = (s32[8,2]{1,0:T(8,128)S(1)}, s32[8,2]{1,0:T(8,128)}, u32[]{:S(2)}) copy-start(s32[8,2]{1,0:T(8,128)} %get-tuple-element.28.uses_ref) | copy-start | bytes 196
  28.0 15.3 %collective-permute-start.1 = (bf16[512,512]{1,0:T(8,128)(2,1)}, bf16[512,512]{1,0:T(8,128)(2,1)}, u32[]{:S(2)}, u32[]{:S(2)}) collective-permute-start(bf16[512,512]{1,0:T(8,128)(2,1)} %collective-permute-done), channel_id=1, source_target_pairs={{0,2},{1,3},{2,4},{3,5},{4,6},{5,7},{6,0},{7,1},{8,10},{9,11},{10,... | collective-permute-start | bytes 1572872 | tf_op jit(solution)/shard_map/ppermute | solution.py:362
  29.1 6.8 %copy-start = (bf16[4,656,128]{2,1,0:T(8,128)(2,1)}, bf16[4,656,128]{2,1,0:T(8,128)(2,1)S(1)}, u32[]{:S(2)}) copy-start(bf16[4,656,128]{2,1,0:T(8,128)(2,1)S(1)} %collective-permute-done.2.one_ref.x_low) | copy-start | bytes 2015236
  29.1 19.0 %collective-permute-start.10 = (bf16[4,656,128]{2,1,0:T(8,128)(2,1)}, bf16[4,656,128]{2,1,0:T(8,128)(2,1)}, u32[]{:S(2)}, u32[]{:S(2)}) collective-permute-start(bf16[4,656,128]{2,1,0:T(8,128)(2,1)} %get-tuple-element.46.low_ref), channel_id=1, source_target_pairs={{0,16},{8,24},{16,0},{24,8},{1,17},{9,25},{17,1},{25,9},{2,18},{10... | collective-permute-start | bytes 2015240 | tf_op jit(solution)/shard_map/ppermute | solution.py:359
  30.6 5.3 %copy-start.2 = (bf16[4,656,128]{2,1,0:T(8,128)(2,1)}, bf16[4,656,128]{2,1,0:T(8,128)(2,1)S(1)}, u32[]{:S(2)}) copy-start(bf16[4,656,128]{2,1,0:T(8,128)(2,1)S(1)} %collective-permute-done.3.two_ref.y_high) | copy-start | bytes 2015236
  30.6 5.3 %collective-permute-start.4 = (bf16[512,512]{1,0:T(8,128)(2,1)S(1)}, bf16[512,512]{1,0:T(8,128)(2,1)S(1)}, u32[]{:S(2)}, u32[]{:S(2)}) collective-permute-start(bf16[512,512]{1,0:T(8,128)(2,1)S(1)} %bitcast.18), channel_id=1, source_target_pairs={{0,1},{1,0},{2,3},{3,2},{4,5},{5,4},{6,7},{7,6},{8,9},{9,8},{10,11... | collective-permute-start | bytes 1572872 | tf_op jit(solution)/shard_map/ppermute | solution.py:365
  30.6 5.3 %collective-permute-start.5 = (bf16[512,512]{1,0:T(8,128)(2,1)}, bf16[512,512]{1,0:T(8,128)(2,1)S(1)}, u32[]{:S(2)}, u32[]{:S(2)}) collective-permute-start(bf16[512,512]{1,0:T(8,128)(2,1)} %collective-permute-done), channel_id=1, source_target_pairs={{0,1},{1,0},{2,3},{3,2},{4,5},{5,4},{6,7},{7,6},{8,9},{9,8},{10,11... | collective-permute-start | bytes 1572872 | tf_op jit(solution)/shard_map/ppermute | solution.py:365
  35.1 0.8 %copy-start.15 = (f32[8,128,128]{2,1,0:T(8,128)}, f32[8,128,128]{2,1,0:T(8,128)S(1)}, u32[]{:S(2)}) copy-start(f32[8,128,128]{2,1,0:T(8,128)S(1)} %coupled.2.acc_ref) | copy-start | bytes 1572868
  35.9 2.8 %copy-start.5 = (bf16[512,512]{1,0:T(8,128)(2,1)}, bf16[512,512]{1,0:T(8,128)(2,1)S(1)}, u32[]{:S(2)}) copy-start(bf16[512,512]{1,0:T(8,128)(2,1)S(1)} %collective-permute-done.4) | copy-start | bytes 1572868
  35.9 2.8 %copy-start.7 = (bf16[512,512]{1,0:T(8,128)(2,1)}, bf16[512,512]{1,0:T(8,128)(2,1)S(1)}, u32[]{:S(2)}) copy-start(bf16[512,512]{1,0:T(8,128)(2,1)S(1)} %collective-permute-done.5) | copy-start | bytes 1572868
  38.7 14.6 %collective-permute-start.12 = (bf16[4,128,128]{2,1,0:T(8,128)(2,1)}, bf16[4,128,128]{2,1,0:T(8,128)(2,1)S(1)}, u32[]{:S(2)}, u32[]{:S(2)}) collective-permute-start(bf16[4,128,128]{2,1,0:T(8,128)(2,1)} %get-tuple-element.49), channel_id=1, source_target_pairs={{0,16},{8,24},{16,0},{24,8},{1,17},{9,25},{17,1},{25,9},{2,18},{10... | collective-permute-start | bytes 393224 | tf_op jit(solution)/shard_map/ppermute | solution.py:359
  39.2 20.1 %collective-permute-start.11 = (bf16[4,128,128]{2,1,0:T(8,128)(2,1)S(1)}, bf16[4,128,128]{2,1,0:T(8,128)(2,1)S(1)}, u32[]{:S(2)}, u32[]{:S(2)}) collective-permute-start(bf16[4,128,128]{2,1,0:T(8,128)(2,1)S(1)} %get-tuple-element.40), channel_id=1, source_target_pairs={{0,8},{8,0},{16,24},{24,16},{1,9},{9,1},{17,25},{25,17},{2,10},{10... | collective-permute-start | bytes 393224 | tf_op jit(solution)/shard_map/ppermute | solution.py:356
  43.3 1.0 %copy-start.6 = (bf16[512,512]{1,0:T(8,128)(2,1)S(1)}, bf16[512,512]{1,0:T(8,128)(2,1)}, u32[]{:S(2)}) copy-start(bf16[512,512]{1,0:T(8,128)(2,1)} %copy-done.5) | copy-start | bytes 1572868
  44.3 1.0 %copy-start.8 = (bf16[512,512]{1,0:T(8,128)(2,1)S(1)}, bf16[512,512]{1,0:T(8,128)(2,1)}, u32[]{:S(2)}) copy-start(bf16[512,512]{1,0:T(8,128)(2,1)} %copy-done.7) | copy-start | bytes 1572868
  45.4 2.7 %copy-start.1 = (bf16[4,656,128]{2,1,0:T(8,128)(2,1)S(1)}, bf16[4,656,128]{2,1,0:T(8,128)(2,1)}, u32[]{:S(2)}) copy-start(bf16[4,656,128]{2,1,0:T(8,128)(2,1)} %copy-done) | copy-start | bytes 2015236
  45.4 2.7 %copy-start.3 = (bf16[4,656,128]{2,1,0:T(8,128)(2,1)S(1)}, bf16[4,656,128]{2,1,0:T(8,128)(2,1)}, u32[]{:S(2)}) copy-start(bf16[4,656,128]{2,1,0:T(8,128)(2,1)} %copy-done.2) | copy-start | bytes 2015236
  47.5 7.1 %copy-start.16 = (f32[8,128,128]{2,1,0:T(8,128)S(1)}, f32[8,128,128]{2,1,0:T(8,128)}, u32[]{:S(2)}) copy-start(f32[8,128,128]{2,1,0:T(8,128)} %copy-done.15) | copy-start | bytes 1572868
  47.5 11.8 %collective-permute-start.7 = (bf16[512,512]{1,0:T(8,128)(2,1)}, bf16[512,512]{1,0:T(8,128)(2,1)S(1)}, u32[]{:S(2)}, u32[]{:S(2)}) collective-permute-start(bf16[512,512]{1,0:T(8,128)(2,1)} %collective-permute-done.1), channel_id=1, source_target_pairs={{0,1},{1,0},{2,3},{3,2},{4,5},{5,4},{6,7},{7,6},{8,9},{9,8},{10,11... | collective-permute-start | bytes 1572872 | tf_op jit(solution)/shard_map/ppermute | solution.py:365
  47.6 11.7 %collective-permute-start.8 = (bf16[512,512]{1,0:T(8,128)(2,1)}, bf16[512,512]{1,0:T(8,128)(2,1)S(1)}, u32[]{:S(2)}, u32[]{:S(2)}) collective-permute-start(bf16[512,512]{1,0:T(8,128)(2,1)} %collective-permute-done.6), channel_id=1, source_target_pairs={{0,1},{1,0},{2,3},{3,2},{4,5},{5,4},{6,7},{7,6},{8,9},{9,8},{10,11... | collective-permute-start | bytes 1572872 | tf_op jit(solution)/shard_map/ppermute | solution.py:365
  51.7 7.6 %collective-permute-start.13 = (bf16[4,128,128]{2,1,0:T(8,128)(2,1)S(1)}, bf16[4,128,128]{2,1,0:T(8,128)(2,1)S(1)}, u32[]{:S(2)}, u32[]{:S(2)}) collective-permute-start(bf16[4,128,128]{2,1,0:T(8,128)(2,1)S(1)} %get-tuple-element.47), channel_id=1, source_target_pairs={{0,8},{8,0},{16,24},{24,16},{1,9},{9,1},{17,25},{25,17},{2,10},{10... | collective-permute-start | bytes 393224 | tf_op jit(solution)/shard_map/ppermute | solution.py:356
  53.3 6.1 %copy-start.13 = (s32[16]{0:T(128)S(1)}, s32[16]{0:T(128)}, u32[]{:S(2)}) copy-start(s32[16]{0:T(128)} %get-tuple-element.29.turn_ref) | copy-start | bytes 196
  53.3 6.0 %collective-permute-start.14 = (bf16[4,128,128]{2,1,0:T(8,128)(2,1)S(1)}, bf16[4,128,128]{2,1,0:T(8,128)(2,1)S(1)}, u32[]{:S(2)}, u32[]{:S(2)}) collective-permute-start(bf16[4,128,128]{2,1,0:T(8,128)(2,1)S(1)} %get-tuple-element.50), channel_id=1, source_target_pairs={{0,16},{8,24},{16,0},{24,8},{1,17},{9,25},{17,1},{25,9},{2,18},{10... | collective-permute-start | bytes 393224 | tf_op jit(solution)/shard_map/ppermute | solution.py:359

commit v5 on v3

--- a/solution.py
+++ b/solution.py
@@ -13,6 +13,7 @@
 RING_CHIPS = 4
 DECLARED = 20_000_000_000
 OWN_COST, FIRST_COST, SECOND_COST, LAST_COST = 0, 0, 0, DECLARED
+MORE_COST, EXCHANGE_COST = 0, 0
 SMEM_SPEC = pl.BlockSpec(memory_space=pltpu.SMEM)
 VMEM_SPEC = pl.BlockSpec(memory_space=pltpu.VMEM)
 HBM_SPEC = pl.BlockSpec(memory_space=pltpu.HBM)
@@ -221,9 +222,8 @@
     halves_kernel(base, uses_ref, *slab_refs, own_ref, half_ref)
 
 
-def exchange_kernel(scale, base, uses_ref, turn_ref, upper_ref, *refs):
-    *slab_refs, own_ref, early_ref, acc_ref, low_ref, high_ref, row_ref, column_ref, out_ref, late_ref = refs
-    half_count = low_ref.shape[0]
+def exchange_kernel(scale, base, uses_ref, turn_ref, *refs):
+    *slab_refs, own_ref, early_ref, acc_ref, out_ref, late_ref = refs
 
     def store(k, use, side, half):
         late_ref[2 * (k - base) + use] = half
@@ -236,10 +236,16 @@
     half_transforms(uses_ref, slab_refs, own_ref, store, base, out_ref.shape[1])
     for p in range(out_ref.shape[0]):
         product = lax.dot_general(half(p, 0), half(p, 1), (((0,), (0,)), ((), ())), preferred_element_type=jnp.float32)
-        k, upper = p % half_count, p // half_count
+        out_ref[p] = acc_ref[p] + product * scale
+
+
+def finish_kernel(upper_ref, acc_ref, low_ref, high_ref, row_ref, column_ref, out_ref):
+    half = low_ref.shape[0]
+    for p in range(out_ref.shape[0]):
+        k, upper = p % half, p // half
         first = (low_ref, high_ref)[upper][k].astype(jnp.float32)
         second = jnp.where(upper_ref[0] == upper, row_ref[k], column_ref[k]).astype(jnp.float32)
-        out_ref[p] = acc_ref[p] + (first + second) + product * scale
+        out_ref[p] = acc_ref[p] + (first + second)
 
 
 def half_products(uses, base, slabs, own_t, pno, done, flops):
@@ -253,16 +259,21 @@
     )
 
 
-def add_exchange(uses, turn, upper, base, slabs, own_t, early, sums):
+def add_exchange(uses, turn, base, slabs, own_t, early, acc):
     return call_kernel(
         functools.partial(exchange_kernel, 1.0 / math.sqrt(slabs[0].shape[1]), base),
-        jax.ShapeDtypeStruct(sums[0].shape, jnp.float32),
+        jax.ShapeDtypeStruct(acc.shape, jnp.float32),
         [pltpu.VMEM((2 * sum(slab.shape[0] for slab in slabs),) + early.shape[1:], jnp.bfloat16)],
         "exchange",
-        (uses, turn, upper),
-        (*slabs, own_t, early, *sums),
-        0,
-    )
+        (uses, turn),
+        (*slabs, own_t, early, acc),
+        EXCHANGE_COST,
+    )
+
+
+def finish(upper, acc, backs):
+    shape = jax.ShapeDtypeStruct(acc.shape, jnp.float32)
+    return call_kernel(finish_kernel, shape, [], "finish", (upper,), (acc, *backs), 0)
 
 
 def pack_kernel(scale, chips, group_ref, me_ref, coupled_ref, length_ref, owner_ref, orbs_ref, base_ref, amp_ref, *refs):
@@ -312,7 +323,8 @@
         if chips <= RING_CHIPS:
             steps = lax.rem((me >> 1) - (position >> 1) + chips, chips)
             swapped = (position ^ me) & 1
-            k = jnp.where(steps < 2, steps + 2 * swapped, steps + 2 + 2 * swapped)
+            late = jnp.where(steps == 2, 5 + swapped, 4 + 3 * swapped)
+            k = jnp.where(steps < 2, steps + 2 * swapped, late)
         turn_ref[f] = k
         uses_ref[k, 1] = uses_ref[k, 0]
         uses_ref[k, 0] = f
@@ -375,7 +387,7 @@
 
     slab = integral_slabs[0]
     around = chips <= RING_CHIPS
-    ahead = 6 if around else n_dev // 2
+    ahead = 5 if around else n_dev // 2
     acc, own_t = own_coupled(weights, own, orbs, OWN_COST)
     if around:
         below, above = along_chips(slab, 1), along_chips(slab, -1)
@@ -391,22 +403,20 @@
     acc = add_coupled(lanes, weights, own_t, acc, (x_lo, y_hi), DECLARED)
     first = across(first_across_kernel, "first_across", (), (after(x_lo, acc), after(y_hi, acc)), orbs, FIRST_COST)
     back_low, back_high = along_x(first[0]), along_y(first[1])
-    gate = first[0]
     if around:
         swaps = [other_core(after(value, x_lo, y_hi)) for value in (slab, below)]
-        more = [value[None] for value in (*swaps, beyond, above)]
-        halves = half_products(uses, 2, more, after(own_t, gate), pno, halves, 0)
-        beyond, above = after(beyond, halves), after(above, halves)
-        rest = [other_core(beyond)[None], other_core(above)[None]]
-        gate = halves
+        more = [value[None] for value in (*swaps, above)]
+        halves = half_products(uses, 2, more, after(own_t, first[0]), pno, halves, MORE_COST)
+        beyond = after(beyond, halves)
+        rest = [value[None] for value in (beyond, other_core(beyond), other_core(above))]
+    acc = add_exchange(uses, turns, ahead, rest, own_t, halves, acc)
     second = across(
-        second_across_kernel, "second_across", (upper,), (after(x_lo, gate), x_hi, y_lo, y_hi), orbs, SECOND_COST
+        second_across_kernel, "second_across", (upper,), (after(x_lo, acc), x_hi, y_lo, y_hi), orbs, SECOND_COST
     )
     back_row, back_column = along_x(second[0]), along_y(second[1])
     lanes = [*range(pairs + half, 2 * pairs), *range(2 * pairs, 2 * pairs + half)]
     acc = add_coupled(lanes, weights, own_t, after(acc, second[0]), (x_hi, y_lo), LAST_COST)
-    sums = (acc, back_low, back_high, back_row, back_column)
-    return add_exchange(uses, turns, upper, ahead, rest, own_t, halves, sums)
+    return finish(upper, acc, (back_low, back_high, back_row, back_column))
 
 
 def solution(mesh):

time: 59.9 us -> 59.6 us (level)
  starting transfers between devices: 15.7 us -> 17.4 us
  waiting for transfers between devices: 9.43 us -> 8.09 us
  local copies, waits for them, and re-layouts: 4.36 us -> 3.57 us
    ppermute x3, waiting for transfers between devices: 3.55 us -> 2.26 us  [along_chips(): lax.ppermute(value, 'dev', [(d, (d + 2 * step) % n_dev) for d in range(n_...]
    ppermute x4, starting transfers between devices: 5.12 us -> 6.33 us  [along_y(): return lax.ppermute(value, 'grp', [(g, g ^ 2) for g in range(n_grp)])]
    ppermute x4, starting transfers between devices: 4.4 us -> 5.31 us  [along_x(): return lax.ppermute(value, 'grp', [(g, g ^ 1) for g in range(n_grp)])]
    unnamed x28 -> x26, local copies, waits for them, and re-layouts: 4.36 us -> 3.57 us
    pallas_call x8 -> x9, Pallas kernels: 26 us -> 25.6 us  [call_kernel(): pl.pallas_call(body, out_shape=out_shape, in_specs=[SMEM_SPEC] * len(smem...]
  transfers between devices with their start and end apart: 15 -> 15, of which waited for: 3 -> 3; matrix products, arithmetic and copies ran while one was open for 0% -> 0% of each run, Pallas kernels for 46% -> 49%
where the time goes in v5:
time: 59.6 us; the launch traced here: 58.8 us
  Pallas kernels  29.5 us (49%)
  starting transfers between devices  17.4 us (29%)
  waiting for transfers between devices  8.09 us (14%)
  local copies, waits for them, and re-layouts  3.57 us (6%)
    pallas_call x9, Pallas kernels, call_kernel(): pl.pallas_call(body, out_shape=out_shape, in_specs=[SMEM_SPEC] * len(smem...  25.6 us
    ppermute x4, starting transfers between devices, along_y(): return lax.ppermute(value, 'grp', [(g, g ^ 2) for g in range(n_grp)])  6.33 us
    ppermute x4, waiting for transfers between devices, along_x(): return lax.ppermute(value, 'grp', [(g, g ^ 1) for g in range(n_grp)])  5.81 us
    ppermute x4, starting transfers between devices, along_x(): return lax.ppermute(value, 'grp', [(g, g ^ 1) for g in range(n_grp)])  5.31 us
    ppermute x3, starting transfers between devices, along_chips(): lax.ppermute(value, 'dev', [(d, (d + 2 * step) % n_dev) for d in range(n_...  5.11 us
    pallas_call x1, Pallas kernels, pack(): pl.pallas_call(functools.partial(pack_kernel, orbs / pno, chips), out_sha...  3.92 us
    unnamed x26, local copies, waits for them, and re-layouts  3.57 us
    ppermute x3, waiting for transfers between devices, along_chips(): lax.ppermute(value, 'dev', [(d, (d + 2 * step) % n_dev) for d in range(n_...  2.26 us
  transfers between devices with their start and end apart: 15, of which 3 were waited for; matrix products, arithmetic and copies ran while one was open for 0% of the time, Pallas kernels for 49%

profile of v5, /device:TPU:0, one launch (start us, length us, event | category | flops | bytes accessed | tf_op | source)
XLA Modules:
  0.0 58.8 jit_solution(17272145600978637826)
XLA Ops:
  0.0 3.0 %collective-permute-start = (bf16[512,512]{1,0:T(8,128)(2,1)}, bf16[512,512]{1,0:T(8,128)(2,1)}, u32[]{:S(2)}, u32[]{:S(2)}) collective-permute-start(bf16[512,512]{1,0:T(8,128)(2,1)} %bitcast.14), channel_id=1, source_target_pairs={{0,2},{1,3},{2,4},{3,5},{4,6},{5,7},{6,0},{7,1},{8,10},{9,11},{10,... | collective-permute-start | bytes 1572872 | tf_op jit(solution)/shard_map/ppermute | solution.py:374
  3.0 2.0 %collective-permute-start.6 = (bf16[512,512]{1,0:T(8,128)(2,1)}, bf16[512,512]{1,0:T(8,128)(2,1)}, u32[]{:S(2)}, u32[]{:S(2)}) collective-permute-start(bf16[512,512]{1,0:T(8,128)(2,1)} %bitcast.15), channel_id=1, source_target_pairs={{0,6},{1,7},{2,0},{3,1},{4,2},{5,3},{6,4},{7,5},{8,14},{9,15},{10,... | collective-permute-start | bytes 1572872 | tf_op jit(solution)/shard_map/ppermute | solution.py:374
  5.1 3.9 %pack.1 = (bf16[4,656,128]{2,1,0:T(8,128)(2,1)}, bf16[4,656,128]{2,1,0:T(8,128)(2,1)}, f32[8,128]{1,0:T(8,128)}, s32[8,2]{1,0:T(8,128)}, s32[16]{0:T(128)}) custom-call(s32[1]{0:T(128)} %bitcast.1.group_ref, s32[1]{0:T(128)} %bitcast.2.me_ref, s32[8,32]{1,0:T(8,128)} %coupled_ref.1, s32[8]{0:T(128)} %length_ref.1, s32[8]{0:T(128)} %owner_ref.1, ...), custom_call_target="tpu_custom_call" | custom-call | tf_op jit(solution)/shard_map/pack/pallas_call | solution.py:338
  9.0 1.8 %collective-permute-start.2 = (bf16[4,656,128]{2,1,0:T(8,128)(2,1)}, bf16[4,656,128]{2,1,0:T(8,128)(2,1)S(1)}, u32[]{:S(2)}, u32[]{:S(2)}) collective-permute-start(bf16[4,656,128]{2,1,0:T(8,128)(2,1)} %get-tuple-element.44.low_ref), channel_id=1, source_target_pairs={{0,8},{8,0},{16,24},{24,16},{1,9},{9,1},{17,25},{25,17},{2,10},{10... | collective-permute-start | bytes 2015240 | tf_op jit(solution)/shard_map/ppermute | solution.py:368
  10.8 1.5 %collective-permute-start.3 = (bf16[4,656,128]{2,1,0:T(8,128)(2,1)}, bf16[4,656,128]{2,1,0:T(8,128)(2,1)S(1)}, u32[]{:S(2)}, u32[]{:S(2)}) collective-permute-start(bf16[4,656,128]{2,1,0:T(8,128)(2,1)} %get-tuple-element.43.high_ref), channel_id=1, source_target_pairs={{0,16},{8,24},{16,0},{24,8},{1,17},{9,25},{17,1},{25,9},{2,18},{10... | collective-permute-start | bytes 2015240 | tf_op jit(solution)/shard_map/ppermute | solution.py:371
  12.3 0.5 collective-permute-start.9
  12.8 1.1 %copy-done.4 = bf16[4,656,128]{2,1,0:T(8,128)(2,1)S(1)} copy-done((bf16[4,656,128]{2,1,0:T(8,128)(2,1)S(1)}, bf16[4,656,128]{2,1,0:T(8,128)(2,1)}, u32[]{:S(2)}) %copy-start.4) | copy-done | bytes 671768
  13.9 0.7 %copy-done.9 = f32[8,128]{1,0:T(8,128)S(1)} copy-done((f32[8,128]{1,0:T(8,128)S(1)}, f32[8,128]{1,0:T(8,128)}, u32[]{:S(2)}) %copy-start.9) | copy-done | bytes 4120
  14.6 4.5 %own_coupled.1 = (f32[8,128,128]{2,1,0:T(8,128)S(1)}, bf16[1024,512]{1,0:T(8,128)(2,1)S(1)}) custom-call(f32[8,128]{1,0:T(8,128)S(1)} %copy-done.9, bf16[4,656,128]{2,1,0:T(8,128)(2,1)} %get-tuple-element.44.low_ref, bf16[4,656,128]{2,1,0:T(8,128)(2,1)S(1)} %copy-done.4), custom_call_target="tpu_custom_call" | custom-call | tf_op jit(solution)/shard_map/own_coupled/pallas_call | solution.py:25
  19.1 0.7 %copy-done.7 = s32[8,2]{1,0:T(8,128)S(1)} copy-done((s32[8,2]{1,0:T(8,128)S(1)}, s32[8,2]{1,0:T(8,128)}, u32[]{:S(2)}) %copy-start.7) | copy-done | bytes 88
  19.8 1.6 %halves.1.refs_4_ = bf16[17,512,128]{2,1,0:T(8,128)(2,1)S(1)} custom-call(s32[8,2]{1,0:T(8,128)S(1)} %copy-done.7, bf16[1,512,512]{2,1,0:T(8,128)(2,1)S(1)} %copy-done.12, bf16[1,512,512]{2,1,0:T(8,128)(2,1)} %bitcast.8.refs_1_, bf16[1024,512]{1,0:T(8,128)(2,1)S(1)} %get-tuple-element.40.refs_2_.left_ref.refs_3_), custom_call_target="tpu_custom_call" | custom-call | flops 20000000000 | tf_op jit(solution)/shard_map/halves/pallas_call | solution.py:25
  21.4 0.1 collective-permute-start.1
  21.5 5.8 %collective-permute-done.2.one_ref.x_low = bf16[4,656,128]{2,1,0:T(8,128)(2,1)S(1)} collective-permute-done((bf16[4,656,128]{2,1,0:T(8,128)(2,1)}, bf16[4,656,128]{2,1,0:T(8,128)(2,1)S(1)}, u32[]{:S(2)}, u32[]{:S(2)}) %collective-permute-start.2) | collective-permute-done | bytes 671776 | tf_op jit(solution)/shard_map/ppermute | solution.py:368
  27.3 0.1 collective-permute-start.4
  27.3 0.5 collective-permute-start.5
  27.8 0.3 collective-permute-done.6
  28.2 1.8 %collective-permute-start.10 = (bf16[4,656,128]{2,1,0:T(8,128)(2,1)}, bf16[4,656,128]{2,1,0:T(8,128)(2,1)}, u32[]{:S(2)}, u32[]{:S(2)}) collective-permute-start(bf16[4,656,128]{2,1,0:T(8,128)(2,1)} %get-tuple-element.44.low_ref), channel_id=1, source_target_pairs={{0,16},{8,24},{16,0},{24,8},{1,17},{9,25},{17,1},{25,9},{2,18},{10... | collective-permute-start | bytes 2015240 | tf_op jit(solution)/shard_map/ppermute | solution.py:371
  29.9 4.0 %coupled.2.refs_5_ = f32[8,128,128]{2,1,0:T(8,128)S(1)} custom-call(f32[8,128]{1,0:T(8,128)S(1)} %copy-done.10, bf16[1024,512]{1,0:T(8,128)(2,1)S(1)} %get-tuple-element.40.refs_2_.left_ref.refs_3_, f32[8,128,128]{2,1,0:T(8,128)S(1)} %get-tuple-element.36.acc_ref, bf16[4,656,128]{2,1,0:T(8,128)(2,1)S(1)} %collective-permute-done.2.one_ref.x_low, ...), custom_call_target="tpu_custom_call" | custom-call | flops 20000000000 | tf_op jit(solution)/shard_map/coupled/pallas_call | solution.py:25
  33.9 0.0 copy-start.5
  33.9 2.1 %first_across.1 = (bf16[4,128,128]{2,1,0:T(8,128)(2,1)S(1)}, bf16[4,128,128]{2,1,0:T(8,128)(2,1)S(1)}) custom-call(bf16[4,656,128]{2,1,0:T(8,128)(2,1)S(1)} %collective-permute-done.2.one_ref.x_low, bf16[4,656,128]{2,1,0:T(8,128)(2,1)S(1)} %collective-permute-done.3.two_ref.y_high), custom_call_target="tpu_custom_call" | custom-call | tf_op jit(solution)/shard_map/first_across/pallas_call | solution.py:25
  36.0 0.1 collective-permute-start.8
  36.2 1.7 %more_halves.1.refs_4_ = bf16[17,512,128]{2,1,0:T(8,128)(2,1)S(1)} custom-call(s32[8,2]{1,0:T(8,128)S(1)} %copy-done.8, bf16[1,512,512]{2,1,0:T(8,128)(2,1)S(1)} %bitcast.12, bf16[1,512,512]{2,1,0:T(8,128)(2,1)S(1)} %bitcast.13, bf16[1,512,512]{2,1,0:T(8,128)(2,1)} %bitcast.7.refs_2_, ...), custom_call_target="tpu_custom_call", output_to_operand_aliasing={{}: (5, {})} | custom-call | tf_op jit(solution)/shard_map/more_halves/pallas_call | solution.py:25
  37.9 1.9 %collective-permute-done.1 = bf16[512,512]{1,0:T(8,128)(2,1)} collective-permute-done((bf16[512,512]{1,0:T(8,128)(2,1)}, bf16[512,512]{1,0:T(8,128)(2,1)}, u32[]{:S(2)}, u32[]{:S(2)}) %collective-permute-start.1) | collective-permute-done | bytes 524320 | tf_op jit(solution)/shard_map/ppermute | solution.py:374
  39.8 1.5 %collective-permute-start.11 = (bf16[4,128,128]{2,1,0:T(8,128)(2,1)S(1)}, bf16[4,128,128]{2,1,0:T(8,128)(2,1)S(1)}, u32[]{:S(2)}, u32[]{:S(2)}) collective-permute-start(bf16[4,128,128]{2,1,0:T(8,128)(2,1)S(1)} %get-tuple-element.39), channel_id=1, source_target_pairs={{0,8},{8,0},{16,24},{24,16},{1,9},{9,1},{17,25},{25,17},{2,10},{10... | collective-permute-start | bytes 393224 | tf_op jit(solution)/shard_map/ppermute | solution.py:368
  41.3 1.5 %collective-permute-start.12 = (bf16[4,128,128]{2,1,0:T(8,128)(2,1)S(1)}, bf16[4,128,128]{2,1,0:T(8,128)(2,1)S(1)}, u32[]{:S(2)}, u32[]{:S(2)}) collective-permute-start(bf16[4,128,128]{2,1,0:T(8,128)(2,1)S(1)} %get-tuple-element.47), channel_id=1, source_target_pairs={{0,16},{8,24},{16,0},{24,8},{1,17},{9,25},{17,1},{25,9},{2,18},{10... | collective-permute-start | bytes 393224 | tf_op jit(solution)/shard_map/ppermute | solution.py:371
  42.8 1.0 %copy-done.6 = f32[8,128,128]{2,1,0:T(8,128)S(1)} copy-done((f32[8,128,128]{2,1,0:T(8,128)S(1)}, f32[8,128,128]{2,1,0:T(8,128)}, u32[]{:S(2)}) %copy-start.6) | copy-done | bytes 524312
  43.9 2.9 %exchange.1.acc_ref = f32[8,128,128]{2,1,0:T(8,128)S(1)} custom-call(s32[8,2]{1,0:T(8,128)S(1)} %copy-done.8, s32[16]{0:T(128)S(1)} %copy-done.11, bf16[1,512,512]{2,1,0:T(8,128)(2,1)} %bitcast.9.refs_0_, bf16[1,512,512]{2,1,0:T(8,128)(2,1)} %bitcast.10.refs_1_, bf16[1,512,512]{2,1,0:T(8,128)(2,1)} %bitcast.11.refs_2_, ...), custom_call_target="tpu_custom_call" | custom-call | tf_op jit(solution)/shard_map/exchange/pallas_call | solution.py:25
  46.8 3.4 %second_across.1 = (bf16[4,128,128]{2,1,0:T(8,128)(2,1)S(1)}, bf16[4,128,128]{2,1,0:T(8,128)(2,1)S(1)}) custom-call(s32[1]{0:T(128)} %bitcast.upper_ref, bf16[4,656,128]{2,1,0:T(8,128)(2,1)S(1)} %copy-done.1, bf16[4,656,128]{2,1,0:T(8,128)(2,1)} %collective-permute-done.9.x_high.one_ref, bf16[4,656,128]{2,1,0:T(8,128)(2,1)} %collective-permute-done.10.y_low.two_ref, ...), custom_call_target="tpu_custom_call" | custom-call | tf_op jit(solution)/shard_map/second_across/pallas_call | solution.py:25
  50.2 1.5 %collective-permute-start.13 = (bf16[4,128,128]{2,1,0:T(8,128)(2,1)S(1)}, bf16[4,128,128]{2,1,0:T(8,128)(2,1)S(1)}, u32[]{:S(2)}, u32[]{:S(2)}) collective-permute-start(bf16[4,128,128]{2,1,0:T(8,128)(2,1)S(1)} %get-tuple-element.45), channel_id=1, source_target_pairs={{0,8},{8,0},{16,24},{24,16},{1,9},{9,1},{17,25},{25,17},{2,10},{10... | collective-permute-start | bytes 393224 | tf_op jit(solution)/shard_map/ppermute | solution.py:368
  51.7 1.5 %collective-permute-start.14 = (bf16[4,128,128]{2,1,0:T(8,128)(2,1)S(1)}, bf16[4,128,128]{2,1,0:T(8,128)(2,1)S(1)}, u32[]{:S(2)}, u32[]{:S(2)}) collective-permute-start(bf16[4,128,128]{2,1,0:T(8,128)(2,1)S(1)} %get-tuple-element.48), channel_id=1, source_target_pairs={{0,16},{8,24},{16,0},{24,8},{1,17},{9,25},{17,1},{25,9},{2,18},{10... | collective-permute-start | bytes 393224 | tf_op jit(solution)/shard_map/ppermute | solution.py:371
  53.2 4.7 %coupled.3.acc_ref = f32[8,128,128]{2,1,0:T(8,128)S(1)} custom-call(f32[8,128]{1,0:T(8,128)S(1)} %copy-done.10, bf16[1024,512]{1,0:T(8,128)(2,1)S(1)} %get-tuple-element.40.refs_2_.left_ref.refs_3_, f32[8,128,128]{2,1,0:T(8,128)S(1)} %exchange.1.acc_ref, bf16[4,656,128]{2,1,0:T(8,128)(2,1)} %collective-permute-done.9.x_high.one_ref, ...), custom_call_target="tpu_custom_call" | custom-call | flops 20000000000 | tf_op jit(solution)/shard_map/coupled/pallas_call | solution.py:25
  57.9 0.9 %finish.1 = f32[8,128,128]{2,1,0:T(8,128)} custom-call(s32[1]{0:T(128)} %bitcast.upper_ref, f32[8,128,128]{2,1,0:T(8,128)S(1)} %coupled.3.acc_ref, bf16[4,128,128]{2,1,0:T(8,128)(2,1)S(1)} %collective-permute-done.11.low_ref, bf16[4,128,128]{2,1,0:T(8,128)(2,1)S(1)} %collective-permute-done.12.high_ref, ...), custom_call_target="tpu_custom_call" | custom-call | tf_op jit(solution)/shard_map/finish/pallas_call | solution.py:25
  (34 shorter events, 0.1 us)
Async XLA Ops:
  0.0 19.1 %collective-permute-start = (bf16[512,512]{1,0:T(8,128)(2,1)}, bf16[512,512]{1,0:T(8,128)(2,1)}, u32[]{:S(2)}, u32[]{:S(2)}) collective-permute-start(bf16[512,512]{1,0:T(8,128)(2,1)} %bitcast.14), channel_id=1, source_target_pairs={{0,2},{1,3},{2,4},{3,5},{4,6},{5,7},{6,0},{7,1},{8,10},{9,11},{10,... | collective-permute-start | bytes 1572872 | tf_op jit(solution)/shard_map/ppermute | solution.py:374
  3.0 25.2 %collective-permute-start.6 = (bf16[512,512]{1,0:T(8,128)(2,1)}, bf16[512,512]{1,0:T(8,128)(2,1)}, u32[]{:S(2)}, u32[]{:S(2)}) collective-permute-start(bf16[512,512]{1,0:T(8,128)(2,1)} %bitcast.15), channel_id=1, source_target_pairs={{0,6},{1,7},{2,0},{3,1},{4,2},{5,3},{6,4},{7,5},{8,14},{9,15},{10,... | collective-permute-start | bytes 1572872 | tf_op jit(solution)/shard_map/ppermute | solution.py:374
  5.1 14.1 %copy-start.12 = (bf16[1,512,512]{2,1,0:T(8,128)(2,1)S(1)}, bf16[1,512,512]{2,1,0:T(8,128)(2,1)}, u32[]{:S(2)}) copy-start(bf16[1,512,512]{2,1,0:T(8,128)(2,1)} %refs_0_.1) | copy-start | bytes 1572868
  9.0 18.3 %collective-permute-start.2 = (bf16[4,656,128]{2,1,0:T(8,128)(2,1)}, bf16[4,656,128]{2,1,0:T(8,128)(2,1)S(1)}, u32[]{:S(2)}, u32[]{:S(2)}) collective-permute-start(bf16[4,656,128]{2,1,0:T(8,128)(2,1)} %get-tuple-element.44.low_ref), channel_id=1, source_target_pairs={{0,8},{8,0},{16,24},{24,16},{1,9},{9,1},{17,25},{25,17},{2,10},{10... | collective-permute-start | bytes 2015240 | tf_op jit(solution)/shard_map/ppermute | solution.py:368
  10.8 16.5 %collective-permute-start.3 = (bf16[4,656,128]{2,1,0:T(8,128)(2,1)}, bf16[4,656,128]{2,1,0:T(8,128)(2,1)S(1)}, u32[]{:S(2)}, u32[]{:S(2)}) collective-permute-start(bf16[4,656,128]{2,1,0:T(8,128)(2,1)} %get-tuple-element.43.high_ref), channel_id=1, source_target_pairs={{0,16},{8,24},{16,0},{24,8},{1,17},{9,25},{17,1},{25,9},{2,18},{10... | collective-permute-start | bytes 2015240 | tf_op jit(solution)/shard_map/ppermute | solution.py:371
  12.3 34.5 %collective-permute-start.9 = (bf16[4,656,128]{2,1,0:T(8,128)(2,1)}, bf16[4,656,128]{2,1,0:T(8,128)(2,1)}, u32[]{:S(2)}, u32[]{:S(2)}) collective-permute-start(bf16[4,656,128]{2,1,0:T(8,128)(2,1)} %get-tuple-element.43.high_ref), channel_id=1, source_target_pairs={{0,8},{8,0},{16,24},{24,16},{1,9},{9,1},{17,25},{25,17},{2,10},{10... | collective-permute-start | bytes 2015240 | tf_op jit(solution)/shard_map/ppermute | solution.py:368
  12.8 1.1 %copy-start.4 = (bf16[4,656,128]{2,1,0:T(8,128)(2,1)S(1)}, bf16[4,656,128]{2,1,0:T(8,128)(2,1)}, u32[]{:S(2)}) copy-start(bf16[4,656,128]{2,1,0:T(8,128)(2,1)} %get-tuple-element.43.high_ref) | copy-start | bytes 2015236
  13.9 0.7 %copy-start.9 = (f32[8,128]{1,0:T(8,128)S(1)}, f32[8,128]{1,0:T(8,128)}, u32[]{:S(2)}) copy-start(f32[8,128]{1,0:T(8,128)} %get-tuple-element.27.weight_ref) | copy-start | bytes 12292
  19.1 0.7 %copy-start.7 = (s32[8,2]{1,0:T(8,128)S(1)}, s32[8,2]{1,0:T(8,128)}, u32[]{:S(2)}) copy-start(s32[8,2]{1,0:T(8,128)} %get-tuple-element.31.uses_ref) | copy-start | bytes 196
  19.8 10.1 %copy-start.10 = (f32[8,128]{1,0:T(8,128)S(1)}, f32[8,128]{1,0:T(8,128)}, u32[]{:S(2)}) copy-start(f32[8,128]{1,0:T(8,128)} %get-tuple-element.27.weight_ref) | copy-start | bytes 12292
  21.4 14.8 %copy-start.8 = (s32[8,2]{1,0:T(8,128)S(1)}, s32[8,2]{1,0:T(8,128)}, u32[]{:S(2)}) copy-start(s32[8,2]{1,0:T(8,128)} %get-tuple-element.31.uses_ref) | copy-start | bytes 196
  21.4 18.4 %collective-permute-start.1 = (bf16[512,512]{1,0:T(8,128)(2,1)}, bf16[512,512]{1,0:T(8,128)(2,1)}, u32[]{:S(2)}, u32[]{:S(2)}) collective-permute-start(bf16[512,512]{1,0:T(8,128)(2,1)} %collective-permute-done), channel_id=1, source_target_pairs={{0,2},{1,3},{2,4},{3,5},{4,6},{5,7},{6,0},{7,1},{8,10},{9,11},{10,... | collective-permute-start | bytes 1572872 | tf_op jit(solution)/shard_map/ppermute | solution.py:374
  27.3 6.6 %copy-start = (bf16[4,656,128]{2,1,0:T(8,128)(2,1)}, bf16[4,656,128]{2,1,0:T(8,128)(2,1)S(1)}, u32[]{:S(2)}) copy-start(bf16[4,656,128]{2,1,0:T(8,128)(2,1)S(1)} %collective-permute-done.2.one_ref.x_low) | copy-start | bytes 2015236
  27.3 6.7 %copy-start.2 = (bf16[4,656,128]{2,1,0:T(8,128)(2,1)}, bf16[4,656,128]{2,1,0:T(8,128)(2,1)S(1)}, u32[]{:S(2)}) copy-start(bf16[4,656,128]{2,1,0:T(8,128)(2,1)S(1)} %collective-permute-done.3.two_ref.y_high) | copy-start | bytes 2015236
  27.3 8.8 %collective-permute-start.4 = (bf16[512,512]{1,0:T(8,128)(2,1)S(1)}, bf16[512,512]{1,0:T(8,128)(2,1)S(1)}, u32[]{:S(2)}, u32[]{:S(2)}) collective-permute-start(bf16[512,512]{1,0:T(8,128)(2,1)S(1)} %bitcast.16), channel_id=1, source_target_pairs={{0,1},{1,0},{2,3},{3,2},{4,5},{5,4},{6,7},{7,6},{8,9},{9,8},{10,11... | collective-permute-start | bytes 1572872 | tf_op jit(solution)/shard_map/ppermute | solution.py:377
  27.3 8.8 %collective-permute-start.5 = (bf16[512,512]{1,0:T(8,128)(2,1)}, bf16[512,512]{1,0:T(8,128)(2,1)S(1)}, u32[]{:S(2)}, u32[]{:S(2)}) collective-permute-start(bf16[512,512]{1,0:T(8,128)(2,1)} %collective-permute-done), channel_id=1, source_target_pairs={{0,1},{1,0},{2,3},{3,2},{4,5},{5,4},{6,7},{7,6},{8,9},{9,8},{10,11... | collective-permute-start | bytes 1572872 | tf_op jit(solution)/shard_map/ppermute | solution.py:377
  28.2 18.6 %collective-permute-start.10 = (bf16[4,656,128]{2,1,0:T(8,128)(2,1)}, bf16[4,656,128]{2,1,0:T(8,128)(2,1)}, u32[]{:S(2)}, u32[]{:S(2)}) collective-permute-start(bf16[4,656,128]{2,1,0:T(8,128)(2,1)} %get-tuple-element.44.low_ref), channel_id=1, source_target_pairs={{0,16},{8,24},{16,0},{24,8},{1,17},{9,25},{17,1},{25,9},{2,18},{10... | collective-permute-start | bytes 2015240 | tf_op jit(solution)/shard_map/ppermute | solution.py:371
  33.9 3.9 %copy-start.5 = (f32[8,128,128]{2,1,0:T(8,128)}, f32[8,128,128]{2,1,0:T(8,128)S(1)}, u32[]{:S(2)}) copy-start(f32[8,128,128]{2,1,0:T(8,128)S(1)} %coupled.2.refs_5_) | copy-start | bytes 1572868
  36.0 5.3 %collective-permute-start.8 = (bf16[512,512]{1,0:T(8,128)(2,1)}, bf16[512,512]{1,0:T(8,128)(2,1)}, u32[]{:S(2)}, u32[]{:S(2)}) collective-permute-start(bf16[512,512]{1,0:T(8,128)(2,1)} %collective-permute-done.6), channel_id=1, source_target_pairs={{0,1},{1,0},{2,3},{3,2},{4,5},{5,4},{6,7},{7,6},{8,9},{9,8},{10,11... | collective-permute-start | bytes 1572872 | tf_op jit(solution)/shard_map/ppermute | solution.py:377
  36.1 6.7 %copy-start.11 = (s32[16]{0:T(128)S(1)}, s32[16]{0:T(128)}, u32[]{:S(2)}) copy-start(s32[16]{0:T(128)} %get-tuple-element.32.turn_ref) | copy-start | bytes 196
  39.8 3.0 %collective-permute-start.7 = (bf16[512,512]{1,0:T(8,128)(2,1)}, bf16[512,512]{1,0:T(8,128)(2,1)}, u32[]{:S(2)}, u32[]{:S(2)}) collective-permute-start(bf16[512,512]{1,0:T(8,128)(2,1)} %collective-permute-done.1), channel_id=1, source_target_pairs={{0,1},{1,0},{2,3},{3,2},{4,5},{5,4},{6,7},{7,6},{8,9},{9,8},{10,11... | collective-permute-start | bytes 1572872 | tf_op jit(solution)/shard_map/ppermute | solution.py:377
  39.8 18.1 %collective-permute-start.11 = (bf16[4,128,128]{2,1,0:T(8,128)(2,1)S(1)}, bf16[4,128,128]{2,1,0:T(8,128)(2,1)S(1)}, u32[]{:S(2)}, u32[]{:S(2)}) collective-permute-start(bf16[4,128,128]{2,1,0:T(8,128)(2,1)S(1)} %get-tuple-element.39), channel_id=1, source_target_pairs={{0,8},{8,0},{16,24},{24,16},{1,9},{9,1},{17,25},{25,17},{2,10},{10... | collective-permute-start | bytes 393224 | tf_op jit(solution)/shard_map/ppermute | solution.py:368
  41.3 16.6 %collective-permute-start.12 = (bf16[4,128,128]{2,1,0:T(8,128)(2,1)S(1)}, bf16[4,128,128]{2,1,0:T(8,128)(2,1)S(1)}, u32[]{:S(2)}, u32[]{:S(2)}) collective-permute-start(bf16[4,128,128]{2,1,0:T(8,128)(2,1)S(1)} %get-tuple-element.47), channel_id=1, source_target_pairs={{0,16},{8,24},{16,0},{24,8},{1,17},{9,25},{17,1},{25,9},{2,18},{10... | collective-permute-start | bytes 393224 | tf_op jit(solution)/shard_map/ppermute | solution.py:371
  42.8 1.0 %copy-start.6 = (f32[8,128,128]{2,1,0:T(8,128)S(1)}, f32[8,128,128]{2,1,0:T(8,128)}, u32[]{:S(2)}) copy-start(f32[8,128,128]{2,1,0:T(8,128)} %copy-done.5) | copy-start | bytes 1572868
  43.9 2.9 %copy-start.1 = (bf16[4,656,128]{2,1,0:T(8,128)(2,1)S(1)}, bf16[4,656,128]{2,1,0:T(8,128)(2,1)}, u32[]{:S(2)}) copy-start(bf16[4,656,128]{2,1,0:T(8,128)(2,1)} %copy-done) | copy-start | bytes 2015236
  43.9 2.9 %copy-start.3 = (bf16[4,656,128]{2,1,0:T(8,128)(2,1)S(1)}, bf16[4,656,128]{2,1,0:T(8,128)(2,1)}, u32[]{:S(2)}) copy-start(bf16[4,656,128]{2,1,0:T(8,128)(2,1)} %copy-done.2) | copy-start | bytes 2015236
  50.2 7.7 %collective-permute-start.13 = (bf16[4,128,128]{2,1,0:T(8,128)(2,1)S(1)}, bf16[4,128,128]{2,1,0:T(8,128)(2,1)S(1)}, u32[]{:S(2)}, u32[]{:S(2)}) collective-permute-start(bf16[4,128,128]{2,1,0:T(8,128)(2,1)S(1)} %get-tuple-element.45), channel_id=1, source_target_pairs={{0,8},{8,0},{16,24},{24,16},{1,9},{9,1},{17,25},{25,17},{2,10},{10... | collective-permute-start | bytes 393224 | tf_op jit(solution)/shard_map/ppermute | solution.py:368
  51.7 6.2 %collective-permute-start.14 = (bf16[4,128,128]{2,1,0:T(8,128)(2,1)S(1)}, bf16[4,128,128]{2,1,0:T(8,128)(2,1)S(1)}, u32[]{:S(2)}, u32[]{:S(2)}) collective-permute-start(bf16[4,128,128]{2,1,0:T(8,128)(2,1)S(1)} %get-tuple-element.48), channel_id=1, source_target_pairs={{0,16},{8,24},{16,0},{24,8},{1,17},{9,25},{17,1},{25,9},{2,18},{10... | collective-permute-start | bytes 393224 | tf_op jit(solution)/shard_map/ppermute | solution.py:371

commit v6 on v5

--- a/solution.py
+++ b/solution.py
@@ -223,7 +223,7 @@
 
 
 def exchange_kernel(scale, base, uses_ref, turn_ref, *refs):
-    *slab_refs, own_ref, early_ref, acc_ref, out_ref, late_ref = refs
+    *slab_refs, own_ref, early_ref, out_ref, late_ref = refs
 
     def store(k, use, side, half):
         late_ref[2 * (k - base) + use] = half
@@ -236,16 +236,16 @@
     half_transforms(uses_ref, slab_refs, own_ref, store, base, out_ref.shape[1])
     for p in range(out_ref.shape[0]):
         product = lax.dot_general(half(p, 0), half(p, 1), (((0,), (0,)), ((), ())), preferred_element_type=jnp.float32)
-        out_ref[p] = acc_ref[p] + product * scale
-
-
-def finish_kernel(upper_ref, acc_ref, low_ref, high_ref, row_ref, column_ref, out_ref):
+        out_ref[p] = product * scale
+
+
+def finish_kernel(upper_ref, acc_ref, rest_ref, low_ref, high_ref, row_ref, column_ref, out_ref):
     half = low_ref.shape[0]
     for p in range(out_ref.shape[0]):
         k, upper = p % half, p // half
         first = (low_ref, high_ref)[upper][k].astype(jnp.float32)
         second = jnp.where(upper_ref[0] == upper, row_ref[k], column_ref[k]).astype(jnp.float32)
-        out_ref[p] = acc_ref[p] + (first + second)
+        out_ref[p] = acc_ref[p] + rest_ref[p] + (first + second)
 
 
 def half_products(uses, base, slabs, own_t, pno, done, flops):
@@ -259,21 +259,21 @@
     )
 
 
-def add_exchange(uses, turn, base, slabs, own_t, early, acc):
+def exchange(uses, turn, base, slabs, own_t, early, shape):
     return call_kernel(
         functools.partial(exchange_kernel, 1.0 / math.sqrt(slabs[0].shape[1]), base),
-        jax.ShapeDtypeStruct(acc.shape, jnp.float32),
+        jax.ShapeDtypeStruct(shape, jnp.float32),
         [pltpu.VMEM((2 * sum(slab.shape[0] for slab in slabs),) + early.shape[1:], jnp.bfloat16)],
         "exchange",
         (uses, turn),
-        (*slabs, own_t, early, acc),
+        (*slabs, own_t, early),
         EXCHANGE_COST,
     )
 
 
-def finish(upper, acc, backs):
+def finish(upper, acc, rest, backs):
     shape = jax.ShapeDtypeStruct(acc.shape, jnp.float32)
-    return call_kernel(finish_kernel, shape, [], "finish", (upper,), (acc, *backs), 0)
+    return call_kernel(finish_kernel, shape, [], "finish", (upper,), (acc, rest, *backs), 0)
 
 
 def pack_kernel(scale, chips, group_ref, me_ref, coupled_ref, length_ref, owner_ref, orbs_ref, base_ref, amp_ref, *refs):
@@ -409,14 +409,14 @@
         halves = half_products(uses, 2, more, after(own_t, first[0]), pno, halves, MORE_COST)
         beyond = after(beyond, halves)
         rest = [value[None] for value in (beyond, other_core(beyond), other_core(above))]
-    acc = add_exchange(uses, turns, ahead, rest, own_t, halves, acc)
+    rest_sum = exchange(uses, turns, ahead, rest, own_t, halves, acc.shape)
     second = across(
-        second_across_kernel, "second_across", (upper,), (after(x_lo, acc), x_hi, y_lo, y_hi), orbs, SECOND_COST
+        second_across_kernel, "second_across", (upper,), (after(x_lo, rest_sum), x_hi, y_lo, y_hi), orbs, SECOND_COST
     )
     back_row, back_column = along_x(second[0]), along_y(second[1])
     lanes = [*range(pairs + half, 2 * pairs), *range(2 * pairs, 2 * pairs + half)]
-    acc = add_coupled(lanes, weights, own_t, after(acc, second[0]), (x_hi, y_lo), LAST_COST)
-    return finish(upper, acc, (back_low, back_high, back_row, back_column))
+    rest_sum = add_coupled(lanes, weights, own_t, after(rest_sum, second[0]), (x_hi, y_lo), LAST_COST)
+    return finish(upper, acc, rest_sum, (back_low, back_high, back_row, back_column))
 
 
 def solution(mesh):

time: 59.6 us -> 59.6 us (level)
  local copies, waits for them, and re-layouts: 3.57 us -> 2.53 us
  starting transfers between devices: 17.4 us -> 18 us
    unnamed x26, local copies, waits for them, and re-layouts: 3.57 us -> 2.53 us
    ppermute x4, starting transfers between devices: 5.31 us -> 5.91 us  [along_x(): return lax.ppermute(value, 'grp', [(g, g ^ 1) for g in range(n_grp)])]
  transfers between devices with their start and end apart: 15 -> 15, of which waited for: 3 -> 4; matrix products, arithmetic and copies ran while one was open for 0% -> 0% of each run, Pallas kernels for 49% -> 49%
where the time goes in v6:
time: 59.6 us; the launch traced here: 58.9 us
  Pallas kernels  29.5 us (49%)
  starting transfers between devices  18 us (30%)
  waiting for transfers between devices  8.56 us (14%)
  local copies, waits for them, and re-layouts  2.53 us (4%)
    pallas_call x9, Pallas kernels, call_kernel(): pl.pallas_call(body, out_shape=out_shape, in_specs=[SMEM_SPEC] * len(smem...  25.6 us
    ppermute x4, starting transfers between devices, along_y(): return lax.ppermute(value, 'grp', [(g, g ^ 2) for g in range(n_grp)])  6.33 us
    ppermute x4, starting transfers between devices, along_x(): return lax.ppermute(value, 'grp', [(g, g ^ 1) for g in range(n_grp)])  5.91 us
    ppermute x4, waiting for transfers between devices, along_x(): return lax.ppermute(value, 'grp', [(g, g ^ 1) for g in range(n_grp)])  5.81 us
    ppermute x3, starting transfers between devices, along_chips(): lax.ppermute(value, 'dev', [(d, (d + 2 * step) % n_dev) for d in range(n_...  5.11 us
    pallas_call x1, Pallas kernels, pack(): pl.pallas_call(functools.partial(pack_kernel, orbs / pno, chips), out_sha...  3.92 us
    unnamed x26, local copies, waits for them, and re-layouts  2.53 us
    ppermute x3, waiting for transfers between devices, along_chips(): lax.ppermute(value, 'dev', [(d, (d + 2 * step) % n_dev) for d in range(n_...  2.26 us
  transfers between devices with their start and end apart: 15, of which 4 were waited for; matrix products, arithmetic and copies ran while one was open for 0% of the time, Pallas kernels for 49%

profile of v6, /device:TPU:0, one launch (start us, length us, event | category | flops | bytes accessed | tf_op | source)
XLA Modules:
  0.0 58.9 jit_solution(77143483501187234)
XLA Ops:
  0.0 3.0 %collective-permute-start = (bf16[512,512]{1,0:T(8,128)(2,1)}, bf16[512,512]{1,0:T(8,128)(2,1)}, u32[]{:S(2)}, u32[]{:S(2)}) collective-permute-start(bf16[512,512]{1,0:T(8,128)(2,1)} %bitcast.14), channel_id=1, source_target_pairs={{0,2},{1,3},{2,4},{3,5},{4,6},{5,7},{6,0},{7,1},{8,10},{9,11},{10,... | collective-permute-start | bytes 1572872 | tf_op jit(solution)/shard_map/ppermute | solution.py:374
  3.0 2.0 %collective-permute-start.6 = (bf16[512,512]{1,0:T(8,128)(2,1)}, bf16[512,512]{1,0:T(8,128)(2,1)}, u32[]{:S(2)}, u32[]{:S(2)}) collective-permute-start(bf16[512,512]{1,0:T(8,128)(2,1)} %bitcast.15), channel_id=1, source_target_pairs={{0,6},{1,7},{2,0},{3,1},{4,2},{5,3},{6,4},{7,5},{8,14},{9,15},{10,... | collective-permute-start | bytes 1572872 | tf_op jit(solution)/shard_map/ppermute | solution.py:374
  5.1 3.9 %pack.1 = (bf16[4,656,128]{2,1,0:T(8,128)(2,1)}, bf16[4,656,128]{2,1,0:T(8,128)(2,1)}, f32[8,128]{1,0:T(8,128)}, s32[8,2]{1,0:T(8,128)}, s32[16]{0:T(128)}) custom-call(s32[1]{0:T(128)} %bitcast.1.group_ref, s32[1]{0:T(128)} %bitcast.2.me_ref, s32[8,32]{1,0:T(8,128)} %coupled_ref.1, s32[8]{0:T(128)} %length_ref.1, s32[8]{0:T(128)} %owner_ref.1, ...), custom_call_target="tpu_custom_call" | custom-call | tf_op jit(solution)/shard_map/pack/pallas_call | solution.py:338
  9.0 1.8 %collective-permute-start.1 = (bf16[4,656,128]{2,1,0:T(8,128)(2,1)}, bf16[4,656,128]{2,1,0:T(8,128)(2,1)S(1)}, u32[]{:S(2)}, u32[]{:S(2)}) collective-permute-start(bf16[4,656,128]{2,1,0:T(8,128)(2,1)} %get-tuple-element.44.low_ref), channel_id=1, source_target_pairs={{0,8},{8,0},{16,24},{24,16},{1,9},{9,1},{17,25},{25,17},{2,10},{10... | collective-permute-start | bytes 2015240 | tf_op jit(solution)/shard_map/ppermute | solution.py:368
  10.8 1.5 %collective-permute-start.2 = (bf16[4,656,128]{2,1,0:T(8,128)(2,1)}, bf16[4,656,128]{2,1,0:T(8,128)(2,1)S(1)}, u32[]{:S(2)}, u32[]{:S(2)}) collective-permute-start(bf16[4,656,128]{2,1,0:T(8,128)(2,1)} %get-tuple-element.43.high_ref), channel_id=1, source_target_pairs={{0,16},{8,24},{16,0},{24,8},{1,17},{9,25},{17,1},{25,9},{2,18},{10... | collective-permute-start | bytes 2015240 | tf_op jit(solution)/shard_map/ppermute | solution.py:371
  12.3 0.5 collective-permute-start.9
  12.8 1.1 %copy-done.4 = bf16[4,656,128]{2,1,0:T(8,128)(2,1)S(1)} copy-done((bf16[4,656,128]{2,1,0:T(8,128)(2,1)S(1)}, bf16[4,656,128]{2,1,0:T(8,128)(2,1)}, u32[]{:S(2)}) %copy-start.4) | copy-done | bytes 671768
  13.9 0.7 %copy-done.9 = f32[8,128]{1,0:T(8,128)S(1)} copy-done((f32[8,128]{1,0:T(8,128)S(1)}, f32[8,128]{1,0:T(8,128)}, u32[]{:S(2)}) %copy-start.9) | copy-done | bytes 4120
  14.6 4.5 %own_coupled.1 = (f32[8,128,128]{2,1,0:T(8,128)S(1)}, bf16[1024,512]{1,0:T(8,128)(2,1)S(1)}) custom-call(f32[8,128]{1,0:T(8,128)S(1)} %copy-done.9, bf16[4,656,128]{2,1,0:T(8,128)(2,1)} %get-tuple-element.44.low_ref, bf16[4,656,128]{2,1,0:T(8,128)(2,1)S(1)} %copy-done.4), custom_call_target="tpu_custom_call" | custom-call | tf_op jit(solution)/shard_map/own_coupled/pallas_call | solution.py:25
  19.1 0.7 %copy-done.7 = s32[8,2]{1,0:T(8,128)S(1)} copy-done((s32[8,2]{1,0:T(8,128)S(1)}, s32[8,2]{1,0:T(8,128)}, u32[]{:S(2)}) %copy-start.7) | copy-done | bytes 88
  19.8 1.6 %halves.1.refs_4_ = bf16[17,512,128]{2,1,0:T(8,128)(2,1)S(1)} custom-call(s32[8,2]{1,0:T(8,128)S(1)} %copy-done.7, bf16[1,512,512]{2,1,0:T(8,128)(2,1)S(1)} %copy-done.12, bf16[1,512,512]{2,1,0:T(8,128)(2,1)} %bitcast.5.refs_1_, bf16[1024,512]{1,0:T(8,128)(2,1)S(1)} %get-tuple-element.40.refs_2_.left_ref.refs_3_), custom_call_target="tpu_custom_call" | custom-call | flops 20000000000 | tf_op jit(solution)/shard_map/halves/pallas_call | solution.py:25
  21.4 0.1 collective-permute-start.3
  21.5 5.8 %collective-permute-done.1.one_ref.x_low = bf16[4,656,128]{2,1,0:T(8,128)(2,1)S(1)} collective-permute-done((bf16[4,656,128]{2,1,0:T(8,128)(2,1)}, bf16[4,656,128]{2,1,0:T(8,128)(2,1)S(1)}, u32[]{:S(2)}, u32[]{:S(2)}) %collective-permute-start.1) | collective-permute-done | bytes 671776 | tf_op jit(solution)/shard_map/ppermute | solution.py:368
  27.3 0.1 collective-permute-start.4
  27.3 0.5 collective-permute-start.5
  27.8 0.3 collective-permute-done.6
  28.2 1.8 %collective-permute-start.10 = (bf16[4,656,128]{2,1,0:T(8,128)(2,1)}, bf16[4,656,128]{2,1,0:T(8,128)(2,1)}, u32[]{:S(2)}, u32[]{:S(2)}) collective-permute-start(bf16[4,656,128]{2,1,0:T(8,128)(2,1)} %get-tuple-element.44.low_ref), channel_id=1, source_target_pairs={{0,16},{8,24},{16,0},{24,8},{1,17},{9,25},{17,1},{25,9},{2,18},{10... | collective-permute-start | bytes 2015240 | tf_op jit(solution)/shard_map/ppermute | solution.py:371
  29.9 4.0 %coupled.2.acc_ref = f32[8,128,128]{2,1,0:T(8,128)S(1)} custom-call(f32[8,128]{1,0:T(8,128)S(1)} %copy-done.10, bf16[1024,512]{1,0:T(8,128)(2,1)S(1)} %get-tuple-element.40.refs_2_.left_ref.refs_3_, f32[8,128,128]{2,1,0:T(8,128)S(1)} %get-tuple-element.33.acc_ref, bf16[4,656,128]{2,1,0:T(8,128)(2,1)S(1)} %collective-permute-done.1.one_ref.x_low, ...), custom_call_target="tpu_custom_call" | custom-call | flops 20000000000 | tf_op jit(solution)/shard_map/coupled/pallas_call | solution.py:25
  33.9 0.0 copy-start.5
  33.9 2.1 %first_across.1 = (bf16[4,128,128]{2,1,0:T(8,128)(2,1)S(1)}, bf16[4,128,128]{2,1,0:T(8,128)(2,1)S(1)}) custom-call(bf16[4,656,128]{2,1,0:T(8,128)(2,1)S(1)} %collective-permute-done.1.one_ref.x_low, bf16[4,656,128]{2,1,0:T(8,128)(2,1)S(1)} %collective-permute-done.2.two_ref.y_high), custom_call_target="tpu_custom_call" | custom-call | tf_op jit(solution)/shard_map/first_across/pallas_call | solution.py:25
  36.0 0.1 collective-permute-start.8
  36.2 1.7 %more_halves.1.refs_4_ = bf16[17,512,128]{2,1,0:T(8,128)(2,1)S(1)} custom-call(s32[8,2]{1,0:T(8,128)S(1)} %copy-done.8, bf16[1,512,512]{2,1,0:T(8,128)(2,1)S(1)} %bitcast.12, bf16[1,512,512]{2,1,0:T(8,128)(2,1)S(1)} %bitcast.13, bf16[1,512,512]{2,1,0:T(8,128)(2,1)} %bitcast.8.refs_2_, ...), custom_call_target="tpu_custom_call", output_to_operand_aliasing={{}: (5, {})} | custom-call | tf_op jit(solution)/shard_map/more_halves/pallas_call | solution.py:25
  37.9 1.9 %collective-permute-done.3 = bf16[512,512]{1,0:T(8,128)(2,1)} collective-permute-done((bf16[512,512]{1,0:T(8,128)(2,1)}, bf16[512,512]{1,0:T(8,128)(2,1)}, u32[]{:S(2)}, u32[]{:S(2)}) %collective-permute-start.3) | collective-permute-done | bytes 524320 | tf_op jit(solution)/shard_map/ppermute | solution.py:374
  39.8 1.5 %collective-permute-start.11 = (bf16[4,128,128]{2,1,0:T(8,128)(2,1)S(1)}, bf16[4,128,128]{2,1,0:T(8,128)(2,1)S(1)}, u32[]{:S(2)}, u32[]{:S(2)}) collective-permute-start(bf16[4,128,128]{2,1,0:T(8,128)(2,1)S(1)} %get-tuple-element.39), channel_id=1, source_target_pairs={{0,8},{8,0},{16,24},{24,16},{1,9},{9,1},{17,25},{25,17},{2,10},{10... | collective-permute-start | bytes 393224 | tf_op jit(solution)/shard_map/ppermute | solution.py:368
  41.3 1.5 %collective-permute-start.12 = (bf16[4,128,128]{2,1,0:T(8,128)(2,1)S(1)}, bf16[4,128,128]{2,1,0:T(8,128)(2,1)S(1)}, u32[]{:S(2)}, u32[]{:S(2)}) collective-permute-start(bf16[4,128,128]{2,1,0:T(8,128)(2,1)S(1)} %get-tuple-element.47), channel_id=1, source_target_pairs={{0,16},{8,24},{16,0},{24,8},{1,17},{9,25},{17,1},{25,9},{2,18},{10... | collective-permute-start | bytes 393224 | tf_op jit(solution)/shard_map/ppermute | solution.py:371
  42.8 2.9 %exchange.1.acc_ref = f32[8,128,128]{2,1,0:T(8,128)S(1)} custom-call(s32[8,2]{1,0:T(8,128)S(1)} %copy-done.8, s32[16]{0:T(128)S(1)} %copy-done.11, bf16[1,512,512]{2,1,0:T(8,128)(2,1)} %bitcast.9.refs_0_, bf16[1,512,512]{2,1,0:T(8,128)(2,1)} %bitcast.10.refs_1_, bf16[1,512,512]{2,1,0:T(8,128)(2,1)} %bitcast.11.refs_2_, ...), custom_call_target="tpu_custom_call" | custom-call | tf_op jit(solution)/shard_map/exchange/pallas_call | solution.py:25
  45.7 0.5 collective-permute-done.10.y_low.two_ref
  46.2 3.4 %second_across.1 = (bf16[4,128,128]{2,1,0:T(8,128)(2,1)S(1)}, bf16[4,128,128]{2,1,0:T(8,128)(2,1)S(1)}) custom-call(s32[1]{0:T(128)} %bitcast.upper_ref, bf16[4,656,128]{2,1,0:T(8,128)(2,1)S(1)} %copy-done.1, bf16[4,656,128]{2,1,0:T(8,128)(2,1)} %collective-permute-done.9.x_high.one_ref, bf16[4,656,128]{2,1,0:T(8,128)(2,1)} %collective-permute-done.10.y_low.two_ref, ...), custom_call_target="tpu_custom_call" | custom-call | tf_op jit(solution)/shard_map/second_across/pallas_call | solution.py:25
  49.6 2.1 %collective-permute-start.13 = (bf16[4,128,128]{2,1,0:T(8,128)(2,1)S(1)}, bf16[4,128,128]{2,1,0:T(8,128)(2,1)S(1)}, u32[]{:S(2)}, u32[]{:S(2)}) collective-permute-start(bf16[4,128,128]{2,1,0:T(8,128)(2,1)S(1)} %get-tuple-element.45), channel_id=1, source_target_pairs={{0,8},{8,0},{16,24},{24,16},{1,9},{9,1},{17,25},{25,17},{2,10},{10... | collective-permute-start | bytes 393224 | tf_op jit(solution)/shard_map/ppermute | solution.py:368
  51.7 1.5 %collective-permute-start.14 = (bf16[4,128,128]{2,1,0:T(8,128)(2,1)S(1)}, bf16[4,128,128]{2,1,0:T(8,128)(2,1)S(1)}, u32[]{:S(2)}, u32[]{:S(2)}) collective-permute-start(bf16[4,128,128]{2,1,0:T(8,128)(2,1)S(1)} %get-tuple-element.48), channel_id=1, source_target_pairs={{0,16},{8,24},{16,0},{24,8},{1,17},{9,25},{17,1},{25,9},{2,18},{10... | collective-permute-start | bytes 393224 | tf_op jit(solution)/shard_map/ppermute | solution.py:371
  53.2 4.7 %coupled.3.rest_ref = f32[8,128,128]{2,1,0:T(8,128)S(1)} custom-call(f32[8,128]{1,0:T(8,128)S(1)} %copy-done.10, bf16[1024,512]{1,0:T(8,128)(2,1)S(1)} %get-tuple-element.40.refs_2_.left_ref.refs_3_, f32[8,128,128]{2,1,0:T(8,128)S(1)} %exchange.1.acc_ref, bf16[4,656,128]{2,1,0:T(8,128)(2,1)} %collective-permute-done.9.x_high.one_ref, ...), custom_call_target="tpu_custom_call" | custom-call | flops 20000000000 | tf_op jit(solution)/shard_map/coupled/pallas_call | solution.py:25
  57.9 0.9 %finish.1 = f32[8,128,128]{2,1,0:T(8,128)} custom-call(s32[1]{0:T(128)} %bitcast.upper_ref, f32[8,128,128]{2,1,0:T(8,128)S(1)} %copy-done.6, f32[8,128,128]{2,1,0:T(8,128)S(1)} %coupled.3.rest_ref, bf16[4,128,128]{2,1,0:T(8,128)(2,1)S(1)} %collective-permute-done.11.low_ref, bf16[4,128,128]{2,1,0:T(8,128)(2,1)S(1)} %collective-permute-done.12.high_ref, ...), custom_call_target="tpu_custom_call" | custom-call | tf_op jit(solution)/shard_map/finish/pallas_call | solution.py:25
  (34 shorter events, 0.1 us)
Async XLA Ops:
  0.0 19.1 %collective-permute-start = (bf16[512,512]{1,0:T(8,128)(2,1)}, bf16[512,512]{1,0:T(8,128)(2,1)}, u32[]{:S(2)}, u32[]{:S(2)}) collective-permute-start(bf16[512,512]{1,0:T(8,128)(2,1)} %bitcast.14), channel_id=1, source_target_pairs={{0,2},{1,3},{2,4},{3,5},{4,6},{5,7},{6,0},{7,1},{8,10},{9,11},{10,... | collective-permute-start | bytes 1572872 | tf_op jit(solution)/shard_map/ppermute | solution.py:374
  3.0 25.2 %collective-permute-start.6 = (bf16[512,512]{1,0:T(8,128)(2,1)}, bf16[512,512]{1,0:T(8,128)(2,1)}, u32[]{:S(2)}, u32[]{:S(2)}) collective-permute-start(bf16[512,512]{1,0:T(8,128)(2,1)} %bitcast.15), channel_id=1, source_target_pairs={{0,6},{1,7},{2,0},{3,1},{4,2},{5,3},{6,4},{7,5},{8,14},{9,15},{10,... | collective-permute-start | bytes 1572872 | tf_op jit(solution)/shard_map/ppermute | solution.py:374
  5.1 14.1 %copy-start.12 = (bf16[1,512,512]{2,1,0:T(8,128)(2,1)S(1)}, bf16[1,512,512]{2,1,0:T(8,128)(2,1)}, u32[]{:S(2)}) copy-start(bf16[1,512,512]{2,1,0:T(8,128)(2,1)} %refs_0_.1) | copy-start | bytes 1572868
  9.0 18.3 %collective-permute-start.1 = (bf16[4,656,128]{2,1,0:T(8,128)(2,1)}, bf16[4,656,128]{2,1,0:T(8,128)(2,1)S(1)}, u32[]{:S(2)}, u32[]{:S(2)}) collective-permute-start(bf16[4,656,128]{2,1,0:T(8,128)(2,1)} %get-tuple-element.44.low_ref), channel_id=1, source_target_pairs={{0,8},{8,0},{16,24},{24,16},{1,9},{9,1},{17,25},{25,17},{2,10},{10... | collective-permute-start | bytes 2015240 | tf_op jit(solution)/shard_map/ppermute | solution.py:368
  10.8 16.5 %collective-permute-start.2 = (bf16[4,656,128]{2,1,0:T(8,128)(2,1)}, bf16[4,656,128]{2,1,0:T(8,128)(2,1)S(1)}, u32[]{:S(2)}, u32[]{:S(2)}) collective-permute-start(bf16[4,656,128]{2,1,0:T(8,128)(2,1)} %get-tuple-element.43.high_ref), channel_id=1, source_target_pairs={{0,16},{8,24},{16,0},{24,8},{1,17},{9,25},{17,1},{25,9},{2,18},{10... | collective-permute-start | bytes 2015240 | tf_op jit(solution)/shard_map/ppermute | solution.py:371
  12.3 33.4 %collective-permute-start.9 = (bf16[4,656,128]{2,1,0:T(8,128)(2,1)}, bf16[4,656,128]{2,1,0:T(8,128)(2,1)}, u32[]{:S(2)}, u32[]{:S(2)}) collective-permute-start(bf16[4,656,128]{2,1,0:T(8,128)(2,1)} %get-tuple-element.43.high_ref), channel_id=1, source_target_pairs={{0,8},{8,0},{16,24},{24,16},{1,9},{9,1},{17,25},{25,17},{2,10},{10... | collective-permute-start | bytes 2015240 | tf_op jit(solution)/shard_map/ppermute | solution.py:368
  12.8 1.1 %copy-start.4 = (bf16[4,656,128]{2,1,0:T(8,128)(2,1)S(1)}, bf16[4,656,128]{2,1,0:T(8,128)(2,1)}, u32[]{:S(2)}) copy-start(bf16[4,656,128]{2,1,0:T(8,128)(2,1)} %get-tuple-element.43.high_ref) | copy-start | bytes 2015236
  13.9 0.7 %copy-start.9 = (f32[8,128]{1,0:T(8,128)S(1)}, f32[8,128]{1,0:T(8,128)}, u32[]{:S(2)}) copy-start(f32[8,128]{1,0:T(8,128)} %get-tuple-element.27.weight_ref) | copy-start | bytes 12292
  19.1 0.7 %copy-start.7 = (s32[8,2]{1,0:T(8,128)S(1)}, s32[8,2]{1,0:T(8,128)}, u32[]{:S(2)}) copy-start(s32[8,2]{1,0:T(8,128)} %get-tuple-element.32.uses_ref) | copy-start | bytes 196
  19.8 10.1 %copy-start.10 = (f32[8,128]{1,0:T(8,128)S(1)}, f32[8,128]{1,0:T(8,128)}, u32[]{:S(2)}) copy-start(f32[8,128]{1,0:T(8,128)} %get-tuple-element.27.weight_ref) | copy-start | bytes 12292
  21.4 14.8 %copy-start.8 = (s32[8,2]{1,0:T(8,128)S(1)}, s32[8,2]{1,0:T(8,128)}, u32[]{:S(2)}) copy-start(s32[8,2]{1,0:T(8,128)} %get-tuple-element.32.uses_ref) | copy-start | bytes 196
  21.4 18.4 %collective-permute-start.3 = (bf16[512,512]{1,0:T(8,128)(2,1)}, bf16[512,512]{1,0:T(8,128)(2,1)}, u32[]{:S(2)}, u32[]{:S(2)}) collective-permute-start(bf16[512,512]{1,0:T(8,128)(2,1)} %collective-permute-done), channel_id=1, source_target_pairs={{0,2},{1,3},{2,4},{3,5},{4,6},{5,7},{6,0},{7,1},{8,10},{9,11},{10,... | collective-permute-start | bytes 1572872 | tf_op jit(solution)/shard_map/ppermute | solution.py:374
  27.3 6.6 %copy-start = (bf16[4,656,128]{2,1,0:T(8,128)(2,1)}, bf16[4,656,128]{2,1,0:T(8,128)(2,1)S(1)}, u32[]{:S(2)}) copy-start(bf16[4,656,128]{2,1,0:T(8,128)(2,1)S(1)} %collective-permute-done.1.one_ref.x_low) | copy-start | bytes 2015236
  27.3 6.7 %copy-start.2 = (bf16[4,656,128]{2,1,0:T(8,128)(2,1)}, bf16[4,656,128]{2,1,0:T(8,128)(2,1)S(1)}, u32[]{:S(2)}) copy-start(bf16[4,656,128]{2,1,0:T(8,128)(2,1)S(1)} %collective-permute-done.2.two_ref.y_high) | copy-start | bytes 2015236
  27.3 8.8 %collective-permute-start.4 = (bf16[512,512]{1,0:T(8,128)(2,1)S(1)}, bf16[512,512]{1,0:T(8,128)(2,1)S(1)}, u32[]{:S(2)}, u32[]{:S(2)}) collective-permute-start(bf16[512,512]{1,0:T(8,128)(2,1)S(1)} %bitcast.16), channel_id=1, source_target_pairs={{0,1},{1,0},{2,3},{3,2},{4,5},{5,4},{6,7},{7,6},{8,9},{9,8},{10,11... | collective-permute-start | bytes 1572872 | tf_op jit(solution)/shard_map/ppermute | solution.py:377
  27.3 8.8 %collective-permute-start.5 = (bf16[512,512]{1,0:T(8,128)(2,1)}, bf16[512,512]{1,0:T(8,128)(2,1)S(1)}, u32[]{:S(2)}, u32[]{:S(2)}) collective-permute-start(bf16[512,512]{1,0:T(8,128)(2,1)} %collective-permute-done), channel_id=1, source_target_pairs={{0,1},{1,0},{2,3},{3,2},{4,5},{5,4},{6,7},{7,6},{8,9},{9,8},{10,11... | collective-permute-start | bytes 1572872 | tf_op jit(solution)/shard_map/ppermute | solution.py:377
  28.2 18.0 %collective-permute-start.10 = (bf16[4,656,128]{2,1,0:T(8,128)(2,1)}, bf16[4,656,128]{2,1,0:T(8,128)(2,1)}, u32[]{:S(2)}, u32[]{:S(2)}) collective-permute-start(bf16[4,656,128]{2,1,0:T(8,128)(2,1)} %get-tuple-element.44.low_ref), channel_id=1, source_target_pairs={{0,16},{8,24},{16,0},{24,8},{1,17},{9,25},{17,1},{25,9},{2,18},{10... | collective-permute-start | bytes 2015240 | tf_op jit(solution)/shard_map/ppermute | solution.py:371
  33.9 3.9 %copy-start.5 = (f32[8,128,128]{2,1,0:T(8,128)}, f32[8,128,128]{2,1,0:T(8,128)S(1)}, u32[]{:S(2)}) copy-start(f32[8,128,128]{2,1,0:T(8,128)S(1)} %coupled.2.acc_ref) | copy-start | bytes 1572868
  36.0 5.3 %collective-permute-start.8 = (bf16[512,512]{1,0:T(8,128)(2,1)}, bf16[512,512]{1,0:T(8,128)(2,1)}, u32[]{:S(2)}, u32[]{:S(2)}) collective-permute-start(bf16[512,512]{1,0:T(8,128)(2,1)} %collective-permute-done.6), channel_id=1, source_target_pairs={{0,1},{1,0},{2,3},{3,2},{4,5},{5,4},{6,7},{7,6},{8,9},{9,8},{10,11... | collective-permute-start | bytes 1572872 | tf_op jit(solution)/shard_map/ppermute | solution.py:377
  36.1 6.7 %copy-start.11 = (s32[16]{0:T(128)S(1)}, s32[16]{0:T(128)}, u32[]{:S(2)}) copy-start(s32[16]{0:T(128)} %get-tuple-element.34.turn_ref) | copy-start | bytes 196
  39.8 3.0 %collective-permute-start.7 = (bf16[512,512]{1,0:T(8,128)(2,1)}, bf16[512,512]{1,0:T(8,128)(2,1)}, u32[]{:S(2)}, u32[]{:S(2)}) collective-permute-start(bf16[512,512]{1,0:T(8,128)(2,1)} %collective-permute-done.3), channel_id=1, source_target_pairs={{0,1},{1,0},{2,3},{3,2},{4,5},{5,4},{6,7},{7,6},{8,9},{9,8},{10,11... | collective-permute-start | bytes 1572872 | tf_op jit(solution)/shard_map/ppermute | solution.py:377
  39.8 18.1 %collective-permute-start.11 = (bf16[4,128,128]{2,1,0:T(8,128)(2,1)S(1)}, bf16[4,128,128]{2,1,0:T(8,128)(2,1)S(1)}, u32[]{:S(2)}, u32[]{:S(2)}) collective-permute-start(bf16[4,128,128]{2,1,0:T(8,128)(2,1)S(1)} %get-tuple-element.39), channel_id=1, source_target_pairs={{0,8},{8,0},{16,24},{24,16},{1,9},{9,1},{17,25},{25,17},{2,10},{10... | collective-permute-start | bytes 393224 | tf_op jit(solution)/shard_map/ppermute | solution.py:368
  41.3 16.6 %collective-permute-start.12 = (bf16[4,128,128]{2,1,0:T(8,128)(2,1)S(1)}, bf16[4,128,128]{2,1,0:T(8,128)(2,1)S(1)}, u32[]{:S(2)}, u32[]{:S(2)}) collective-permute-start(bf16[4,128,128]{2,1,0:T(8,128)(2,1)S(1)} %get-tuple-element.47), channel_id=1, source_target_pairs={{0,16},{8,24},{16,0},{24,8},{1,17},{9,25},{17,1},{25,9},{2,18},{10... | collective-permute-start | bytes 393224 | tf_op jit(solution)/shard_map/ppermute | solution.py:371
  42.8 3.4 %copy-start.1 = (bf16[4,656,128]{2,1,0:T(8,128)(2,1)S(1)}, bf16[4,656,128]{2,1,0:T(8,128)(2,1)}, u32[]{:S(2)}) copy-start(bf16[4,656,128]{2,1,0:T(8,128)(2,1)} %copy-done) | copy-start | bytes 2015236
  42.8 3.4 %copy-start.3 = (bf16[4,656,128]{2,1,0:T(8,128)(2,1)S(1)}, bf16[4,656,128]{2,1,0:T(8,128)(2,1)}, u32[]{:S(2)}) copy-start(bf16[4,656,128]{2,1,0:T(8,128)(2,1)} %copy-done.2) | copy-start | bytes 2015236
  49.6 8.3 %collective-permute-start.13 = (bf16[4,128,128]{2,1,0:T(8,128)(2,1)S(1)}, bf16[4,128,128]{2,1,0:T(8,128)(2,1)S(1)}, u32[]{:S(2)}, u32[]{:S(2)}) collective-permute-start(bf16[4,128,128]{2,1,0:T(8,128)(2,1)S(1)} %get-tuple-element.45), channel_id=1, source_target_pairs={{0,8},{8,0},{16,24},{24,16},{1,9},{9,1},{17,25},{25,17},{2,10},{10... | collective-permute-start | bytes 393224 | tf_op jit(solution)/shard_map/ppermute | solution.py:368
  51.7 6.2 %copy-start.6 = (f32[8,128,128]{2,1,0:T(8,128)S(1)}, f32[8,128,128]{2,1,0:T(8,128)}, u32[]{:S(2)}) copy-start(f32[8,128,128]{2,1,0:T(8,128)} %copy-done.5) | copy-start | bytes 1572868
  51.7 6.2 %collective-permute-start.14 = (bf16[4,128,128]{2,1,0:T(8,128)(2,1)S(1)}, bf16[4,128,128]{2,1,0:T(8,128)(2,1)S(1)}, u32[]{:S(2)}, u32[]{:S(2)}) collective-permute-start(bf16[4,128,128]{2,1,0:T(8,128)(2,1)S(1)} %get-tuple-element.48), channel_id=1, source_target_pairs={{0,16},{8,24},{16,0},{24,8},{1,17},{9,25},{17,1},{25,9},{2,18},{10... | collective-permute-start | bytes 393224 | tf_op jit(solution)/shard_map/ppermute | solution.py:371
